TPU v7x, 32 devices: a whole 2x2x4 slice. The times are simulated.
32 devices in a mesh: grp: 2 (over y), smp: 16 (over z, x, core).
Axes of the slice: x: 2, y: 2, z: 4, core: 2. Of those that a mesh axis runs over, the one named last changes fastest.
Arguments:
- cand_grads: bfloat16 [128, 6144], P(('grp', 'smp')), parts along dimension 0, may hold values from -300 to 300, as said below
- target_grads: bfloat16 [32, 6144], P(('grp', 'smp')), parts along dimension 0, may hold values from -300 to 300, as said below
- projection: bfloat16 [6144, 8192], P('smp'), may hold values from -0.078125 to 0.078125
Outputs:
- scores: float32 [128, 16], P(('grp', 'smp')), parts along dimension 0
There are 2 independent parts, one for each index of `grp`. A program takes and returns all parts, laid end to end along the dimension named above; an argument that names none is the same for every part. Nothing has to cross between parts.
Inputs may be any that keep to these rules, and one draw needn't show every extreme that they name: `cand_grads`: real-valued gradients of mixed scale. `target_grads`: real-valued gradients of mixed scale.
All inputs are finite; a program needn't handle non-finite values.
Results may differ from a plain program's by a relative error of at most 0.0003.
Values may be sent and summed in bfloat16 or wider, within the bound.
No kernel may reach another device: no remote copies, remote signals or barrier semaphores. Data moves between devices by JAX's collectives and lax.ppermute only.
A program may use at most 128 MiB of HBM per device.

v0:
```python
import jax
import jax.numpy as jnp
from jax import lax
from jax.sharding import PartitionSpec as P

K = 8192


EPS = 1e-06


def shards(cand_grads, target_grads, projection):
    devices = lax.axis_size("smp")
    cand_count = cand_grads.shape[0]
    tgt_count = target_grads.shape[0]
    per_device = cand_count + tgt_count
    own_rows = jnp.concatenate([cand_grads, target_grads], axis=0)
    regrouped = lax.all_to_all(own_rows, "smp", split_axis=1, concat_axis=0, tiled=True)
    sketch = lax.psum_scatter(
        lax.dot_general(
            projection, regrouped, (((0,), (1,)), ((), ())), preferred_element_type=jnp.float32
        ),
        "smp",
        scatter_dimension=0,
        tiled=True,
    )
    width = sketch.shape[0]
    grouped = sketch.reshape(width, devices, per_device)
    cand_part = grouped[:, :, :cand_count].reshape(width, devices * cand_count)
    tgt_part = grouped[:, :, cand_count:].reshape(width, devices * tgt_count)
    cand_sq = jnp.sum(cand_part * cand_part, axis=0)
    tgt_sq = jnp.sum(tgt_part * tgt_part, axis=0)
    cand_tot, tgt_tot = lax.psum((cand_sq, tgt_sq), "smp")
    cand_unit = cand_part * lax.rsqrt(cand_tot / K + EPS)[None, :]
    tgt_unit = tgt_part * lax.rsqrt(tgt_tot / K + EPS)[None, :]
    partial_value = lax.dot_general(
        cand_unit,
        tgt_unit,
        (((0,), (0,)), ((), ())),
        precision=lax.Precision.HIGHEST,
        preferred_element_type=jnp.float32,
    )
    scores = lax.psum_scatter(partial_value, "smp", scatter_dimension=0, tiled=True) / K
    return scores


def solution(mesh):
    return jax.shard_map(
        shards,
        mesh=mesh,
        in_specs=(P(("grp", "smp"), None), P(("grp", "smp"), None), P("smp", None)),
        out_specs=P(("grp", "smp"), None),
        check_vma=False,
    )
```

profile of v0, /device:TPU:0, one launch (start us, length us, event | category | flops | bytes accessed | tf_op | source)
XLA Modules:
  0.0 185.9 jit_solution(6205690246852914386)
XLA Ops:
  6.5 0.0 reduce-scatter.2.cloned.1.call-start
  6.5 0.9 pad_maximum_fusion
  7.4 14.6 %all_to_all.19 = bf16[5,16,384]{2,0,1:T(8,128)(2,1)S(1)} all-to-all(bf16[5,16,384]{2,0,1:T(8,128)(2,1)S(1)} %bitcast.16), channel_id=1, replica_groups=mesh['grp'=2,'smp'=16] {'smp'}, dimensions={1} | all-to-all | bytes 122880 | tf_op jit(solution)/shard_map/all_to_all | solution.py:18
  22.0 0.0 copy-start
  22.0 5.6 %convolution_bitcast_fusion = f32[8192,80]{0,1:T(8,128)} fusion(bf16[80,384]{1,0:T(8,128)(2,1)S(1)} %all_to_all.17, bf16[384,8192]{1,0:T(8,128)(2,1)} %param.5), kind=kOutput, calls=%fused_computation | convolution fusion | flops 503316480 | bytes 8974336 | tf_op jit(solution)/shard_map/dot_general | solution.py:20
  27.6 0.0 reduce-scatter.2.cloned.1.call-update
  27.7 0.0 copy-done
  27.7 0.6 dynamic-slice
  28.9 60.3 %reduce-scatter.2.cloned.1.call-done = f32[512,80]{0,1:T(8,128)} async-done(((f32[8192,80]{0,1:T(8,128)}), f32[512,80]{0,1:T(8,128)}) %reduce-scatter.2.cloned.1.call-update) | async-done | bytes 163856 | tf_op jit(solution)/shard_map/reduce_scatter | solution.py:19
  89.2 0.9 reshape.24
  90.1 0.1 multiply_reduce_fusion
  90.2 0.2 multiply_reduce_fusion.1
  90.4 0.1 reduce_sum.21
  90.5 29.7 %all-reduce.1 = (f32[64]{0:T(128)S(1)}, f32[16]{0:T(128)S(1)}) all-reduce(f32[64]{0:T(128)S(1)} %reduce_sum.21, f32[16]{0:T(128)S(1)} %multiply_reduce_fusion.1), channel_id=1, replica_groups=mesh['grp'=2,'smp'=16] {'smp'}, use_global_device_ids=true, to_apply=%region_2.0 | all-reduce | flops 80 | bytes 640 | tf_op jit(solution)/shard_map/psum | solution.py:33
  120.2 0.1 slice_multiply_fusion.1
  120.3 0.1 mul.33
  120.4 0.1 slice_multiply_fusion
  120.5 0.2 fusion
  120.8 57.6 %all-reduce = f32[64,16]{1,0:T(8,128)S(1)} all-reduce(f32[64,16]{1,0:T(8,128)S(1)} %fusion), channel_id=3, replica_groups=mesh['grp'=2,'smp'=16] {'smp'}, use_global_device_ids=true, to_apply=%region_5.0.clone | all-reduce | flops 1024 | bytes 8192
  178.4 0.6 dynamic-slice_multiply_fusion
  (4 shorter events, 0.1 us)
Async XLA Ops:
  6.5 82.6 %reduce-scatter.2.cloned.1.call-start = ((), (), s32[]{:S(2)}) async-start(), calls=%async_computation.2 | async-start | bytes 2785280 | tf_op jit(solution)/shard_map/reduce_scatter | solution.py:19
  22.0 5.6 %copy-start = (u32[32]{0:T(128)S(1)}, u32[32]{0:T(128)}, u32[]{:S(2)}) copy-start(u32[32]{0:T(128)} %constant.16) | copy-start | bytes 388
Sparse Core Ops, SparseCore 0:
  27.8 61.3 reduce-scatter.1
where the time goes:
time: 186 us
  blocking collectives  102 us (55%)
  waiting for transfers between devices  60.3 us (32%)
  between operations  14.1 us (8%)
  matrix products  5.85 us (3%)
  other arithmetic  1.97 us (1%)
    reduce_scatter x1, waiting for transfers between devices, shards(): lax.psum_scatter(lax.dot_general(projection, regrouped, (((0,), (1,)), ((...  60.3 us
    unnamed x1, blocking collectives  57.6 us
    psum x1, blocking collectives, shards(): cand_tot, tgt_tot = lax.psum((cand_sq, tgt_sq), 'smp')  29.7 us
    all_to_all x1, blocking collectives, shards(): lax.all_to_all(own_rows, 'smp', split_axis=1, concat_axis=0, tiled=True)  14.6 us
    dot_general x1, matrix products, shards(): lax.dot_general(projection, regrouped, (((0,), (1,)), ((), ())), preferre...  5.6 us
  transfers between devices with their start and end apart: 1, of which 1 were waited for; matrix products, arithmetic and copies ran while one was open for 0% of the time, Pallas kernels for 0%

commit v1 on v0

v1 whole, which is shorter than its diff:
```python
import functools

import jax
import jax.numpy as jnp
from jax import lax
from jax.experimental import pallas as pl
from jax.experimental.pallas import tpu as pltpu
from jax.sharding import PartitionSpec as P

K = 8192
EPS = 1e-06
LANES = 128
PAD = 8
TOP = 32.0


def prep_kernel(cand_ref, tgt_ref, rows_ref, inv_ref):
    count = cand_ref.shape[0] + tgt_ref.shape[0]
    cand = cand_ref[...].astype(jnp.float32)
    tgt = tgt_ref[...].astype(jnp.float32)
    fill = jnp.zeros((PAD - count, cand.shape[1]), jnp.float32)
    rows = jnp.concatenate([cand, tgt, fill], axis=0)
    largest = jnp.max(jnp.abs(rows), axis=1, keepdims=True)
    scale = jnp.full((PAD, 1), 2.0**-4, jnp.float32)
    inv = jnp.full((PAD, 1), 2.0**4, jnp.float32)
    for power in (60, 30, 15, 8, 4, 2, 1):
        fits = largest * scale * 2.0**power < TOP
        scale = jnp.where(fits, scale * 2.0**power, scale)
        inv = jnp.where(fits, inv * 2.0**-power, inv)
    rows_ref[...] = (rows * scale).astype(rows_ref.dtype)
    inv_ref[...] = jnp.broadcast_to(inv, inv_ref.shape)


def prepare(cand_grads, tgt_grads):
    params = cand_grads.shape[1]
    return pl.pallas_call(
        prep_kernel,
        out_shape=(
            jax.ShapeDtypeStruct((PAD, params), jnp.bfloat16),
            jax.ShapeDtypeStruct((PAD, LANES), jnp.float32),
        ),
        compiler_params=pltpu.CompilerParams(vmem_limit_bytes=16 << 20),
        name="prepare",
    )(cand_grads, tgt_grads)


def sketch_kernel(count, devices, off_ref, gathered_ref, proj_ref, out_ref):
    rows = count * devices
    row = lax.broadcasted_iota(jnp.int32, (rows, devices * PAD), 0)
    col = lax.broadcasted_iota(jnp.int32, (rows, devices * PAD), 1)
    pick = col == (row % devices) * PAD + row // devices
    order = jnp.dot(
        pick.astype(jnp.bfloat16), gathered_ref[...], preferred_element_type=jnp.float32
    ).astype(jnp.bfloat16)
    width = out_ref.shape[2]
    for block in range(out_ref.shape[0]):
        out_ref[block] = jnp.dot(
            order,
            proj_ref[:, block * width : (block + 1) * width],
            preferred_element_type=jnp.float32,
        )


def sketch_half(gathered, projection, half, count, devices, blocks):
    params, columns = projection.shape
    span = columns // 2
    width = span // blocks
    per_step = max(1, blocks // 2)
    steps = blocks // per_step
    rows = count * devices
    return pl.pallas_call(
        functools.partial(sketch_kernel, count, devices),
        grid_spec=pltpu.PrefetchScalarGridSpec(
            num_scalar_prefetch=1,
            grid=(steps,),
            in_specs=[
                pl.BlockSpec(gathered.shape, lambda i, off: (0, 0)),
                pl.BlockSpec((params, span // steps), lambda i, off: (0, off[0] * steps + i)),
            ],
            out_specs=pl.BlockSpec((per_step, rows, width), lambda i, off: (i, 0, 0)),
        ),
        out_shape=jax.ShapeDtypeStruct((blocks, rows, width), jnp.float32),
        compiler_params=pltpu.CompilerParams(vmem_limit_bytes=40 << 20),
        name="sketch_half",
    )(half.reshape(1), gathered, projection)


def gram_kernel(pc, devices, me_ref, sum_ref, inv_ref, out_ref):
    cands = pc * devices
    c = sum_ref[:cands, :]
    t = sum_ref[cands:, :]
    exact = functools.partial(
        lax.dot_general,
        dimension_numbers=(((1,), (1,)), ((), ())),
        precision=lax.Precision.HIGHEST,
        preferred_element_type=jnp.float32,
    )
    scores = exact(c, t)
    c_sq = jnp.sum(c * c, axis=1, keepdims=True)
    t_sq = exact(jnp.ones((PAD, t.shape[1]), jnp.float32), t * t)[0:1, :]
    lane = lax.broadcasted_iota(jnp.int32, (1, devices), 1)
    t_inv = jnp.where(lane == me_ref[0], inv_ref[pc : pc + 1, 0:1], 0.0)
    out_ref[...] = jnp.zeros_like(out_ref)
    for slot in range(pc):
        out_ref[:, slot, :devices] = scores[slot * devices : (slot + 1) * devices, :]
        out_ref[:, PAD - 1, slot : slot + 1] = c_sq[slot * devices : (slot + 1) * devices, :]
    out_ref[:, pc, :devices] = jnp.broadcast_to(t_sq, (devices, devices))
    out_ref[:, pc + 1, :devices] = jnp.broadcast_to(t_inv, (devices, devices))


def gram(summed, inv, me, pc, devices):
    return pl.pallas_call(
        functools.partial(gram_kernel, pc, devices),
        in_specs=[
            pl.BlockSpec(memory_space=pltpu.SMEM),
            pl.BlockSpec(memory_space=pltpu.VMEM),
            pl.BlockSpec(memory_space=pltpu.VMEM),
        ],
        out_shape=jax.ShapeDtypeStruct((devices, PAD, LANES), jnp.float32),
        compiler_params=pltpu.CompilerParams(vmem_limit_bytes=16 << 20),
        name="gram",
    )(me.reshape(1), summed, inv)


def finish_kernel(pc, devices, parts_ref, inv_ref, out_ref):
    total = jnp.sum(parts_ref[...], axis=0)
    inv_c = inv_ref[:pc, 0:1]
    inv_t = total[pc + 1 : pc + 2, :devices]
    row = lax.broadcasted_iota(jnp.int32, (pc, LANES), 0)
    lane = lax.broadcasted_iota(jnp.int32, (pc, LANES), 1)
    c_sq = jnp.sum(
        jnp.where(row == lane, jnp.broadcast_to(total[PAD - 1 : PAD, :], (pc, LANES)), 0.0),
        axis=1,
        keepdims=True,
    )
    t_sq = total[pc : pc + 1, :devices]
    c_scale = inv_c * lax.rsqrt(c_sq / K * inv_c * inv_c + EPS)
    t_scale = inv_t * lax.rsqrt(t_sq / K * inv_t * inv_t + EPS)
    out_ref[...] = total[:pc, :devices] * c_scale * t_scale / K


def finish(parts, inv, pc, devices):
    return pl.pallas_call(
        functools.partial(finish_kernel, pc, devices),
        out_shape=jax.ShapeDtypeStruct((pc, devices), jnp.float32),
        compiler_params=pltpu.CompilerParams(vmem_limit_bytes=16 << 20),
        name="finish",
    )(parts, inv)


def shards(cand_grads, tgt_grads, projection):
    devices = lax.axis_size("smp")
    me = lax.axis_index("smp")
    pc, pt = cand_grads.shape[0], tgt_grads.shape[0]
    count = pc + pt
    params = projection.shape[0]
    blocks = devices // 2
    core = me % 2

    rows, inv = prepare(cand_grads, tgt_grads)
    rows = rows.reshape(PAD, devices, params)
    gathered = lax.all_to_all(rows, "smp", split_axis=1, concat_axis=0, tiled=False)
    gathered = gathered.reshape(devices * PAD, params)

    theirs = sketch_half(gathered, projection, 1 - core, count, devices, blocks)
    arrived = lax.ppermute(theirs, "smp", [(i, i ^ 1) for i in range(devices)])
    mine = sketch_half(gathered, projection, core, count, devices, blocks)
    chip = (mine + arrived).astype(jnp.float16)
    same_core = [[i for i in range(devices) if i % 2 == c] for c in range(2)]
    chip = lax.all_to_all(
        chip, "smp", split_axis=0, concat_axis=0, axis_index_groups=same_core, tiled=True
    )
    summed = jnp.sum(chip.astype(jnp.float32), axis=0)

    message = gram(summed, inv, me, pc, devices)
    parts = lax.all_to_all(message, "smp", split_axis=0, concat_axis=0, tiled=True)
    return finish(parts, inv, pc, devices)


def solution(mesh):
    return jax.shard_map(
        shards,
        mesh=mesh,
        in_specs=(P(("grp", "smp"), None), P(("grp", "smp"), None), P("smp", None)),
        out_specs=P(("grp", "smp"), None),
        check_vma=False,
    )
```

time: 186 us -> 56.9 us (0.31)
  blocking collectives: 102 us -> 30.7 us
  waiting for transfers between devices: 60.3 us -> 7.7 us
  between operations: 14.1 us -> 0.07 us
  starting transfers between devices: 0.01 us -> 7.43 us
  matrix products: 5.85 us -> 0 us
  Pallas kernels: 0 us -> 4.34 us
  local copies, waits for them, and re-layouts: 1.78 us -> 5.77 us
    reduce_scatter x1 -> x0, waiting for transfers between devices: 60.3 us -> none  [shards(): lax.psum_scatter(lax.dot_general(projection, regrouped, (((0,), (1,)), ((...]
    unnamed x1 -> x0, blocking collectives: 57.6 us -> none
    psum x1 -> x0, blocking collectives: 29.7 us -> none  [shards(): cand_tot, tgt_tot = lax.psum((cand_sq, tgt_sq), 'smp')]
    all_to_all x1 -> x2, blocking collectives: 14.6 us -> 30.7 us  [the longest x1 20.6 us: shards(): lax.all_to_all(chip, 'smp', split_axis=0, concat_axis=0, axis_index_group...]
    all_to_all x0 -> x1, waiting for transfers between devices: none -> 7.4 us  [shards(): lax.all_to_all(rows, 'smp', split_axis=1, concat_axis=0, tiled=False)]
    all_to_all x0 -> x1, starting transfers between devices: none -> 7.36 us  [shards(): lax.all_to_all(rows, 'smp', split_axis=1, concat_axis=0, tiled=False)]
    dot_general x2 -> x0, matrix products: 5.85 us -> none  [the longest x1 5.6 us: shards(): lax.dot_general(projection, regrouped, (((0,), (1,)), ((), ())), preferre...]
    unnamed x3 -> x8, local copies, waits for them, and re-layouts: 0.59 us -> 5.77 us
  transfers between devices with their start and end apart: 1 -> 2, of which waited for: 1 -> 2; matrix products, arithmetic and copies ran while one was open for 0% -> 0% of each run, Pallas kernels for 0% -> 2%
where the time goes in v1:
time: 56.9 us; the launch traced here: 56.4 us
  blocking collectives  30.7 us (54%)
  waiting for transfers between devices  7.7 us (14%)
  starting transfers between devices  7.43 us (13%)
  local copies, waits for them, and re-layouts  5.77 us (10%)
  Pallas kernels  4.34 us (8%)
    all_to_all x1, blocking collectives, shards(): lax.all_to_all(chip, 'smp', split_axis=0, concat_axis=0, axis_index_group...  20.6 us
    all_to_all x1, blocking collectives, shards(): lax.all_to_all(message, 'smp', split_axis=0, concat_axis=0, tiled=True)  10.1 us
    all_to_all x1, waiting for transfers between devices, shards(): lax.all_to_all(rows, 'smp', split_axis=1, concat_axis=0, tiled=False)  7.4 us
    all_to_all x1, starting transfers between devices, shards(): lax.all_to_all(rows, 'smp', split_axis=1, concat_axis=0, tiled=False)  7.36 us
    unnamed x8, local copies, waits for them, and re-layouts  5.77 us
    pallas_call x2, Pallas kernels, sketch_half(): pl.pallas_call(functools.partial(sketch_kernel, count, devices), grid_spe...  2.51 us
  transfers between devices with their start and end apart: 2, of which 2 were waited for; matrix products, arithmetic and copies ran while one was open for 0% of the time, Pallas kernels for 2%

profile of v1, /device:TPU:0, one launch (start us, length us, event | category | flops | bytes accessed | tf_op | source)
XLA Modules:
  0.0 56.4 jit_solution(1076543322488504619)
XLA Ops:
  0.0 0.0 copy-start.2
  0.0 0.8 %copy-done.2 = bf16[4,6144]{1,0:T(4,128)(2,1)S(1)} copy-done((bf16[4,6144]{1,0:T(4,128)(2,1)S(1)}, bf16[4,6144]{1,0:T(4,128)(2,1)}, u32[]{:S(2)}) %copy-start.2) | copy-done | bytes 49176
  0.8 0.0 copy-start.3
  0.8 0.7 %copy-done.3 = bf16[1,6144]{1,0:T(2,128)(2,1)S(1)} copy-done((bf16[1,6144]{1,0:T(2,128)(2,1)S(1)}, bf16[1,6144]{1,0:T(2,128)(2,1)}, u32[]{:S(2)}) %copy-start.3) | copy-done | bytes 12312
  1.5 0.8 %prepare.1 = (bf16[8,6144]{1,0:T(8,128)(2,1)}, f32[8,128]{1,0:T(8,128)S(1)}) custom-call(bf16[4,6144]{1,0:T(4,128)(2,1)S(1)} %copy-done.2, bf16[1,6144]{1,0:T(2,128)(2,1)S(1)} %copy-done.3), custom_call_target="tpu_custom_call" | custom-call | tf_op jit(solution)/shard_map/prepare/pallas_call | solution.py:36
  2.3 7.4 %all-to-all-start = ((bf16[1,8,16,384]{3,1,0,2:T(8,128)(2,1)}), bf16[1,8,16,384]{3,1,0,2:T(8,128)(2,1)S(1)}, u32[]{:S(2)}, u32[]{:S(2)}) async-start(bf16[1,8,16,384]{3,1,0,2:T(8,128)(2,1)} %bitcast.3), calls=%async_computation | async-start | bytes 196608 | tf_op jit(solution)/shard_map/all_to_all | solution.py:162
  9.7 7.4 %all-to-all-done = bf16[1,8,16,384]{3,1,0,2:T(8,128)(2,1)S(1)} async-done(((bf16[1,8,16,384]{3,1,0,2:T(8,128)(2,1)}), bf16[1,8,16,384]{3,1,0,2:T(8,128)(2,1)S(1)}, u32[]{:S(2)}, u32[]{:S(2)}) %all-to-all-start) | async-done | bytes 98336 | tf_op jit(solution)/shard_map/all_to_all | solution.py:162
  17.1 0.0 copy-start
  17.1 2.8 %copy-done = bf16[384,8192]{1,0:T(8,128)(2,1)S(1)} copy-done((bf16[384,8192]{1,0:T(8,128)(2,1)S(1)}, bf16[384,8192]{1,0:T(8,128)(2,1)}, u32[]{:S(2)}) %copy-start) | copy-done | bytes 6291480
  19.9 0.0 copy-start.1
  19.9 1.2 %sketch_half.3 = f32[8,80,512]{2,1,0:T(8,128)S(1)} custom-call(s32[1]{0:T(128)} %bitcast.7.off_ref, bf16[128,384]{1,0:T(8,128)(2,1)S(1)} %bitcast.11, bf16[384,8192]{1,0:T(8,128)(2,1)S(1)} %copy-done), custom_call_target="tpu_custom_call" | custom-call | tf_op jit(solution)/shard_map/sketch_half/pallas_call | solution.py:71
  21.1 0.1 collective-permute-start
  21.2 1.4 %copy-done.1 = bf16[384,8192]{1,0:T(8,128)(2,1)S(1)} copy-done((bf16[384,8192]{1,0:T(8,128)(2,1)S(1)}, bf16[384,8192]{1,0:T(8,128)(2,1)}, u32[]{:S(2)}) %copy-start.1) | copy-done | bytes 6291480
  22.7 1.3 %sketch_half.2 = f32[8,80,512]{2,1,0:T(8,128)S(1)} custom-call(s32[1]{0:T(128)} %bitcast.1.off_ref, bf16[128,384]{1,0:T(8,128)(2,1)S(1)} %bitcast.12, bf16[384,8192]{1,0:T(8,128)(2,1)S(1)} %copy-done.1), custom_call_target="tpu_custom_call" | custom-call | tf_op jit(solution)/shard_map/sketch_half/pallas_call | solution.py:71
  23.9 0.3 collective-permute-done
  24.2 0.3 add_convert_fusion
  24.6 20.6 %all_to_all.25 = f16[8,80,512]{2,1,0:T(8,128)(2,1)S(1)} all-to-all(f16[8,80,512]{2,1,0:T(8,128)(2,1)S(1)} %add_convert_fusion), channel_id=1, replica_groups={{0,2,4,6,8,10,12,14},{1,3,5,7,9,11,13,15},{16,18,20,22,24,26,28,30},{17..., dimensions={0} | all-to-all | bytes 1310720 | tf_op jit(solution)/shard_map/all_to_all | solution.py:170
  45.2 0.1 convert_reduce_fusion.sum_ref
  45.3 0.3 gram.1
  45.6 10.1 %all_to_all.26.parts_ref = f32[16,8,128]{2,1,0:T(8,128)S(1)} all-to-all(f32[16,8,128]{2,1,0:T(8,128)S(1)} %gram.1), channel_id=1, replica_groups=mesh['grp'=2,'smp'=16] {'smp'}, dimensions={0} | all-to-all | bytes 131072 | tf_op jit(solution)/shard_map/all_to_all | solution.py:176
  55.7 0.8 %finish.1 = f32[4,16]{1,0:T(4,128)} custom-call(f32[16,8,128]{2,1,0:T(8,128)S(1)} %all_to_all.26.parts_ref, f32[8,128]{1,0:T(8,128)S(1)} %get-tuple-element.8.inv_ref), custom_call_target="tpu_custom_call" | custom-call | tf_op jit(solution)/shard_map/finish/pallas_call | solution.py:143
Async XLA Ops:
  0.0 0.8 %copy-start.2 = (bf16[4,6144]{1,0:T(4,128)(2,1)S(1)}, bf16[4,6144]{1,0:T(4,128)(2,1)}, u32[]{:S(2)}) copy-start(bf16[4,6144]{1,0:T(4,128)(2,1)} %cand_ref.1) | copy-start | bytes 147460
  0.8 0.7 %copy-start.3 = (bf16[1,6144]{1,0:T(2,128)(2,1)S(1)}, bf16[1,6144]{1,0:T(2,128)(2,1)}, u32[]{:S(2)}) copy-start(bf16[1,6144]{1,0:T(2,128)(2,1)} %tgt_ref.1) | copy-start | bytes 36868
  2.3 14.8 %all-to-all-start = ((bf16[1,8,16,384]{3,1,0,2:T(8,128)(2,1)}), bf16[1,8,16,384]{3,1,0,2:T(8,128)(2,1)S(1)}, u32[]{:S(2)}, u32[]{:S(2)}) async-start(bf16[1,8,16,384]{3,1,0,2:T(8,128)(2,1)} %bitcast.3), calls=%async_computation | async-start | bytes 196608 | tf_op jit(solution)/shard_map/all_to_all | solution.py:162
  17.1 2.8 %copy-start = (bf16[384,8192]{1,0:T(8,128)(2,1)S(1)}, bf16[384,8192]{1,0:T(8,128)(2,1)}, u32[]{:S(2)}) copy-start(bf16[384,8192]{1,0:T(8,128)(2,1)} %proj_ref.3) | copy-start | bytes 18874372
  19.9 2.8 %copy-start.1 = (bf16[384,8192]{1,0:T(8,128)(2,1)S(1)}, bf16[384,8192]{1,0:T(8,128)(2,1)}, u32[]{:S(2)}) copy-start(bf16[384,8192]{1,0:T(8,128)(2,1)} %proj_ref.3) | copy-start | bytes 18874372
  21.1 3.1 %collective-permute-start = (f32[8,80,512]{2,1,0:T(8,128)S(1)}, f32[8,80,512]{2,1,0:T(8,128)S(1)}, u32[]{:S(2)}, u32[]{:S(2)}) collective-permute-start(f32[8,80,512]{2,1,0:T(8,128)S(1)} %sketch_half.3), channel_id=1, source_target_pairs={{0,1},{1,0},{2,3},{3,2},{4,5},{5,4},{6,7},{7,6},{8,9},{9,8},{10,11... | collective-permute-start | bytes 3932168 | tf_op jit(solution)/shard_map/ppermute | solution.py:166

commit v2 on v1

--- a/solution.py
+++ b/solution.py
@@ -1,4 +1,5 @@
 import functools
+import math
 
 import jax
 import jax.numpy as jnp
@@ -12,6 +13,9 @@
 LANES = 128
 PAD = 8
 TOP = 32.0
+STEP = 512
+PIECE = 2048
+KEEP = 13 << 18
 
 
 def prep_kernel(cand_ref, tgt_ref, rows_ref, inv_ref):
@@ -39,50 +43,128 @@
             jax.ShapeDtypeStruct((PAD, params), jnp.bfloat16),
             jax.ShapeDtypeStruct((PAD, LANES), jnp.float32),
         ),
-        compiler_params=pltpu.CompilerParams(vmem_limit_bytes=16 << 20),
+        compiler_params=pltpu.CompilerParams(vmem_limit_bytes=60 << 20),
         name="prepare",
     )(cand_grads, tgt_grads)
 
 
-def sketch_kernel(count, devices, off_ref, gathered_ref, proj_ref, out_ref):
+def in_vmem(shape, dtype):
+    size = math.prod(shape) * jnp.dtype(dtype).itemsize
+    if size <= KEEP:
+        return pltpu.VMEM(shape, dtype)
+    return jax.ShapeDtypeStruct(shape, dtype)
+
+
+def load_kernel(half_ref, proj_ref, out_ref, sem):
+    span = out_ref.shape[1]
+    offset = pl.multiple_of(half_ref[0] * span, span)
+    copy = pltpu.make_async_copy(proj_ref.at[:, pl.ds(offset, span)], out_ref, sem)
+    copy.start()
+    copy.wait()
+
+
+def load(projection, half):
+    params, columns = projection.shape
+    return pl.pallas_call(
+        load_kernel,
+        in_specs=[
+            pl.BlockSpec(memory_space=pltpu.SMEM),
+            pl.BlockSpec(memory_space=pl.ANY),
+        ],
+        out_specs=pl.BlockSpec(memory_space=pltpu.VMEM),
+        out_shape=in_vmem((params, columns // 2), projection.dtype),
+        scratch_shapes=[pltpu.SemaphoreType.DMA],
+        cost_estimate=pl.CostEstimate(
+            flops=0, bytes_accessed=2 * projection.size, transcendentals=0
+        ),
+        compiler_params=pltpu.CompilerParams(vmem_limit_bytes=60 << 20),
+        name="load",
+    )(half.reshape(1), pltpu.with_memory_space_constraint(projection, pltpu.HBM))
+
+
+def in_order(gathered_ref, count, devices):
     rows = count * devices
     row = lax.broadcasted_iota(jnp.int32, (rows, devices * PAD), 0)
     col = lax.broadcasted_iota(jnp.int32, (rows, devices * PAD), 1)
     pick = col == (row % devices) * PAD + row // devices
-    order = jnp.dot(
+    return jnp.dot(
         pick.astype(jnp.bfloat16), gathered_ref[...], preferred_element_type=jnp.float32
     ).astype(jnp.bfloat16)
+
+
+def store_blocks(out_ref, start, part):
     width = out_ref.shape[2]
-    for block in range(out_ref.shape[0]):
-        out_ref[block] = jnp.dot(
-            order,
-            proj_ref[:, block * width : (block + 1) * width],
-            preferred_element_type=jnp.float32,
+    for at in range(0, part.shape[1], width):
+        out_ref[(start + at) // width] = part[:, at : at + width]
+
+
+def theirs_kernel(count, devices, gathered_ref, proj_ref, out_ref):
+    rows = in_order(gathered_ref, count, devices)
+    step = STEP
+    for start in range(0, proj_ref.shape[1], step):
+        part = jnp.dot(
+            rows, proj_ref[:, start : start + step], preferred_element_type=jnp.float32
         )
-
-
-def sketch_half(gathered, projection, half, count, devices, blocks):
+        store_blocks(out_ref, start, part)
+
+
+def mine_kernel(count, devices, half_ref, gathered_ref, proj_ref, out_ref, held, sems):
+    pieces, _, step = held.shape
+    copies = []
+    for piece in range(pieces):
+        offset = pl.multiple_of(half_ref[0] * (pieces * step) + piece * step, step)
+        copy = pltpu.make_async_copy(
+            proj_ref.at[:, pl.ds(offset, step)], held.at[piece], sems.at[piece]
+        )
+        copy.start()
+        copies.append(copy)
+    rows = in_order(gathered_ref, count, devices)
+    for piece in range(pieces):
+        copies[piece].wait()
+        for start in range(0, step, STEP):
+            part = jnp.dot(
+                rows, held[piece, :, start : start + STEP], preferred_element_type=jnp.float32
+            )
+            store_blocks(out_ref, piece * step + start, part)
+
+
+def sketch_theirs(gathered, loaded, count, devices, blocks):
+    params, span = loaded.shape
+    rows = count * devices
+    return pl.pallas_call(
+        functools.partial(theirs_kernel, count, devices),
+        out_shape=in_vmem((blocks, rows, span // blocks), jnp.float32),
+        cost_estimate=pl.CostEstimate(
+            flops=2 * rows * params * span, bytes_accessed=params * span, transcendentals=0
+        ),
+        compiler_params=pltpu.CompilerParams(vmem_limit_bytes=40 << 20),
+        name="sketch_theirs",
+    )(gathered, pltpu.with_memory_space_constraint(loaded, pltpu.VMEM))
+
+
+def sketch_mine(gathered, projection, half, count, devices, blocks):
     params, columns = projection.shape
     span = columns // 2
-    width = span // blocks
-    per_step = max(1, blocks // 2)
-    steps = blocks // per_step
     rows = count * devices
     return pl.pallas_call(
-        functools.partial(sketch_kernel, count, devices),
-        grid_spec=pltpu.PrefetchScalarGridSpec(
-            num_scalar_prefetch=1,
-            grid=(steps,),
-            in_specs=[
-                pl.BlockSpec(gathered.shape, lambda i, off: (0, 0)),
-                pl.BlockSpec((params, span // steps), lambda i, off: (0, off[0] * steps + i)),
-            ],
-            out_specs=pl.BlockSpec((per_step, rows, width), lambda i, off: (i, 0, 0)),
-        ),
-        out_shape=jax.ShapeDtypeStruct((blocks, rows, width), jnp.float32),
-        compiler_params=pltpu.CompilerParams(vmem_limit_bytes=40 << 20),
-        name="sketch_half",
-    )(half.reshape(1), gathered, projection)
+        functools.partial(mine_kernel, count, devices),
+        in_specs=[
+            pl.BlockSpec(memory_space=pltpu.SMEM),
+            pl.BlockSpec(memory_space=pltpu.VMEM),
+            pl.BlockSpec(memory_space=pl.ANY),
+        ],
+        out_specs=pl.BlockSpec(memory_space=pltpu.VMEM),
+        out_shape=in_vmem((blocks, rows, span // blocks), jnp.float32),
+        scratch_shapes=[
+            pltpu.VMEM((span // PIECE, params, PIECE), projection.dtype),
+            pltpu.SemaphoreType.DMA((span // PIECE,)),
+        ],
+        cost_estimate=pl.CostEstimate(
+            flops=2 * rows * params * span, bytes_accessed=params * span * 2, transcendentals=0
+        ),
+        compiler_params=pltpu.CompilerParams(vmem_limit_bytes=58 << 20),
+        name="sketch_mine",
+    )(half.reshape(1), gathered, pltpu.with_memory_space_constraint(projection, pltpu.HBM))
 
 
 def gram_kernel(pc, devices, me_ref, sum_ref, inv_ref, out_ref):
@@ -161,10 +243,11 @@
     rows = rows.reshape(PAD, devices, params)
     gathered = lax.all_to_all(rows, "smp", split_axis=1, concat_axis=0, tiled=False)
     gathered = gathered.reshape(devices * PAD, params)
-
-    theirs = sketch_half(gathered, projection, 1 - core, count, devices, blocks)
+    loaded = load(projection, 1 - core)
+
+    theirs = sketch_theirs(gathered, loaded, count, devices, blocks)
     arrived = lax.ppermute(theirs, "smp", [(i, i ^ 1) for i in range(devices)])
-    mine = sketch_half(gathered, projection, core, count, devices, blocks)
+    mine = sketch_mine(gathered, projection, core, count, devices, blocks)
     chip = (mine + arrived).astype(jnp.float16)
     same_core = [[i for i in range(devices) if i % 2 == c] for c in range(2)]
     chip = lax.all_to_all(

time: 56.9 us -> 53.4 us (0.938)
  local copies, waits for them, and re-layouts: 5.77 us -> 0.01 us
  Pallas kernels: 4.34 us -> 8.53 us
  waiting for transfers between devices: 7.7 us -> 5.49 us
    unnamed x8 -> x4, local copies, waits for them, and re-layouts: 5.77 us -> 0.01 us
    pallas_call x2 -> x3, Pallas kernels: 2.51 us -> 5.91 us  [the longest x1 3.21 us: sketch_mine(): pl.pallas_call(functools.partial(mine_kernel, count, devices), in_specs=[...]
    all_to_all x1, waiting for transfers between devices: 7.4 us -> 5.49 us  [shards(): lax.all_to_all(rows, 'smp', split_axis=1, concat_axis=0, tiled=False)]
    pallas_call x1, Pallas kernels: 0.78 us -> 1.57 us  [prepare(): pl.pallas_call(prep_kernel, out_shape=(jax.ShapeDtypeStruct((PAD, params)...]
  transfers between devices with their start and end apart: 2 -> 2, of which waited for: 2 -> 1; matrix products, arithmetic and copies ran while one was open for 0% -> 0% of each run, Pallas kernels for 2% -> 10%
where the time goes in v2:
time: 53.4 us; the launch traced here: 53 us
  blocking collectives  31.1 us (58%)
  Pallas kernels  8.53 us (16%)
  starting transfers between devices  7.43 us (14%)
  waiting for transfers between devices  5.49 us (10%)
    all_to_all x1, blocking collectives, shards(): lax.all_to_all(chip, 'smp', split_axis=0, concat_axis=0, axis_index_group...  20.9 us
    all_to_all x1, blocking collectives, shards(): lax.all_to_all(message, 'smp', split_axis=0, concat_axis=0, tiled=True)  10.2 us
    all_to_all x1, starting transfers between devices, shards(): lax.all_to_all(rows, 'smp', split_axis=1, concat_axis=0, tiled=False)  7.36 us
    all_to_all x1, waiting for transfers between devices, shards(): lax.all_to_all(rows, 'smp', split_axis=1, concat_axis=0, tiled=False)  5.49 us
    pallas_call x1, Pallas kernels, sketch_mine(): pl.pallas_call(functools.partial(mine_kernel, count, devices), in_specs=[...  3.21 us
    pallas_call x1, Pallas kernels, load(): pl.pallas_call(load_kernel, in_specs=[pl.BlockSpec(memory_space=pltpu.SME...  1.9 us
    pallas_call x1, Pallas kernels, prepare(): pl.pallas_call(prep_kernel, out_shape=(jax.ShapeDtypeStruct((PAD, params)...  1.57 us
  transfers between devices with their start and end apart: 2, of which 1 were waited for; matrix products, arithmetic and copies ran while one was open for 0% of the time, Pallas kernels for 10%

profile of v2, /device:TPU:0, one launch (start us, length us, event | category | flops | bytes accessed | tf_op | source)
XLA Modules:
  0.0 53.0 jit_solution(7169518219577768216)
XLA Ops:
  0.0 1.6 %prepare.1 = (bf16[8,6144]{1,0:T(8,128)(2,1)}, f32[8,128]{1,0:T(8,128)}) custom-call(bf16[4,6144]{1,0:T(4,128)(2,1)} %cand_ref.1, bf16[1,6144]{1,0:T(2,128)(2,1)} %tgt_ref.1), custom_call_target="tpu_custom_call" | custom-call | tf_op jit(solution)/shard_map/prepare/pallas_call | solution.py:40
  1.6 7.4 %all-to-all-start = ((bf16[1,8,16,384]{3,1,0,2:T(8,128)(2,1)}), bf16[1,8,16,384]{3,1,0,2:T(8,128)(2,1)S(1)}, u32[]{:S(2)}, u32[]{:S(2)}) async-start(bf16[1,8,16,384]{3,1,0,2:T(8,128)(2,1)} %bitcast.13), calls=%async_computation | async-start | bytes 196608 | tf_op jit(solution)/shard_map/all_to_all | solution.py:244
  8.9 1.9 %load.1.proj_ref = bf16[384,4096]{1,0:T(8,128)(2,1)S(1)} custom-call(s32[1]{0:T(128)} %bitcast.9.half_ref, bf16[384,8192]{1,0:T(8,128)(2,1)} %proj_ref.3), custom_call_target="tpu_custom_call" | custom-call | bytes 6291456 | tf_op jit(solution)/shard_map/load/pallas_call | solution.py:68
  10.9 5.5 %all-to-all-done = bf16[1,8,16,384]{3,1,0,2:T(8,128)(2,1)S(1)} async-done(((bf16[1,8,16,384]{3,1,0,2:T(8,128)(2,1)}), bf16[1,8,16,384]{3,1,0,2:T(8,128)(2,1)S(1)}, u32[]{:S(2)}, u32[]{:S(2)}) %all-to-all-start) | async-done | bytes 98336 | tf_op jit(solution)/shard_map/all_to_all | solution.py:244
  16.3 0.0 copy-start
  16.3 0.8 %sketch_theirs.1 = f32[8,80,512]{2,1,0:T(8,128)S(1)} custom-call(bf16[128,384]{1,0:T(8,128)(2,1)S(1)} %bitcast.11, bf16[384,4096]{1,0:T(8,128)(2,1)S(1)} %load.1.proj_ref), custom_call_target="tpu_custom_call" | custom-call | flops 251658240 | bytes 1572864 | tf_op jit(solution)/shard_map/sketch_theirs/pallas_call | solution.py:134
  17.1 0.0 copy-done
  17.2 0.1 collective-permute-start
  17.2 3.2 %sketch_mine.1 = f32[8,80,512]{2,1,0:T(8,128)S(1)} custom-call(s32[1]{0:T(128)} %bitcast.1.half_ref, bf16[128,384]{1,0:T(8,128)(2,1)} %bitcast.12, bf16[384,8192]{1,0:T(8,128)(2,1)} %proj_ref.3), custom_call_target="tpu_custom_call" | custom-call | flops 251658240 | bytes 3145728 | tf_op jit(solution)/shard_map/sketch_mine/pallas_call | solution.py:149
  20.5 0.0 collective-permute-done
  20.5 0.3 add_convert_fusion
  20.8 0.0 copy-start.1
  20.8 20.9 %all_to_all.25 = f16[8,80,512]{2,1,0:T(8,128)(2,1)S(1)} all-to-all(f16[8,80,512]{2,1,0:T(8,128)(2,1)S(1)} %add_convert_fusion), channel_id=1, replica_groups={{0,2,4,6,8,10,12,14},{1,3,5,7,9,11,13,15},{16,18,20,22,24,26,28,30},{17..., dimensions={0} | all-to-all | bytes 1310720 | tf_op jit(solution)/shard_map/all_to_all | solution.py:253
  41.7 0.1 convert_reduce_fusion.sum_ref
  41.8 0.0 copy-done.1
  41.8 0.3 gram.1
  42.1 10.2 %all_to_all.26.parts_ref = f32[16,8,128]{2,1,0:T(8,128)S(1)} all-to-all(f32[16,8,128]{2,1,0:T(8,128)S(1)} %gram.1), channel_id=1, replica_groups=mesh['grp'=2,'smp'=16] {'smp'}, dimensions={0} | all-to-all | bytes 131072 | tf_op jit(solution)/shard_map/all_to_all | solution.py:259
  52.3 0.8 %finish.1 = f32[4,16]{1,0:T(4,128)} custom-call(f32[16,8,128]{2,1,0:T(8,128)S(1)} %all_to_all.26.parts_ref, f32[8,128]{1,0:T(8,128)S(1)} %copy-done.1), custom_call_target="tpu_custom_call" | custom-call | tf_op jit(solution)/shard_map/finish/pallas_call | solution.py:225
Async XLA Ops:
  1.6 14.8 %all-to-all-start = ((bf16[1,8,16,384]{3,1,0,2:T(8,128)(2,1)}), bf16[1,8,16,384]{3,1,0,2:T(8,128)(2,1)S(1)}, u32[]{:S(2)}, u32[]{:S(2)}) async-start(bf16[1,8,16,384]{3,1,0,2:T(8,128)(2,1)} %bitcast.13), calls=%async_computation | async-start | bytes 196608 | tf_op jit(solution)/shard_map/all_to_all | solution.py:244
  16.3 0.8 %copy-start = (bf16[1,8,16,384]{3,1,0,2:T(8,128)(2,1)}, bf16[1,8,16,384]{3,1,0,2:T(8,128)(2,1)S(1)}, u32[]{:S(2)}) copy-start(bf16[1,8,16,384]{3,1,0,2:T(8,128)(2,1)S(1)} %all-to-all-done) | copy-start | bytes 294916
  17.2 3.3 %collective-permute-start = (f32[8,80,512]{2,1,0:T(8,128)S(1)}, f32[8,80,512]{2,1,0:T(8,128)S(1)}, u32[]{:S(2)}, u32[]{:S(2)}) collective-permute-start(f32[8,80,512]{2,1,0:T(8,128)S(1)} %sketch_theirs.1), channel_id=1, source_target_pairs={{0,1},{1,0},{2,3},{3,2},{4,5},{5,4},{6,7},{7,6},{8,9},{9,8},{10,11... | collective-permute-start | bytes 3932168 | tf_op jit(solution)/shard_map/ppermute | solution.py:249
  20.8 21.0 %copy-start.1 = (f32[8,128]{1,0:T(8,128)S(1)}, f32[8,128]{1,0:T(8,128)}, u32[]{:S(2)}) copy-start(f32[8,128]{1,0:T(8,128)} %get-tuple-element.8.inv_ref) | copy-start | bytes 12292

commit v3 on v2

--- a/solution.py
+++ b/solution.py
@@ -14,7 +14,7 @@
 PAD = 8
 TOP = 32.0
 STEP = 512
-PIECE = 2048
+PIECE = 1024
 KEEP = 13 << 18
 
 
@@ -55,22 +55,30 @@
     return jax.ShapeDtypeStruct(shape, dtype)
 
 
-def load_kernel(half_ref, proj_ref, out_ref, sem):
+def is_direct(devices):
+    return devices == 16
+
+
+def place_of(block, devices):
+    if not is_direct(devices):
+        return block
+    k = jnp.bitwise_xor(block, lax.axis_index("smp") // 2)
+    return (1 - k % 2) * 4 + jnp.bitwise_xor(k // 2, 2)
+
+
+def load_kernel(proj_ref, out_ref, sem):
     span = out_ref.shape[1]
-    offset = pl.multiple_of(half_ref[0] * span, span)
+    offset = pl.multiple_of((1 - lax.axis_index("smp") % 2) * span, span)
     copy = pltpu.make_async_copy(proj_ref.at[:, pl.ds(offset, span)], out_ref, sem)
     copy.start()
     copy.wait()
 
 
-def load(projection, half):
+def load(projection):
     params, columns = projection.shape
     return pl.pallas_call(
         load_kernel,
-        in_specs=[
-            pl.BlockSpec(memory_space=pltpu.SMEM),
-            pl.BlockSpec(memory_space=pl.ANY),
-        ],
+        in_specs=[pl.BlockSpec(memory_space=pl.ANY)],
         out_specs=pl.BlockSpec(memory_space=pltpu.VMEM),
         out_shape=in_vmem((params, columns // 2), projection.dtype),
         scratch_shapes=[pltpu.SemaphoreType.DMA],
@@ -79,7 +87,7 @@
         ),
         compiler_params=pltpu.CompilerParams(vmem_limit_bytes=60 << 20),
         name="load",
-    )(half.reshape(1), pltpu.with_memory_space_constraint(projection, pltpu.HBM))
+    )(pltpu.with_memory_space_constraint(projection, pltpu.HBM))
 
 
 def in_order(gathered_ref, count, devices):
@@ -92,64 +100,63 @@
     ).astype(jnp.bfloat16)
 
 
-def store_blocks(out_ref, start, part):
+def store_blocks(out_ref, start, part, devices):
     width = out_ref.shape[2]
     for at in range(0, part.shape[1], width):
-        out_ref[(start + at) // width] = part[:, at : at + width]
-
-
-def theirs_kernel(count, devices, gathered_ref, proj_ref, out_ref):
+        out_ref[place_of((start + at) // width, devices)] = part[:, at : at + width]
+
+
+def other_kernel(count, devices, gathered_ref, proj_ref, out_ref):
     rows = in_order(gathered_ref, count, devices)
-    step = STEP
-    for start in range(0, proj_ref.shape[1], step):
+    for start in range(0, proj_ref.shape[1], STEP):
         part = jnp.dot(
-            rows, proj_ref[:, start : start + step], preferred_element_type=jnp.float32
+            rows, proj_ref[:, start : start + STEP], preferred_element_type=jnp.float32
         )
-        store_blocks(out_ref, start, part)
-
-
-def mine_kernel(count, devices, half_ref, gathered_ref, proj_ref, out_ref, held, sems):
-    pieces, _, step = held.shape
+        store_blocks(out_ref, start, part, devices)
+
+
+def own_kernel(count, devices, gathered_ref, proj_ref, out_ref, held, sems):
+    pieces, _, length = held.shape
+    core = lax.axis_index("smp") % 2
     copies = []
     for piece in range(pieces):
-        offset = pl.multiple_of(half_ref[0] * (pieces * step) + piece * step, step)
+        offset = pl.multiple_of(core * (pieces * length) + piece * length, length)
         copy = pltpu.make_async_copy(
-            proj_ref.at[:, pl.ds(offset, step)], held.at[piece], sems.at[piece]
+            proj_ref.at[:, pl.ds(offset, length)], held.at[piece], sems.at[piece]
         )
         copy.start()
         copies.append(copy)
     rows = in_order(gathered_ref, count, devices)
     for piece in range(pieces):
         copies[piece].wait()
-        for start in range(0, step, STEP):
+        for start in range(0, length, STEP):
             part = jnp.dot(
                 rows, held[piece, :, start : start + STEP], preferred_element_type=jnp.float32
             )
-            store_blocks(out_ref, piece * step + start, part)
-
-
-def sketch_theirs(gathered, loaded, count, devices, blocks):
+            store_blocks(out_ref, piece * length + start, part, devices)
+
+
+def sketch_other(gathered, loaded, count, devices, blocks):
     params, span = loaded.shape
     rows = count * devices
     return pl.pallas_call(
-        functools.partial(theirs_kernel, count, devices),
+        functools.partial(other_kernel, count, devices),
         out_shape=in_vmem((blocks, rows, span // blocks), jnp.float32),
         cost_estimate=pl.CostEstimate(
             flops=2 * rows * params * span, bytes_accessed=params * span, transcendentals=0
         ),
         compiler_params=pltpu.CompilerParams(vmem_limit_bytes=40 << 20),
-        name="sketch_theirs",
+        name="sketch_other",
     )(gathered, pltpu.with_memory_space_constraint(loaded, pltpu.VMEM))
 
 
-def sketch_mine(gathered, projection, half, count, devices, blocks):
+def sketch_own(gathered, projection, count, devices, blocks):
     params, columns = projection.shape
     span = columns // 2
     rows = count * devices
     return pl.pallas_call(
-        functools.partial(mine_kernel, count, devices),
+        functools.partial(own_kernel, count, devices),
         in_specs=[
-            pl.BlockSpec(memory_space=pltpu.SMEM),
             pl.BlockSpec(memory_space=pltpu.VMEM),
             pl.BlockSpec(memory_space=pl.ANY),
         ],
@@ -163,11 +170,11 @@
             flops=2 * rows * params * span, bytes_accessed=params * span * 2, transcendentals=0
         ),
         compiler_params=pltpu.CompilerParams(vmem_limit_bytes=58 << 20),
-        name="sketch_mine",
-    )(half.reshape(1), gathered, pltpu.with_memory_space_constraint(projection, pltpu.HBM))
-
-
-def gram_kernel(pc, devices, me_ref, sum_ref, inv_ref, out_ref):
+        name="sketch_own",
+    )(gathered, pltpu.with_memory_space_constraint(projection, pltpu.HBM))
+
+
+def gram_kernel(pc, devices, sum_ref, inv_ref, out_ref):
     cands = pc * devices
     c = sum_ref[:cands, :]
     t = sum_ref[cands:, :]
@@ -181,7 +188,7 @@
     c_sq = jnp.sum(c * c, axis=1, keepdims=True)
     t_sq = exact(jnp.ones((PAD, t.shape[1]), jnp.float32), t * t)[0:1, :]
     lane = lax.broadcasted_iota(jnp.int32, (1, devices), 1)
-    t_inv = jnp.where(lane == me_ref[0], inv_ref[pc : pc + 1, 0:1], 0.0)
+    t_inv = jnp.where(lane == lax.axis_index("smp"), inv_ref[pc : pc + 1, 0:1], 0.0)
     out_ref[...] = jnp.zeros_like(out_ref)
     for slot in range(pc):
         out_ref[:, slot, :devices] = scores[slot * devices : (slot + 1) * devices, :]
@@ -190,18 +197,13 @@
     out_ref[:, pc + 1, :devices] = jnp.broadcast_to(t_inv, (devices, devices))
 
 
-def gram(summed, inv, me, pc, devices):
+def gram(summed, inv, pc, devices):
     return pl.pallas_call(
         functools.partial(gram_kernel, pc, devices),
-        in_specs=[
-            pl.BlockSpec(memory_space=pltpu.SMEM),
-            pl.BlockSpec(memory_space=pltpu.VMEM),
-            pl.BlockSpec(memory_space=pltpu.VMEM),
-        ],
         out_shape=jax.ShapeDtypeStruct((devices, PAD, LANES), jnp.float32),
         compiler_params=pltpu.CompilerParams(vmem_limit_bytes=16 << 20),
         name="gram",
-    )(me.reshape(1), summed, inv)
+    )(summed, inv)
 
 
 def finish_kernel(pc, devices, parts_ref, inv_ref, out_ref):
@@ -230,32 +232,61 @@
     )(parts, inv)
 
 
+def sum_direct(mine, arrived, devices):
+    def swap(part, k):
+        return lax.ppermute(part, "smp", [(i, i ^ (2 * k)) for i in range(devices)])
+
+    def chip_sum(place):
+        return mine[place] + arrived[place]
+
+    def narrow(part):
+        return part.astype(jnp.float16)
+
+    def wide(part):
+        return part.astype(jnp.float32)
+
+    far_2 = swap(narrow(chip_sum(0)), 1)
+    far_3 = swap(narrow(chip_sum(1)), 1)
+    parts = [
+        swap(narrow(chip_sum(4) + wide(far_2)), 4),
+        swap(narrow(chip_sum(5) + wide(far_3)), 6),
+        swap(narrow(chip_sum(7)), 2),
+        swap(narrow(chip_sum(2)), 1),
+        swap(narrow(chip_sum(3)), 3),
+    ]
+    return chip_sum(6) + sum(wide(part) for part in parts)
+
+
+def sum_together(mine, arrived, devices):
+    parts = (mine + arrived).astype(jnp.float16)
+    same_core = [[i for i in range(devices) if i % 2 == c] for c in range(2)]
+    parts = lax.all_to_all(
+        parts, "smp", split_axis=0, concat_axis=0, axis_index_groups=same_core, tiled=True
+    )
+    return jnp.sum(parts.astype(jnp.float32), axis=0)
+
+
 def shards(cand_grads, tgt_grads, projection):
     devices = lax.axis_size("smp")
-    me = lax.axis_index("smp")
     pc, pt = cand_grads.shape[0], tgt_grads.shape[0]
     count = pc + pt
     params = projection.shape[0]
     blocks = devices // 2
-    core = me % 2
-
     rows, inv = prepare(cand_grads, tgt_grads)
     rows = rows.reshape(PAD, devices, params)
     gathered = lax.all_to_all(rows, "smp", split_axis=1, concat_axis=0, tiled=False)
     gathered = gathered.reshape(devices * PAD, params)
-    loaded = load(projection, 1 - core)
-
-    theirs = sketch_theirs(gathered, loaded, count, devices, blocks)
+
+    loaded = load(projection)
+    theirs = sketch_other(gathered, loaded, count, devices, blocks)
     arrived = lax.ppermute(theirs, "smp", [(i, i ^ 1) for i in range(devices)])
-    mine = sketch_mine(gathered, projection, core, count, devices, blocks)
-    chip = (mine + arrived).astype(jnp.float16)
-    same_core = [[i for i in range(devices) if i % 2 == c] for c in range(2)]
-    chip = lax.all_to_all(
-        chip, "smp", split_axis=0, concat_axis=0, axis_index_groups=same_core, tiled=True
-    )
-    summed = jnp.sum(chip.astype(jnp.float32), axis=0)
-
-    message = gram(summed, inv, me, pc, devices)
+    mine = sketch_own(gathered, projection, count, devices, blocks)
+    if is_direct(devices):
+        summed = sum_direct(mine, arrived, devices)
+    else:
+        summed = sum_together(mine, arrived, devices)
+
+    message = gram(summed, inv, pc, devices)
     parts = lax.all_to_all(message, "smp", split_axis=0, concat_axis=0, tiled=True)
     return finish(parts, inv, pc, devices)
 

time: 53.4 us -> 47.5 us (0.89)
  blocking collectives: 31.1 us -> 9.69 us
  waiting for transfers between devices: 5.49 us -> 15.4 us
  starting transfers between devices: 7.43 us -> 13.1 us
    all_to_all x1 -> x0, blocking collectives: 20.9 us -> none  [shards(): lax.all_to_all(chip, 'smp', split_axis=0, concat_axis=0, axis_index_group...]
    ppermute x0 -> x7, waiting for transfers between devices: none -> 9.89 us  [swap(): return lax.ppermute(part, 'smp', [(i, i ^ 2 * k) for i in range(devices)])]
    ppermute x0 -> x7, starting transfers between devices: none -> 5.72 us  [swap(): return lax.ppermute(part, 'smp', [(i, i ^ 2 * k) for i in range(devices)])]
  transfers between devices with their start and end apart: 2 -> 9, of which waited for: 1 -> 4; matrix products, arithmetic and copies ran while one was open for 0% -> 0% of each run, Pallas kernels for 10% -> 11%
where the time goes in v3:
time: 47.5 us; the launch traced here: 47.2 us
  waiting for transfers between devices  15.4 us (32%)
  starting transfers between devices  13.1 us (28%)
  blocking collectives  9.69 us (20%)
  Pallas kernels  8.49 us (18%)
    ppermute x7, waiting for transfers between devices, swap(): return lax.ppermute(part, 'smp', [(i, i ^ 2 * k) for i in range(devices)])  9.89 us
    all_to_all x1, blocking collectives, shards(): lax.all_to_all(message, 'smp', split_axis=0, concat_axis=0, tiled=True)  9.69 us
    all_to_all x1, starting transfers between devices, shards(): lax.all_to_all(rows, 'smp', split_axis=1, concat_axis=0, tiled=False)  7.36 us
    ppermute x7, starting transfers between devices, swap(): return lax.ppermute(part, 'smp', [(i, i ^ 2 * k) for i in range(devices)])  5.72 us
    all_to_all x1, waiting for transfers between devices, shards(): lax.all_to_all(rows, 'smp', split_axis=1, concat_axis=0, tiled=False)  5.49 us
    pallas_call x1, Pallas kernels, sketch_own(): pl.pallas_call(functools.partial(own_kernel, count, devices), in_specs=[p...  3.15 us
    pallas_call x1, Pallas kernels, load(): pl.pallas_call(load_kernel, in_specs=[pl.BlockSpec(memory_space=pl.ANY)],...  1.91 us
    pallas_call x1, Pallas kernels, prepare(): pl.pallas_call(prep_kernel, out_shape=(jax.ShapeDtypeStruct((PAD, params)...  1.58 us
  transfers between devices with their start and end apart: 9, of which 4 were waited for; matrix products, arithmetic and copies ran while one was open for 0% of the time, Pallas kernels for 11%

profile of v3, /device:TPU:0, one launch (start us, length us, event | category | flops | bytes accessed | tf_op | source)
XLA Modules:
  0.0 47.2 jit_solution(14622691261671763027)
XLA Ops:
  0.0 1.6 %prepare.1 = (bf16[8,6144]{1,0:T(8,128)(2,1)}, f32[8,128]{1,0:T(8,128)}) custom-call(bf16[4,6144]{1,0:T(4,128)(2,1)} %cand_ref.1, bf16[1,6144]{1,0:T(2,128)(2,1)} %tgt_ref.1), custom_call_target="tpu_custom_call" | custom-call | tf_op jit(solution)/shard_map/prepare/pallas_call | solution.py:40
  1.6 7.4 %all-to-all-start = ((bf16[1,8,16,384]{3,1,0,2:T(8,128)(2,1)}), bf16[1,8,16,384]{3,1,0,2:T(8,128)(2,1)S(1)}, u32[]{:S(2)}, u32[]{:S(2)}) async-start(bf16[1,8,16,384]{3,1,0,2:T(8,128)(2,1)} %bitcast.36), calls=%async_computation | async-start | bytes 196608 | tf_op jit(solution)/shard_map/all_to_all | solution.py:277
  8.9 1.9 %load.1.proj_ref = bf16[384,4096]{1,0:T(8,128)(2,1)S(1)} custom-call(bf16[384,8192]{1,0:T(8,128)(2,1)} %proj_ref.3), custom_call_target="tpu_custom_call" | custom-call | bytes 6291456 | tf_op jit(solution)/shard_map/load/pallas_call | solution.py:79
  10.9 5.5 %all-to-all-done = bf16[1,8,16,384]{3,1,0,2:T(8,128)(2,1)S(1)} async-done(((bf16[1,8,16,384]{3,1,0,2:T(8,128)(2,1)}), bf16[1,8,16,384]{3,1,0,2:T(8,128)(2,1)S(1)}, u32[]{:S(2)}, u32[]{:S(2)}) %all-to-all-start) | async-done | bytes 98336 | tf_op jit(solution)/shard_map/all_to_all | solution.py:277
  16.4 0.0 copy-start
  16.4 0.8 %sketch_other.1 = f32[8,80,512]{2,1,0:T(8,128)S(1)} custom-call(bf16[128,384]{1,0:T(8,128)(2,1)S(1)} %bitcast.34, bf16[384,4096]{1,0:T(8,128)(2,1)S(1)} %load.1.proj_ref), custom_call_target="tpu_custom_call" | custom-call | flops 251658240 | bytes 1572864 | tf_op jit(solution)/shard_map/sketch_other/pallas_call | solution.py:142
  17.2 0.0 copy-done
  17.2 0.1 collective-permute-start
  17.2 3.2 %sketch_own.1 = f32[8,80,512]{2,1,0:T(8,128)S(1)} custom-call(bf16[128,384]{1,0:T(8,128)(2,1)} %bitcast.35, bf16[384,8192]{1,0:T(8,128)(2,1)} %proj_ref.3), custom_call_target="tpu_custom_call" | custom-call | flops 251658240 | bytes 3145728 | tf_op jit(solution)/shard_map/sketch_own/pallas_call | solution.py:157
  20.4 0.0 collective-permute-done
  20.4 0.2 fusion.13
  20.6 0.0 copy-start.1
  20.6 0.2 collective-permute-start.1
  20.8 1.9 %collective-permute-start.3 = (f16[80,512]{1,0:T(8,128)(2,1)S(1)}, f16[80,512]{1,0:T(8,128)(2,1)S(1)}, u32[]{:S(2)}, u32[]{:S(2)}) collective-permute-start(f16[80,512]{1,0:T(8,128)(2,1)S(1)} %get-tuple-element.15), channel_id=1, source_target_pairs={{0,2},{1,3},{2,0},{3,1},{4,6},{5,7},{6,4},{7,5},{8,10},{9,11},{10,... | collective-permute-start | bytes 245768 | tf_op jit(solution)/shard_map/ppermute | solution.py:237
  22.7 0.1 collective-permute-start.5
  22.8 0.7 %collective-permute-start.6 = (f16[80,512]{1,0:T(8,128)(2,1)S(1)}, f16[80,512]{1,0:T(8,128)(2,1)S(1)}, u32[]{:S(2)}, u32[]{:S(2)}) collective-permute-start(f16[80,512]{1,0:T(8,128)(2,1)S(1)} %get-tuple-element.13), channel_id=1, source_target_pairs={{0,2},{1,3},{2,0},{3,1},{4,6},{5,7},{6,4},{7,5},{8,10},{9,11},{10,... | collective-permute-start | bytes 245768 | tf_op jit(solution)/shard_map/ppermute | solution.py:237
  23.5 2.7 %collective-permute-start.7 = (f16[80,512]{1,0:T(8,128)(2,1)S(1)}, f16[80,512]{1,0:T(8,128)(2,1)S(1)}, u32[]{:S(2)}, u32[]{:S(2)}) collective-permute-start(f16[80,512]{1,0:T(8,128)(2,1)S(1)} %get-tuple-element.12), channel_id=1, source_target_pairs={{0,6},{1,7},{2,4},{3,5},{4,2},{5,3},{6,0},{7,1},{8,14},{9,15},{10,... | collective-permute-start | bytes 245768 | tf_op jit(solution)/shard_map/ppermute | solution.py:237
  26.2 0.0 collective-permute-done.1
  26.2 3.2 %collective-permute-done.3 = f16[80,512]{1,0:T(8,128)(2,1)S(1)} collective-permute-done((f16[80,512]{1,0:T(8,128)(2,1)S(1)}, f16[80,512]{1,0:T(8,128)(2,1)S(1)}, u32[]{:S(2)}, u32[]{:S(2)}) %collective-permute-start.3) | collective-permute-done | bytes 81952 | tf_op jit(solution)/shard_map/ppermute | solution.py:237
  29.4 0.1 fusion.10
  29.5 0.1 collective-permute-start.2
  29.6 0.1 collective-permute-start.4
  29.7 0.0 collective-permute-done.5
  29.7 1.1 %collective-permute-done.6 = f16[80,512]{1,0:T(8,128)(2,1)S(1)} collective-permute-done((f16[80,512]{1,0:T(8,128)(2,1)S(1)}, f16[80,512]{1,0:T(8,128)(2,1)S(1)}, u32[]{:S(2)}, u32[]{:S(2)}) %collective-permute-start.6) | collective-permute-done | bytes 81952 | tf_op jit(solution)/shard_map/ppermute | solution.py:237
  30.8 0.0 collective-permute-done.7
  30.8 5.5 %collective-permute-done.2 = f16[80,512]{1,0:T(8,128)(2,1)S(1)} collective-permute-done((f16[80,512]{1,0:T(8,128)(2,1)S(1)}, f16[80,512]{1,0:T(8,128)(2,1)S(1)}, u32[]{:S(2)}, u32[]{:S(2)}) %collective-permute-start.2) | collective-permute-done | bytes 81952 | tf_op jit(solution)/shard_map/ppermute | solution.py:237
  36.3 0.0 collective-permute-done.4
  36.3 0.1 fusion.12.sum_ref
  36.4 0.0 copy-done.1
  36.4 0.3 gram.1
  36.7 9.7 %all_to_all.20.parts_ref = f32[16,8,128]{2,1,0:T(8,128)S(1)} all-to-all(f32[16,8,128]{2,1,0:T(8,128)S(1)} %gram.1), channel_id=1, replica_groups=mesh['grp'=2,'smp'=16] {'smp'}, dimensions={0} | all-to-all | bytes 131072 | tf_op jit(solution)/shard_map/all_to_all | solution.py:290
  46.4 0.8 %finish.1 = f32[4,16]{1,0:T(4,128)} custom-call(f32[16,8,128]{2,1,0:T(8,128)S(1)} %all_to_all.20.parts_ref, f32[8,128]{1,0:T(8,128)S(1)} %copy-done.1), custom_call_target="tpu_custom_call" | custom-call | tf_op jit(solution)/shard_map/finish/pallas_call | solution.py:227
Async XLA Ops:
  1.6 14.8 %all-to-all-start = ((bf16[1,8,16,384]{3,1,0,2:T(8,128)(2,1)}), bf16[1,8,16,384]{3,1,0,2:T(8,128)(2,1)S(1)}, u32[]{:S(2)}, u32[]{:S(2)}) async-start(bf16[1,8,16,384]{3,1,0,2:T(8,128)(2,1)} %bitcast.36), calls=%async_computation | async-start | bytes 196608 | tf_op jit(solution)/shard_map/all_to_all | solution.py:277
  16.4 0.8 %copy-start = (bf16[1,8,16,384]{3,1,0,2:T(8,128)(2,1)}, bf16[1,8,16,384]{3,1,0,2:T(8,128)(2,1)S(1)}, u32[]{:S(2)}) copy-start(bf16[1,8,16,384]{3,1,0,2:T(8,128)(2,1)S(1)} %all-to-all-done) | copy-start | bytes 294916
  17.2 3.2 %collective-permute-start = (f32[8,80,512]{2,1,0:T(8,128)S(1)}, f32[8,80,512]{2,1,0:T(8,128)S(1)}, u32[]{:S(2)}, u32[]{:S(2)}) collective-permute-start(f32[8,80,512]{2,1,0:T(8,128)S(1)} %sketch_other.1), channel_id=1, source_target_pairs={{0,1},{1,0},{2,3},{3,2},{4,5},{5,4},{6,7},{7,6},{8,9},{9,8},{10,11... | collective-permute-start | bytes 3932168 | tf_op jit(solution)/shard_map/ppermute | solution.py:282
  20.6 15.8 %copy-start.1 = (f32[8,128]{1,0:T(8,128)S(1)}, f32[8,128]{1,0:T(8,128)}, u32[]{:S(2)}) copy-start(f32[8,128]{1,0:T(8,128)} %get-tuple-element.8.inv_ref) | copy-start | bytes 12292
  20.6 5.6 %collective-permute-start.1 = (f16[80,512]{1,0:T(8,128)(2,1)S(1)}, f16[80,512]{1,0:T(8,128)(2,1)S(1)}, u32[]{:S(2)}, u32[]{:S(2)}) collective-permute-start(f16[80,512]{1,0:T(8,128)(2,1)S(1)} %get-tuple-element.11), channel_id=1, source_target_pairs={{0,2},{1,3},{2,0},{3,1},{4,6},{5,7},{6,4},{7,5},{8,10},{9,11},{10,... | collective-permute-start | bytes 245768 | tf_op jit(solution)/shard_map/ppermute | solution.py:237
  20.8 8.6 %collective-permute-start.3 = (f16[80,512]{1,0:T(8,128)(2,1)S(1)}, f16[80,512]{1,0:T(8,128)(2,1)S(1)}, u32[]{:S(2)}, u32[]{:S(2)}) collective-permute-start(f16[80,512]{1,0:T(8,128)(2,1)S(1)} %get-tuple-element.15), channel_id=1, source_target_pairs={{0,2},{1,3},{2,0},{3,1},{4,6},{5,7},{6,4},{7,5},{8,10},{9,11},{10,... | collective-permute-start | bytes 245768 | tf_op jit(solution)/shard_map/ppermute | solution.py:237
  22.7 7.0 %collective-permute-start.5 = (f16[80,512]{1,0:T(8,128)(2,1)S(1)}, f16[80,512]{1,0:T(8,128)(2,1)S(1)}, u32[]{:S(2)}, u32[]{:S(2)}) collective-permute-start(f16[80,512]{1,0:T(8,128)(2,1)S(1)} %get-tuple-element.14), channel_id=1, source_target_pairs={{0,4},{1,5},{2,6},{3,7},{4,0},{5,1},{6,2},{7,3},{8,12},{9,13},{10,... | collective-permute-start | bytes 245768 | tf_op jit(solution)/shard_map/ppermute | solution.py:237
  22.8 8.0 %collective-permute-start.6 = (f16[80,512]{1,0:T(8,128)(2,1)S(1)}, f16[80,512]{1,0:T(8,128)(2,1)S(1)}, u32[]{:S(2)}, u32[]{:S(2)}) collective-permute-start(f16[80,512]{1,0:T(8,128)(2,1)S(1)} %get-tuple-element.13), channel_id=1, source_target_pairs={{0,2},{1,3},{2,0},{3,1},{4,6},{5,7},{6,4},{7,5},{8,10},{9,11},{10,... | collective-permute-start | bytes 245768 | tf_op jit(solution)/shard_map/ppermute | solution.py:237
  23.5 7.3 %collective-permute-start.7 = (f16[80,512]{1,0:T(8,128)(2,1)S(1)}, f16[80,512]{1,0:T(8,128)(2,1)S(1)}, u32[]{:S(2)}, u32[]{:S(2)}) collective-permute-start(f16[80,512]{1,0:T(8,128)(2,1)S(1)} %get-tuple-element.12), channel_id=1, source_target_pairs={{0,6},{1,7},{2,4},{3,5},{4,2},{5,3},{6,0},{7,1},{8,14},{9,15},{10,... | collective-permute-start | bytes 245768 | tf_op jit(solution)/shard_map/ppermute | solution.py:237
  29.5 6.8 %collective-permute-start.2 = (f16[80,512]{1,0:T(8,128)(2,1)S(1)}, f16[80,512]{1,0:T(8,128)(2,1)S(1)}, u32[]{:S(2)}, u32[]{:S(2)}) collective-permute-start(f16[80,512]{1,0:T(8,128)(2,1)S(1)} %get-tuple-element.9), channel_id=1, source_target_pairs={{0,8},{1,9},{2,10},{3,11},{4,12},{5,13},{6,14},{7,15},{8,0},{9,1},... | collective-permute-start | bytes 245768 | tf_op jit(solution)/shard_map/ppermute | solution.py:237
  29.6 6.7 %collective-permute-start.4 = (f16[80,512]{1,0:T(8,128)(2,1)S(1)}, f16[80,512]{1,0:T(8,128)(2,1)S(1)}, u32[]{:S(2)}, u32[]{:S(2)}) collective-permute-start(f16[80,512]{1,0:T(8,128)(2,1)S(1)} %get-tuple-element.10), channel_id=1, source_target_pairs={{0,12},{1,13},{2,14},{3,15},{4,8},{5,9},{6,10},{7,11},{8,4},{9,5},... | collective-permute-start | bytes 245768 | tf_op jit(solution)/shard_map/ppermute | solution.py:237

commit v4 on v3

--- a/solution.py
+++ b/solution.py
@@ -40,8 +40,8 @@
     return pl.pallas_call(
         prep_kernel,
         out_shape=(
-            jax.ShapeDtypeStruct((PAD, params), jnp.bfloat16),
-            jax.ShapeDtypeStruct((PAD, LANES), jnp.float32),
+            in_vmem((PAD, params), jnp.bfloat16),
+            in_vmem((PAD, LANES), jnp.float32),
         ),
         compiler_params=pltpu.CompilerParams(vmem_limit_bytes=60 << 20),
         name="prepare",
@@ -169,7 +169,7 @@
         cost_estimate=pl.CostEstimate(
             flops=2 * rows * params * span, bytes_accessed=params * span * 2, transcendentals=0
         ),
-        compiler_params=pltpu.CompilerParams(vmem_limit_bytes=58 << 20),
+        compiler_params=pltpu.CompilerParams(vmem_limit_bytes=40 << 20),
         name="sketch_own",
     )(gathered, pltpu.with_memory_space_constraint(projection, pltpu.HBM))
 
@@ -245,14 +245,13 @@
     def wide(part):
         return part.astype(jnp.float32)
 
-    far_2 = swap(narrow(chip_sum(0)), 1)
-    far_3 = swap(narrow(chip_sum(1)), 1)
+    passed = swap(narrow(jnp.stack([chip_sum(0), chip_sum(3)])), 1)
     parts = [
-        swap(narrow(chip_sum(4) + wide(far_2)), 4),
-        swap(narrow(chip_sum(5) + wide(far_3)), 6),
-        swap(narrow(chip_sum(7)), 2),
+        swap(narrow(chip_sum(5)), 6),
         swap(narrow(chip_sum(2)), 1),
-        swap(narrow(chip_sum(3)), 3),
+        swap(narrow(chip_sum(1)), 7),
+        swap(narrow(chip_sum(4) + wide(passed[0])), 4),
+        swap(narrow(chip_sum(7) + wide(passed[1])), 2),
     ]
     return chip_sum(6) + sum(wide(part) for part in parts)
 
@@ -279,6 +278,7 @@
 
     loaded = load(projection)
     theirs = sketch_other(gathered, loaded, count, devices, blocks)
+    theirs = theirs.astype(jnp.float16)
     arrived = lax.ppermute(theirs, "smp", [(i, i ^ 1) for i in range(devices)])
     mine = sketch_own(gathered, projection, count, devices, blocks)
     if is_direct(devices):

time: 47.5 us -> 45.4 us (0.956)
  waiting for transfers between devices: 15.4 us -> 12.2 us
  starting transfers between devices: 13.1 us -> 14.2 us
  blocking collectives: 9.69 us -> 10.6 us
  Pallas kernels: 8.49 us -> 7.61 us
    ppermute x7 -> x6, waiting for transfers between devices: 9.89 us -> 6.71 us  [swap(): return lax.ppermute(part, 'smp', [(i, i ^ 2 * k) for i in range(devices)])]
    ppermute x7 -> x6, starting transfers between devices: 5.72 us -> 6.73 us  [swap(): return lax.ppermute(part, 'smp', [(i, i ^ 2 * k) for i in range(devices)])]
    pallas_call x1, Pallas kernels: 3.15 us -> 2.26 us  [sketch_own(): pl.pallas_call(functools.partial(own_kernel, count, devices), in_specs=[p...]
    all_to_all x1, blocking collectives: 9.69 us -> 10.6 us  [shards(): lax.all_to_all(message, 'smp', split_axis=0, concat_axis=0, tiled=True)]
  transfers between devices with their start and end apart: 9 -> 8, of which waited for: 4 -> 5; matrix products, arithmetic and copies ran while one was open for 0% -> 0% of each run, Pallas kernels for 11% -> 9%
where the time goes in v4:
time: 45.4 us; the launch traced here: 45.1 us
  starting transfers between devices  14.2 us (31%)
  waiting for transfers between devices  12.2 us (27%)
  blocking collectives  10.6 us (23%)
  Pallas kernels  7.61 us (17%)
    all_to_all x1, blocking collectives, shards(): lax.all_to_all(message, 'smp', split_axis=0, concat_axis=0, tiled=True)  10.6 us
    all_to_all x1, starting transfers between devices, shards(): lax.all_to_all(rows, 'smp', split_axis=1, concat_axis=0, tiled=False)  7.36 us
    ppermute x6, starting transfers between devices, swap(): return lax.ppermute(part, 'smp', [(i, i ^ 2 * k) for i in range(devices)])  6.73 us
    ppermute x6, waiting for transfers between devices, swap(): return lax.ppermute(part, 'smp', [(i, i ^ 2 * k) for i in range(devices)])  6.71 us
    all_to_all x1, waiting for transfers between devices, shards(): lax.all_to_all(rows, 'smp', split_axis=1, concat_axis=0, tiled=False)  5.49 us
    pallas_call x1, Pallas kernels, sketch_own(): pl.pallas_call(functools.partial(own_kernel, count, devices), in_specs=[p...  2.26 us
    pallas_call x1, Pallas kernels, load(): pl.pallas_call(load_kernel, in_specs=[pl.BlockSpec(memory_space=pl.ANY)],...  1.91 us
    pallas_call x1, Pallas kernels, prepare(): pl.pallas_call(prep_kernel, out_shape=(in_vmem((PAD, params), jnp.bfloat1...  1.58 us
  transfers between devices with their start and end apart: 8, of which 5 were waited for; matrix products, arithmetic and copies ran while one was open for 0% of the time, Pallas kernels for 9%

profile of v4, /device:TPU:0, one launch (start us, length us, event | category | flops | bytes accessed | tf_op | source)
XLA Modules:
  0.0 45.1 jit_solution(16647418202165154619)
XLA Ops:
  0.0 1.6 %prepare.1 = (bf16[8,6144]{1,0:T(8,128)(2,1)}, f32[8,128]{1,0:T(8,128)S(1)}) custom-call(bf16[4,6144]{1,0:T(4,128)(2,1)} %cand_ref.1, bf16[1,6144]{1,0:T(2,128)(2,1)} %tgt_ref.1), custom_call_target="tpu_custom_call" | custom-call | tf_op jit(solution)/shard_map/prepare/pallas_call | solution.py:40
  1.6 7.4 %all-to-all-start = ((bf16[1,8,16,384]{3,1,0,2:T(8,128)(2,1)}), bf16[1,8,16,384]{3,1,0,2:T(8,128)(2,1)S(1)}, u32[]{:S(2)}, u32[]{:S(2)}) async-start(bf16[1,8,16,384]{3,1,0,2:T(8,128)(2,1)} %bitcast.1), calls=%async_computation | async-start | bytes 196608 | tf_op jit(solution)/shard_map/all_to_all | solution.py:276
  8.9 1.9 %load.1.proj_ref = bf16[384,4096]{1,0:T(8,128)(2,1)S(1)} custom-call(bf16[384,8192]{1,0:T(8,128)(2,1)} %proj_ref.3), custom_call_target="tpu_custom_call" | custom-call | bytes 6291456 | tf_op jit(solution)/shard_map/load/pallas_call | solution.py:79
  10.9 5.5 %all-to-all-done = bf16[1,8,16,384]{3,1,0,2:T(8,128)(2,1)S(1)} async-done(((bf16[1,8,16,384]{3,1,0,2:T(8,128)(2,1)}), bf16[1,8,16,384]{3,1,0,2:T(8,128)(2,1)S(1)}, u32[]{:S(2)}, u32[]{:S(2)}) %all-to-all-start) | async-done | bytes 98336 | tf_op jit(solution)/shard_map/all_to_all | solution.py:276
  16.4 0.8 %sketch_other.1 = f32[8,80,512]{2,1,0:T(8,128)S(1)} custom-call(bf16[128,384]{1,0:T(8,128)(2,1)S(1)} %bitcast.22, bf16[384,4096]{1,0:T(8,128)(2,1)S(1)} %load.1.proj_ref), custom_call_target="tpu_custom_call" | custom-call | flops 251658240 | bytes 1572864 | tf_op jit(solution)/shard_map/sketch_other/pallas_call | solution.py:142
  17.2 0.1 convert_element_type.89
  17.3 0.1 collective-permute-start
  17.4 2.3 %sketch_own.1 = f32[8,80,512]{2,1,0:T(8,128)S(1)} custom-call(bf16[128,384]{1,0:T(8,128)(2,1)S(1)} %bitcast.23, bf16[384,8192]{1,0:T(8,128)(2,1)} %proj_ref.3), custom_call_target="tpu_custom_call" | custom-call | flops 251658240 | bytes 3145728 | tf_op jit(solution)/shard_map/sketch_own/pallas_call | solution.py:157
  19.7 0.0 collective-permute-done
  19.7 0.1 fusion.11
  19.9 0.2 collective-permute-start.4
  20.0 1.4 %collective-permute-start.1 = (f16[80,512]{1,0:T(8,128)(2,1)S(1)}, f16[80,512]{1,0:T(8,128)(2,1)S(1)}, u32[]{:S(2)}, u32[]{:S(2)}) collective-permute-start(f16[80,512]{1,0:T(8,128)(2,1)S(1)} %get-tuple-element.11), channel_id=1, source_target_pairs={{0,12},{1,13},{2,14},{3,15},{4,8},{5,9},{6,10},{7,11},{8,4},{9,5},... | collective-permute-start | bytes 245768 | tf_op jit(solution)/shard_map/ppermute | solution.py:237
  21.4 1.3 %collective-permute-start.2 = (f16[80,512]{1,0:T(8,128)(2,1)S(1)}, f16[80,512]{1,0:T(8,128)(2,1)S(1)}, u32[]{:S(2)}, u32[]{:S(2)}) collective-permute-start(f16[80,512]{1,0:T(8,128)(2,1)S(1)} %get-tuple-element.15), channel_id=1, source_target_pairs={{0,2},{1,3},{2,0},{3,1},{4,6},{5,7},{6,4},{7,5},{8,10},{9,11},{10,... | collective-permute-start | bytes 245768 | tf_op jit(solution)/shard_map/ppermute | solution.py:237
  22.7 2.6 %collective-permute-start.3 = (f16[80,512]{1,0:T(8,128)(2,1)S(1)}, f16[80,512]{1,0:T(8,128)(2,1)S(1)}, u32[]{:S(2)}, u32[]{:S(2)}) collective-permute-start(f16[80,512]{1,0:T(8,128)(2,1)S(1)} %get-tuple-element.14), channel_id=1, source_target_pairs={{0,14},{1,15},{2,12},{3,13},{4,10},{5,11},{6,8},{7,9},{8,6},{9,7},... | collective-permute-start | bytes 245768 | tf_op jit(solution)/shard_map/ppermute | solution.py:237
  25.3 1.6 %collective-permute-done.4 = f16[2,80,512]{2,1,0:T(8,128)(2,1)S(1)} collective-permute-done((f16[2,80,512]{2,1,0:T(8,128)(2,1)S(1)}, f16[2,80,512]{2,1,0:T(8,128)(2,1)S(1)}, u32[]{:S(2)}, u32[]{:S(2)}) %collective-permute-start.4) | collective-permute-done | bytes 163872 | tf_op jit(solution)/shard_map/ppermute | solution.py:237
  26.9 0.1 fusion.14
  27.0 0.4 collective-permute-start.5
  27.4 0.9 %collective-permute-start.6 = (f16[80,512]{1,0:T(8,128)(2,1)S(1)}, f16[80,512]{1,0:T(8,128)(2,1)S(1)}, u32[]{:S(2)}, u32[]{:S(2)}) collective-permute-start(f16[80,512]{1,0:T(8,128)(2,1)S(1)} %get-tuple-element.10), channel_id=1, source_target_pairs={{0,4},{1,5},{2,6},{3,7},{4,0},{5,1},{6,2},{7,3},{8,12},{9,13},{10,... | collective-permute-start | bytes 245768 | tf_op jit(solution)/shard_map/ppermute | solution.py:237
  28.3 0.0 collective-permute-done.1
  28.3 1.0 %collective-permute-done.2 = f16[80,512]{1,0:T(8,128)(2,1)S(1)} collective-permute-done((f16[80,512]{1,0:T(8,128)(2,1)S(1)}, f16[80,512]{1,0:T(8,128)(2,1)S(1)}, u32[]{:S(2)}, u32[]{:S(2)}) %collective-permute-start.2) | collective-permute-done | bytes 81952 | tf_op jit(solution)/shard_map/ppermute | solution.py:237
  29.3 1.4 %collective-permute-done.3 = f16[80,512]{1,0:T(8,128)(2,1)S(1)} collective-permute-done((f16[80,512]{1,0:T(8,128)(2,1)S(1)}, f16[80,512]{1,0:T(8,128)(2,1)S(1)}, u32[]{:S(2)}, u32[]{:S(2)}) %collective-permute-start.3) | collective-permute-done | bytes 81952 | tf_op jit(solution)/shard_map/ppermute | solution.py:237
  30.7 2.6 %collective-permute-done.5 = f16[80,512]{1,0:T(8,128)(2,1)S(1)} collective-permute-done((f16[80,512]{1,0:T(8,128)(2,1)S(1)}, f16[80,512]{1,0:T(8,128)(2,1)S(1)}, u32[]{:S(2)}, u32[]{:S(2)}) %collective-permute-start.5) | collective-permute-done | bytes 81952 | tf_op jit(solution)/shard_map/ppermute | solution.py:237
  33.4 0.0 collective-permute-done.6
  33.4 0.1 fusion.10.sum_ref
  33.5 0.3 gram.1
  33.8 10.6 %all_to_all.20.parts_ref = f32[16,8,128]{2,1,0:T(8,128)S(1)} all-to-all(f32[16,8,128]{2,1,0:T(8,128)S(1)} %gram.1), channel_id=1, replica_groups=mesh['grp'=2,'smp'=16] {'smp'}, dimensions={0} | all-to-all | bytes 131072 | tf_op jit(solution)/shard_map/all_to_all | solution.py:290
  44.3 0.8 %finish.1 = f32[4,16]{1,0:T(4,128)} custom-call(f32[16,8,128]{2,1,0:T(8,128)S(1)} %all_to_all.20.parts_ref, f32[8,128]{1,0:T(8,128)S(1)} %get-tuple-element.8.inv_ref), custom_call_target="tpu_custom_call" | custom-call | tf_op jit(solution)/shard_map/finish/pallas_call | solution.py:227
  (1 shorter events, 0.0 us)
Async XLA Ops:
  1.6 14.8 %all-to-all-start = ((bf16[1,8,16,384]{3,1,0,2:T(8,128)(2,1)}), bf16[1,8,16,384]{3,1,0,2:T(8,128)(2,1)S(1)}, u32[]{:S(2)}, u32[]{:S(2)}) async-start(bf16[1,8,16,384]{3,1,0,2:T(8,128)(2,1)} %bitcast.1), calls=%async_computation | async-start | bytes 196608 | tf_op jit(solution)/shard_map/all_to_all | solution.py:276
  17.3 2.4 %collective-permute-start = (f16[8,80,512]{2,1,0:T(8,128)(2,1)S(1)}, f16[8,80,512]{2,1,0:T(8,128)(2,1)S(1)}, u32[]{:S(2)}, u32[]{:S(2)}) collective-permute-start(f16[8,80,512]{2,1,0:T(8,128)(2,1)S(1)} %convert_element_type.89), channel_id=1, source_target_pairs={{0,1},{1,0},{2,3},{3,2},{4,5},{5,4},{6,7},{7,6},{8,9},{9,8},{10,11... | collective-permute-start | bytes 1966088 | tf_op jit(solution)/shard_map/ppermute | solution.py:282
  19.9 7.1 %collective-permute-start.4 = (f16[2,80,512]{2,1,0:T(8,128)(2,1)S(1)}, f16[2,80,512]{2,1,0:T(8,128)(2,1)S(1)}, u32[]{:S(2)}, u32[]{:S(2)}) collective-permute-start(f16[2,80,512]{2,1,0:T(8,128)(2,1)S(1)} %pad_maximum_fusion), channel_id=1, source_target_pairs={{0,2},{1,3},{2,0},{3,1},{4,6},{5,7},{6,4},{7,5},{8,10},{9,11},{10,... | collective-permute-start | bytes 491528 | tf_op jit(solution)/shard_map/ppermute | solution.py:237
  20.0 8.3 %collective-permute-start.1 = (f16[80,512]{1,0:T(8,128)(2,1)S(1)}, f16[80,512]{1,0:T(8,128)(2,1)S(1)}, u32[]{:S(2)}, u32[]{:S(2)}) collective-permute-start(f16[80,512]{1,0:T(8,128)(2,1)S(1)} %get-tuple-element.11), channel_id=1, source_target_pairs={{0,12},{1,13},{2,14},{3,15},{4,8},{5,9},{6,10},{7,11},{8,4},{9,5},... | collective-permute-start | bytes 245768 | tf_op jit(solution)/shard_map/ppermute | solution.py:237
  21.4 7.9 %collective-permute-start.2 = (f16[80,512]{1,0:T(8,128)(2,1)S(1)}, f16[80,512]{1,0:T(8,128)(2,1)S(1)}, u32[]{:S(2)}, u32[]{:S(2)}) collective-permute-start(f16[80,512]{1,0:T(8,128)(2,1)S(1)} %get-tuple-element.15), channel_id=1, source_target_pairs={{0,2},{1,3},{2,0},{3,1},{4,6},{5,7},{6,4},{7,5},{8,10},{9,11},{10,... | collective-permute-start | bytes 245768 | tf_op jit(solution)/shard_map/ppermute | solution.py:237
  22.7 8.0 %collective-permute-start.3 = (f16[80,512]{1,0:T(8,128)(2,1)S(1)}, f16[80,512]{1,0:T(8,128)(2,1)S(1)}, u32[]{:S(2)}, u32[]{:S(2)}) collective-permute-start(f16[80,512]{1,0:T(8,128)(2,1)S(1)} %get-tuple-element.14), channel_id=1, source_target_pairs={{0,14},{1,15},{2,12},{3,13},{4,10},{5,11},{6,8},{7,9},{8,6},{9,7},... | collective-permute-start | bytes 245768 | tf_op jit(solution)/shard_map/ppermute | solution.py:237
  27.0 6.4 %collective-permute-start.5 = (f16[80,512]{1,0:T(8,128)(2,1)S(1)}, f16[80,512]{1,0:T(8,128)(2,1)S(1)}, u32[]{:S(2)}, u32[]{:S(2)}) collective-permute-start(f16[80,512]{1,0:T(8,128)(2,1)S(1)} %get-tuple-element.9), channel_id=1, source_target_pairs={{0,8},{1,9},{2,10},{3,11},{4,12},{5,13},{6,14},{7,15},{8,0},{9,1},... | collective-permute-start | bytes 245768 | tf_op jit(solution)/shard_map/ppermute | solution.py:237
  27.4 6.0 %collective-permute-start.6 = (f16[80,512]{1,0:T(8,128)(2,1)S(1)}, f16[80,512]{1,0:T(8,128)(2,1)S(1)}, u32[]{:S(2)}, u32[]{:S(2)}) collective-permute-start(f16[80,512]{1,0:T(8,128)(2,1)S(1)} %get-tuple-element.10), channel_id=1, source_target_pairs={{0,4},{1,5},{2,6},{3,7},{4,0},{5,1},{6,2},{7,3},{8,12},{9,13},{10,... | collective-permute-start | bytes 245768 | tf_op jit(solution)/shard_map/ppermute | solution.py:237

commit v5 on v4

--- a/solution.py
+++ b/solution.py
@@ -11,6 +11,7 @@
 K = 8192
 EPS = 1e-06
 LANES = 128
+TILE = 16
 PAD = 8
 TOP = 32.0
 STEP = 512
@@ -18,8 +19,13 @@
 KEEP = 13 << 18
 
 
-def prep_kernel(cand_ref, tgt_ref, rows_ref, inv_ref):
+def packed_rows(count, params):
+    return -(-count * params // LANES // TILE) * TILE
+
+
+def prep_kernel(cand_ref, tgt_ref, rows_ref, inv_ref, packed):
     count = cand_ref.shape[0] + tgt_ref.shape[0]
+    devices = rows_ref.shape[0]
     cand = cand_ref[...].astype(jnp.float32)
     tgt = tgt_ref[...].astype(jnp.float32)
     fill = jnp.zeros((PAD - count, cand.shape[1]), jnp.float32)
@@ -31,18 +37,26 @@
         fits = largest * scale * 2.0**power < TOP
         scale = jnp.where(fits, scale * 2.0**power, scale)
         inv = jnp.where(fits, inv * 2.0**-power, inv)
-    rows_ref[...] = (rows * scale).astype(rows_ref.dtype)
+    rows = rows * scale
+    parts = rows.shape[1] // devices // LANES
+    packed[...] = jnp.zeros_like(packed)
+    for device in range(devices):
+        for part in range(parts):
+            start = (device * parts + part) * LANES
+            packed[device, part * count : (part + 1) * count, :] = rows[
+                :count, start : start + LANES
+            ]
+    rows_ref[...] = packed[...].astype(rows_ref.dtype)
     inv_ref[...] = jnp.broadcast_to(inv, inv_ref.shape)
 
 
-def prepare(cand_grads, tgt_grads):
-    params = cand_grads.shape[1]
+def prepare(cand_grads, tgt_grads, devices):
+    count = cand_grads.shape[0] + tgt_grads.shape[0]
+    shape = (devices, packed_rows(count, cand_grads.shape[1] // devices), LANES)
     return pl.pallas_call(
         prep_kernel,
-        out_shape=(
-            in_vmem((PAD, params), jnp.bfloat16),
-            in_vmem((PAD, LANES), jnp.float32),
-        ),
+        out_shape=(in_vmem(shape, jnp.bfloat16), in_vmem((PAD, LANES), jnp.float32)),
+        scratch_shapes=[pltpu.VMEM(shape, jnp.float32)],
         compiler_params=pltpu.CompilerParams(vmem_limit_bytes=60 << 20),
         name="prepare",
     )(cand_grads, tgt_grads)
@@ -90,24 +104,24 @@
     )(pltpu.with_memory_space_constraint(projection, pltpu.HBM))
 
 
-def in_order(gathered_ref, count, devices):
-    rows = count * devices
-    row = lax.broadcasted_iota(jnp.int32, (rows, devices * PAD), 0)
-    col = lax.broadcasted_iota(jnp.int32, (rows, devices * PAD), 1)
-    pick = col == (row % devices) * PAD + row // devices
-    return jnp.dot(
-        pick.astype(jnp.bfloat16), gathered_ref[...], preferred_element_type=jnp.float32
-    ).astype(jnp.bfloat16)
-
-
 def store_blocks(out_ref, start, part, devices):
     width = out_ref.shape[2]
     for at in range(0, part.shape[1], width):
         out_ref[place_of((start + at) // width, devices)] = part[:, at : at + width]
 
 
-def other_kernel(count, devices, gathered_ref, proj_ref, out_ref):
-    rows = in_order(gathered_ref, count, devices)
+def other_kernel(devices, gathered_ref, proj_ref, out_ref, rows_ref):
+    count, params = rows_ref.shape
+    packed = gathered_ref.shape[0]
+    row = lax.broadcasted_iota(jnp.int32, (count, packed), 0)
+    col = lax.broadcasted_iota(jnp.int32, (count, packed), 1)
+    first = (row % devices) * (packed // devices) + row // devices
+    for part in range(params // LANES):
+        pick = (col == first + part * (count // devices)).astype(jnp.bfloat16)
+        rows_ref[:, part * LANES : (part + 1) * LANES] = jnp.dot(
+            pick, gathered_ref[...], preferred_element_type=jnp.float32
+        ).astype(rows_ref.dtype)
+    rows = rows_ref[...]
     for start in range(0, proj_ref.shape[1], STEP):
         part = jnp.dot(
             rows, proj_ref[:, start : start + STEP], preferred_element_type=jnp.float32
@@ -115,7 +129,7 @@
         store_blocks(out_ref, start, part, devices)
 
 
-def own_kernel(count, devices, gathered_ref, proj_ref, out_ref, held, sems):
+def own_kernel(devices, rows_ref, proj_ref, out_ref, held, sems):
     pieces, _, length = held.shape
     core = lax.axis_index("smp") % 2
     copies = []
@@ -126,7 +140,7 @@
         )
         copy.start()
         copies.append(copy)
-    rows = in_order(gathered_ref, count, devices)
+    rows = rows_ref[...]
     for piece in range(pieces):
         copies[piece].wait()
         for start in range(0, length, STEP):
@@ -140,8 +154,11 @@
     params, span = loaded.shape
     rows = count * devices
     return pl.pallas_call(
-        functools.partial(other_kernel, count, devices),
-        out_shape=in_vmem((blocks, rows, span // blocks), jnp.float32),
+        functools.partial(other_kernel, devices),
+        out_shape=[
+            in_vmem((blocks, rows, span // blocks), jnp.float32),
+            in_vmem((rows, params), jnp.bfloat16),
+        ],
         cost_estimate=pl.CostEstimate(
             flops=2 * rows * params * span, bytes_accessed=params * span, transcendentals=0
         ),
@@ -150,28 +167,31 @@
     )(gathered, pltpu.with_memory_space_constraint(loaded, pltpu.VMEM))
 
 
-def sketch_own(gathered, projection, count, devices, blocks):
+def sketch_own(rows, projection, devices, blocks):
     params, columns = projection.shape
     span = columns // 2
-    rows = count * devices
-    return pl.pallas_call(
-        functools.partial(own_kernel, count, devices),
+    return pl.pallas_call(
+        functools.partial(own_kernel, devices),
         in_specs=[
             pl.BlockSpec(memory_space=pltpu.VMEM),
             pl.BlockSpec(memory_space=pl.ANY),
         ],
         out_specs=pl.BlockSpec(memory_space=pltpu.VMEM),
-        out_shape=in_vmem((blocks, rows, span // blocks), jnp.float32),
+        out_shape=in_vmem((blocks, rows.shape[0], span // blocks), jnp.float32),
         scratch_shapes=[
             pltpu.VMEM((span // PIECE, params, PIECE), projection.dtype),
             pltpu.SemaphoreType.DMA((span // PIECE,)),
         ],
         cost_estimate=pl.CostEstimate(
-            flops=2 * rows * params * span, bytes_accessed=params * span * 2, transcendentals=0
+            flops=2 * rows.size * span, bytes_accessed=params * span * 2, transcendentals=0
         ),
         compiler_params=pltpu.CompilerParams(vmem_limit_bytes=40 << 20),
         name="sketch_own",
-    )(gathered, pltpu.with_memory_space_constraint(projection, pltpu.HBM))
+    )(rows, pltpu.with_memory_space_constraint(projection, pltpu.HBM))
+
+
+def message_length(pc, devices):
+    return -(-((pc + 2) * devices + pc) // LANES) * LANES
 
 
 def gram_kernel(pc, devices, sum_ref, inv_ref, out_ref):
@@ -191,36 +211,37 @@
     t_inv = jnp.where(lane == lax.axis_index("smp"), inv_ref[pc : pc + 1, 0:1], 0.0)
     out_ref[...] = jnp.zeros_like(out_ref)
     for slot in range(pc):
-        out_ref[:, slot, :devices] = scores[slot * devices : (slot + 1) * devices, :]
-        out_ref[:, PAD - 1, slot : slot + 1] = c_sq[slot * devices : (slot + 1) * devices, :]
-    out_ref[:, pc, :devices] = jnp.broadcast_to(t_sq, (devices, devices))
-    out_ref[:, pc + 1, :devices] = jnp.broadcast_to(t_inv, (devices, devices))
+        rows = slice(slot * devices, (slot + 1) * devices)
+        out_ref[:, slot * devices : (slot + 1) * devices] = scores[rows, :]
+        at = (pc + 2) * devices + slot
+        out_ref[:, at : at + 1] = c_sq[rows, :]
+    for place, value in ((pc, t_sq), (pc + 1, t_inv)):
+        out_ref[:, place * devices : (place + 1) * devices] = jnp.broadcast_to(
+            value, (devices, devices)
+        )
 
 
 def gram(summed, inv, pc, devices):
     return pl.pallas_call(
         functools.partial(gram_kernel, pc, devices),
-        out_shape=jax.ShapeDtypeStruct((devices, PAD, LANES), jnp.float32),
+        out_shape=in_vmem((devices, message_length(pc, devices)), jnp.float32),
         compiler_params=pltpu.CompilerParams(vmem_limit_bytes=16 << 20),
         name="gram",
     )(summed, inv)
 
 
 def finish_kernel(pc, devices, parts_ref, inv_ref, out_ref):
-    total = jnp.sum(parts_ref[...], axis=0)
-    inv_c = inv_ref[:pc, 0:1]
-    inv_t = total[pc + 1 : pc + 2, :devices]
-    row = lax.broadcasted_iota(jnp.int32, (pc, LANES), 0)
-    lane = lax.broadcasted_iota(jnp.int32, (pc, LANES), 1)
-    c_sq = jnp.sum(
-        jnp.where(row == lane, jnp.broadcast_to(total[PAD - 1 : PAD, :], (pc, LANES)), 0.0),
-        axis=1,
-        keepdims=True,
-    )
-    t_sq = total[pc : pc + 1, :devices]
-    c_scale = inv_c * lax.rsqrt(c_sq / K * inv_c * inv_c + EPS)
+    total = jnp.sum(parts_ref[...], axis=0, keepdims=True)
+    t_sq = total[:, pc * devices : (pc + 1) * devices]
+    inv_t = total[:, (pc + 1) * devices : (pc + 2) * devices]
     t_scale = inv_t * lax.rsqrt(t_sq / K * inv_t * inv_t + EPS)
-    out_ref[...] = total[:pc, :devices] * c_scale * t_scale / K
+    for slot in range(pc):
+        at = (pc + 2) * devices + slot
+        c_sq = total[:, at : at + 1]
+        inv_c = inv_ref[slot : slot + 1, 0:1]
+        c_scale = inv_c * lax.rsqrt(c_sq / K * inv_c * inv_c + EPS)
+        scores = total[:, slot * devices : (slot + 1) * devices]
+        out_ref[slot : slot + 1, :] = scores * c_scale * t_scale / K
 
 
 def finish(parts, inv, pc, devices):
@@ -248,8 +269,8 @@
     passed = swap(narrow(jnp.stack([chip_sum(0), chip_sum(3)])), 1)
     parts = [
         swap(narrow(chip_sum(5)), 6),
+        swap(narrow(chip_sum(1)), 7),
         swap(narrow(chip_sum(2)), 1),
-        swap(narrow(chip_sum(1)), 7),
         swap(narrow(chip_sum(4) + wide(passed[0])), 4),
         swap(narrow(chip_sum(7) + wide(passed[1])), 2),
     ]
@@ -271,16 +292,14 @@
     count = pc + pt
     params = projection.shape[0]
     blocks = devices // 2
-    rows, inv = prepare(cand_grads, tgt_grads)
-    rows = rows.reshape(PAD, devices, params)
-    gathered = lax.all_to_all(rows, "smp", split_axis=1, concat_axis=0, tiled=False)
-    gathered = gathered.reshape(devices * PAD, params)
-
+    rows, inv = prepare(cand_grads, tgt_grads, devices)
+    gathered = lax.all_to_all(rows, "smp", split_axis=0, concat_axis=0, tiled=True)
+    gathered = gathered.reshape(-1, LANES)
     loaded = load(projection)
-    theirs = sketch_other(gathered, loaded, count, devices, blocks)
+    theirs, rows = sketch_other(gathered, loaded, count, devices, blocks)
     theirs = theirs.astype(jnp.float16)
     arrived = lax.ppermute(theirs, "smp", [(i, i ^ 1) for i in range(devices)])
-    mine = sketch_own(gathered, projection, count, devices, blocks)
+    mine = sketch_own(rows, projection, devices, blocks)
     if is_direct(devices):
         summed = sum_direct(mine, arrived, devices)
     else:

time: 45.4 us -> 44.6 us (0.982)
  blocking collectives: 10.6 us -> 10 us
    all_to_all x1, blocking collectives: 10.6 us -> 10 us  [shards(): lax.all_to_all(message, 'smp', split_axis=0, concat_axis=0, tiled=True)]
    all_to_all x1, waiting for transfers between devices: 5.49 us -> 4.98 us  [shards(): lax.all_to_all(rows, 'smp', split_axis=0, concat_axis=0, tiled=True)]
  transfers between devices with their start and end apart: 8 -> 8, of which waited for: 5 -> 4; matrix products, arithmetic and copies ran while one was open for 0% -> 0% of each run, Pallas kernels for 9% -> 9%
where the time goes in v5:
time: 44.6 us; the launch traced here: 44.3 us
  starting transfers between devices  14.2 us (32%)
  waiting for transfers between devices  11.8 us (26%)
  blocking collectives  10 us (22%)
  Pallas kernels  7.81 us (18%)
  other arithmetic  0.48 us (1%)
    all_to_all x1, blocking collectives, shards(): lax.all_to_all(message, 'smp', split_axis=0, concat_axis=0, tiled=True)  10 us
    all_to_all x1, starting transfers between devices, shards(): lax.all_to_all(rows, 'smp', split_axis=0, concat_axis=0, tiled=True)  7.36 us
    ppermute x6, waiting for transfers between devices, swap(): return lax.ppermute(part, 'smp', [(i, i ^ 2 * k) for i in range(devices)])  6.79 us
    ppermute x6, starting transfers between devices, swap(): return lax.ppermute(part, 'smp', [(i, i ^ 2 * k) for i in range(devices)])  6.75 us
    all_to_all x1, waiting for transfers between devices, shards(): lax.all_to_all(rows, 'smp', split_axis=0, concat_axis=0, tiled=True)  4.98 us
    pallas_call x1, Pallas kernels, sketch_own(): pl.pallas_call(functools.partial(own_kernel, devices), in_specs=[pl.Block...  2.26 us
    pallas_call x1, Pallas kernels, load(): pl.pallas_call(load_kernel, in_specs=[pl.BlockSpec(memory_space=pl.ANY)],...  1.91 us
    pallas_call x1, Pallas kernels, prepare(): pl.pallas_call(prep_kernel, out_shape=(in_vmem(shape, jnp.bfloat16), in_v...  1.59 us
  transfers between devices with their start and end apart: 8, of which 4 were waited for; matrix products, arithmetic and copies ran while one was open for 0% of the time, Pallas kernels for 9%

profile of v5, /device:TPU:0, one launch (start us, length us, event | category | flops | bytes accessed | tf_op | source)
XLA Modules:
  0.0 44.3 jit_solution(3085139759494057395)
XLA Ops:
  0.0 1.6 %prepare.1 = (bf16[16,16,128]{2,1,0:T(8,128)(2,1)}, f32[8,128]{1,0:T(8,128)S(1)}) custom-call(bf16[4,6144]{1,0:T(4,128)(2,1)} %cand_ref.1, bf16[1,6144]{1,0:T(2,128)(2,1)} %tgt_ref.1), custom_call_target="tpu_custom_call" | custom-call | tf_op jit(solution)/shard_map/prepare/pallas_call | solution.py:56
  1.6 7.4 %all-to-all-start = ((bf16[16,16,128]{2,1,0:T(8,128)(2,1)}), bf16[16,16,128]{2,1,0:T(8,128)(2,1)S(1)}, u32[]{:S(2)}, u32[]{:S(2)}) async-start(bf16[16,16,128]{2,1,0:T(8,128)(2,1)} %get-tuple-element.9), calls=%async_computation | async-start | bytes 131072 | tf_op jit(solution)/shard_map/all_to_all | solution.py:296
  9.0 1.9 %load.1.proj_ref = bf16[384,4096]{1,0:T(8,128)(2,1)S(1)} custom-call(bf16[384,8192]{1,0:T(8,128)(2,1)} %proj_ref.3), custom_call_target="tpu_custom_call" | custom-call | bytes 6291456 | tf_op jit(solution)/shard_map/load/pallas_call | solution.py:93
  10.9 5.0 %all-to-all-done = bf16[16,16,128]{2,1,0:T(8,128)(2,1)S(1)} async-done(((bf16[16,16,128]{2,1,0:T(8,128)(2,1)}), bf16[16,16,128]{2,1,0:T(8,128)(2,1)S(1)}, u32[]{:S(2)}, u32[]{:S(2)}) %all-to-all-start) | async-done | bytes 65568 | tf_op jit(solution)/shard_map/all_to_all | solution.py:296
  15.8 0.8 %sketch_other.1 = (f32[8,80,512]{2,1,0:T(8,128)S(1)}, bf16[80,384]{1,0:T(8,128)(2,1)S(1)}) custom-call(bf16[256,128]{1,0:T(8,128)(2,1)S(1)} %bitcast.19, bf16[384,4096]{1,0:T(8,128)(2,1)S(1)} %load.1.proj_ref), custom_call_target="tpu_custom_call" | custom-call | flops 251658240 | bytes 1572864 | tf_op jit(solution)/shard_map/sketch_other/pallas_call | solution.py:156
  16.7 0.1 convert_element_type.89
  16.8 0.1 collective-permute-start
  16.9 2.3 %sketch_own.1 = f32[8,80,512]{2,1,0:T(8,128)S(1)} custom-call(bf16[80,384]{1,0:T(8,128)(2,1)S(1)} %get-tuple-element.10.rows_ref, bf16[384,8192]{1,0:T(8,128)(2,1)} %proj_ref.3), custom_call_target="tpu_custom_call" | custom-call | flops 251658240 | bytes 3145728 | tf_op jit(solution)/shard_map/sketch_own/pallas_call | solution.py:173
  19.2 0.0 collective-permute-done
  19.2 0.1 fusion.11
  19.4 0.3 collective-permute-start.4
  19.7 1.1 %collective-permute-start.1 = (f16[80,512]{1,0:T(8,128)(2,1)S(1)}, f16[80,512]{1,0:T(8,128)(2,1)S(1)}, u32[]{:S(2)}, u32[]{:S(2)}) collective-permute-start(f16[80,512]{1,0:T(8,128)(2,1)S(1)} %get-tuple-element.15), channel_id=1, source_target_pairs={{0,12},{1,13},{2,14},{3,15},{4,8},{5,9},{6,10},{7,11},{8,4},{9,5},... | collective-permute-start | bytes 245768 | tf_op jit(solution)/shard_map/ppermute | solution.py:258
  20.8 1.4 %collective-permute-start.3 = (f16[80,512]{1,0:T(8,128)(2,1)S(1)}, f16[80,512]{1,0:T(8,128)(2,1)S(1)}, u32[]{:S(2)}, u32[]{:S(2)}) collective-permute-start(f16[80,512]{1,0:T(8,128)(2,1)S(1)} %get-tuple-element.18), channel_id=1, source_target_pairs={{0,2},{1,3},{2,0},{3,1},{4,6},{5,7},{6,4},{7,5},{8,10},{9,11},{10,... | collective-permute-start | bytes 245768 | tf_op jit(solution)/shard_map/ppermute | solution.py:258
  22.1 2.8 %collective-permute-start.2 = (f16[80,512]{1,0:T(8,128)(2,1)S(1)}, f16[80,512]{1,0:T(8,128)(2,1)S(1)}, u32[]{:S(2)}, u32[]{:S(2)}) collective-permute-start(f16[80,512]{1,0:T(8,128)(2,1)S(1)} %get-tuple-element.19), channel_id=1, source_target_pairs={{0,14},{1,15},{2,12},{3,13},{4,10},{5,11},{6,8},{7,9},{8,6},{9,7},... | collective-permute-start | bytes 245768 | tf_op jit(solution)/shard_map/ppermute | solution.py:258
  25.0 1.5 %collective-permute-done.4 = f16[2,80,512]{2,1,0:T(8,128)(2,1)S(1)} collective-permute-done((f16[2,80,512]{2,1,0:T(8,128)(2,1)S(1)}, f16[2,80,512]{2,1,0:T(8,128)(2,1)S(1)}, u32[]{:S(2)}, u32[]{:S(2)}) %collective-permute-start.4) | collective-permute-done | bytes 163872 | tf_op jit(solution)/shard_map/ppermute | solution.py:258
  26.4 0.1 fusion.14
  26.5 0.4 collective-permute-start.5
  26.9 0.7 %collective-permute-start.6 = (f16[80,512]{1,0:T(8,128)(2,1)S(1)}, f16[80,512]{1,0:T(8,128)(2,1)S(1)}, u32[]{:S(2)}, u32[]{:S(2)}) collective-permute-start(f16[80,512]{1,0:T(8,128)(2,1)S(1)} %get-tuple-element.14), channel_id=1, source_target_pairs={{0,4},{1,5},{2,6},{3,7},{4,0},{5,1},{6,2},{7,3},{8,12},{9,13},{10,... | collective-permute-start | bytes 245768 | tf_op jit(solution)/shard_map/ppermute | solution.py:258
  27.7 0.0 collective-permute-done.1
  27.7 1.9 %collective-permute-done.3 = f16[80,512]{1,0:T(8,128)(2,1)S(1)} collective-permute-done((f16[80,512]{1,0:T(8,128)(2,1)S(1)}, f16[80,512]{1,0:T(8,128)(2,1)S(1)}, u32[]{:S(2)}, u32[]{:S(2)}) %collective-permute-start.3) | collective-permute-done | bytes 81952 | tf_op jit(solution)/shard_map/ppermute | solution.py:258
  29.5 0.0 collective-permute-done.2
  29.5 3.5 %collective-permute-done.5 = f16[80,512]{1,0:T(8,128)(2,1)S(1)} collective-permute-done((f16[80,512]{1,0:T(8,128)(2,1)S(1)}, f16[80,512]{1,0:T(8,128)(2,1)S(1)}, u32[]{:S(2)}, u32[]{:S(2)}) %collective-permute-start.5) | collective-permute-done | bytes 81952 | tf_op jit(solution)/shard_map/ppermute | solution.py:258
  33.0 0.0 collective-permute-done.6
  33.0 0.1 fusion.10.sum_ref
  33.1 0.3 gram.1
  33.5 10.0 %all_to_all.16 = f32[16,1,128]{2,1,0:T(1,128)S(1)} all-to-all(f32[16,1,128]{2,1,0:T(1,128)S(1)} %bitcast.20), channel_id=1, replica_groups=mesh['grp'=2,'smp'=16] {'smp'}, dimensions={0} | all-to-all | bytes 16384 | tf_op jit(solution)/shard_map/all_to_all | solution.py:309
  43.5 0.9 %finish.1 = f32[4,16]{1,0:T(4,128)} custom-call(f32[16,128]{1,0:T(8,128)S(1)} %bitcast.21, f32[8,128]{1,0:T(8,128)S(1)} %get-tuple-element.12.inv_ref), custom_call_target="tpu_custom_call" | custom-call | tf_op jit(solution)/shard_map/finish/pallas_call | solution.py:248
  (1 shorter events, 0.0 us)
Async XLA Ops:
  1.6 14.3 %all-to-all-start = ((bf16[16,16,128]{2,1,0:T(8,128)(2,1)}), bf16[16,16,128]{2,1,0:T(8,128)(2,1)S(1)}, u32[]{:S(2)}, u32[]{:S(2)}) async-start(bf16[16,16,128]{2,1,0:T(8,128)(2,1)} %get-tuple-element.9), calls=%async_computation | async-start | bytes 131072 | tf_op jit(solution)/shard_map/all_to_all | solution.py:296
  16.8 2.3 %collective-permute-start = (f16[8,80,512]{2,1,0:T(8,128)(2,1)S(1)}, f16[8,80,512]{2,1,0:T(8,128)(2,1)S(1)}, u32[]{:S(2)}, u32[]{:S(2)}) collective-permute-start(f16[8,80,512]{2,1,0:T(8,128)(2,1)S(1)} %convert_element_type.89), channel_id=1, source_target_pairs={{0,1},{1,0},{2,3},{3,2},{4,5},{5,4},{6,7},{7,6},{8,9},{9,8},{10,11... | collective-permute-start | bytes 1966088 | tf_op jit(solution)/shard_map/ppermute | solution.py:301
  19.4 7.1 %collective-permute-start.4 = (f16[2,80,512]{2,1,0:T(8,128)(2,1)S(1)}, f16[2,80,512]{2,1,0:T(8,128)(2,1)S(1)}, u32[]{:S(2)}, u32[]{:S(2)}) collective-permute-start(f16[2,80,512]{2,1,0:T(8,128)(2,1)S(1)} %pad_maximum_fusion), channel_id=1, source_target_pairs={{0,2},{1,3},{2,0},{3,1},{4,6},{5,7},{6,4},{7,5},{8,10},{9,11},{10,... | collective-permute-start | bytes 491528 | tf_op jit(solution)/shard_map/ppermute | solution.py:258
  19.7 8.0 %collective-permute-start.1 = (f16[80,512]{1,0:T(8,128)(2,1)S(1)}, f16[80,512]{1,0:T(8,128)(2,1)S(1)}, u32[]{:S(2)}, u32[]{:S(2)}) collective-permute-start(f16[80,512]{1,0:T(8,128)(2,1)S(1)} %get-tuple-element.15), channel_id=1, source_target_pairs={{0,12},{1,13},{2,14},{3,15},{4,8},{5,9},{6,10},{7,11},{8,4},{9,5},... | collective-permute-start | bytes 245768 | tf_op jit(solution)/shard_map/ppermute | solution.py:258
  20.8 8.8 %collective-permute-start.3 = (f16[80,512]{1,0:T(8,128)(2,1)S(1)}, f16[80,512]{1,0:T(8,128)(2,1)S(1)}, u32[]{:S(2)}, u32[]{:S(2)}) collective-permute-start(f16[80,512]{1,0:T(8,128)(2,1)S(1)} %get-tuple-element.18), channel_id=1, source_target_pairs={{0,2},{1,3},{2,0},{3,1},{4,6},{5,7},{6,4},{7,5},{8,10},{9,11},{10,... | collective-permute-start | bytes 245768 | tf_op jit(solution)/shard_map/ppermute | solution.py:258
  22.1 7.4 %collective-permute-start.2 = (f16[80,512]{1,0:T(8,128)(2,1)S(1)}, f16[80,512]{1,0:T(8,128)(2,1)S(1)}, u32[]{:S(2)}, u32[]{:S(2)}) collective-permute-start(f16[80,512]{1,0:T(8,128)(2,1)S(1)} %get-tuple-element.19), channel_id=1, source_target_pairs={{0,14},{1,15},{2,12},{3,13},{4,10},{5,11},{6,8},{7,9},{8,6},{9,7},... | collective-permute-start | bytes 245768 | tf_op jit(solution)/shard_map/ppermute | solution.py:258
  26.5 6.5 %collective-permute-start.5 = (f16[80,512]{1,0:T(8,128)(2,1)S(1)}, f16[80,512]{1,0:T(8,128)(2,1)S(1)}, u32[]{:S(2)}, u32[]{:S(2)}) collective-permute-start(f16[80,512]{1,0:T(8,128)(2,1)S(1)} %get-tuple-element.13), channel_id=1, source_target_pairs={{0,8},{1,9},{2,10},{3,11},{4,12},{5,13},{6,14},{7,15},{8,0},{9,1},... | collective-permute-start | bytes 245768 | tf_op jit(solution)/shard_map/ppermute | solution.py:258
  26.9 6.1 %collective-permute-start.6 = (f16[80,512]{1,0:T(8,128)(2,1)S(1)}, f16[80,512]{1,0:T(8,128)(2,1)S(1)}, u32[]{:S(2)}, u32[]{:S(2)}) collective-permute-start(f16[80,512]{1,0:T(8,128)(2,1)S(1)} %get-tuple-element.14), channel_id=1, source_target_pairs={{0,4},{1,5},{2,6},{3,7},{4,0},{5,1},{6,2},{7,3},{8,12},{9,13},{10,... | collective-permute-start | bytes 245768 | tf_op jit(solution)/shard_map/ppermute | solution.py:258

commit v6 on v5

--- a/solution.py
+++ b/solution.py
@@ -15,7 +15,7 @@
 PAD = 8
 TOP = 32.0
 STEP = 512
-PIECE = 1024
+GROUP = 2
 KEEP = 13 << 18
 
 
@@ -129,25 +129,27 @@
         store_blocks(out_ref, start, part, devices)
 
 
-def own_kernel(devices, rows_ref, proj_ref, out_ref, held, sems):
-    pieces, _, length = held.shape
+def own_kernel(devices, ks, rows_ref, proj_ref, out_ref, held, sems):
     core = lax.axis_index("smp") % 2
     copies = []
-    for piece in range(pieces):
-        offset = pl.multiple_of(core * (pieces * length) + piece * length, length)
+    for place, k in enumerate(ks):
+        block = jnp.bitwise_xor(lax.axis_index("smp") // 2, k) if is_direct(devices) else k
+        offset = pl.multiple_of((core * (K // 2 // STEP) + block) * STEP, STEP)
         copy = pltpu.make_async_copy(
-            proj_ref.at[:, pl.ds(offset, length)], held.at[piece], sems.at[piece]
+            proj_ref.at[:, pl.ds(offset, STEP)], held.at[place], sems.at[place]
         )
         copy.start()
         copies.append(copy)
     rows = rows_ref[...]
-    for piece in range(pieces):
-        copies[piece].wait()
-        for start in range(0, length, STEP):
-            part = jnp.dot(
-                rows, held[piece, :, start : start + STEP], preferred_element_type=jnp.float32
-            )
-            store_blocks(out_ref, piece * length + start, part, devices)
+    width = out_ref.shape[2]
+    for start in range(0, len(ks), GROUP):
+        places = range(start, min(start + GROUP, len(ks)))
+        for place in places:
+            copies[place].wait()
+        for place in places:
+            part = jnp.dot(rows, held[place], preferred_element_type=jnp.float32)
+            for at in range(0, STEP, width):
+                out_ref[(place * STEP + at) // width] = part[:, at : at + width]
 
 
 def sketch_other(gathered, loaded, count, devices, blocks):
@@ -167,23 +169,25 @@
     )(gathered, pltpu.with_memory_space_constraint(loaded, pltpu.VMEM))
 
 
-def sketch_own(rows, projection, devices, blocks):
-    params, columns = projection.shape
-    span = columns // 2
-    return pl.pallas_call(
-        functools.partial(own_kernel, devices),
+def sketch_own(rows, projection, devices, ks, width):
+    params = projection.shape[0]
+    shape = (len(ks) * STEP // width, rows.shape[0], width)
+    return pl.pallas_call(
+        functools.partial(own_kernel, devices, ks),
         in_specs=[
             pl.BlockSpec(memory_space=pltpu.VMEM),
             pl.BlockSpec(memory_space=pl.ANY),
         ],
         out_specs=pl.BlockSpec(memory_space=pltpu.VMEM),
-        out_shape=in_vmem((blocks, rows.shape[0], span // blocks), jnp.float32),
+        out_shape=in_vmem(shape, jnp.float32),
         scratch_shapes=[
-            pltpu.VMEM((span // PIECE, params, PIECE), projection.dtype),
-            pltpu.SemaphoreType.DMA((span // PIECE,)),
+            pltpu.VMEM((len(ks), params, STEP), projection.dtype),
+            pltpu.SemaphoreType.DMA((len(ks),)),
         ],
         cost_estimate=pl.CostEstimate(
-            flops=2 * rows.size * span, bytes_accessed=params * span * 2, transcendentals=0
+            flops=2 * params * math.prod(shape),
+            bytes_accessed=params * STEP * 2 * len(ks),
+            transcendentals=0,
         ),
         compiler_params=pltpu.CompilerParams(vmem_limit_bytes=40 << 20),
         name="sketch_own",
@@ -253,31 +257,39 @@
     )(parts, inv)
 
 
-def sum_direct(mine, arrived, devices):
+def sum_direct(rows, projection, arrived, devices):
     def swap(part, k):
         return lax.ppermute(part, "smp", [(i, i ^ (2 * k)) for i in range(devices)])
 
-    def chip_sum(place):
-        return mine[place] + arrived[place]
-
     def narrow(part):
         return part.astype(jnp.float16)
 
     def wide(part):
         return part.astype(jnp.float32)
 
-    passed = swap(narrow(jnp.stack([chip_sum(0), chip_sum(3)])), 1)
+    def from_other(k):
+        return arrived[(5, 7, 1, 3, 4, 6, 0, 2).index(k)]
+
+    first, last = (5, 3, 6, 7), (4, 2, 1, 0)
+    own = sketch_own(rows, projection, devices, first, STEP)
+    sums = {k: own[place] + from_other(k) for place, k in enumerate(first)}
+    sends = narrow(jnp.stack([sums[5], sums[3]])), narrow(sums[6]), narrow(sums[7])
+    *sends, rows = lax.optimization_barrier((*sends, rows))
+    passed = swap(sends[0], 1)
+    own = sketch_own(rows, projection, devices, last, STEP)
+    sums.update({k: own[place] + from_other(k) for place, k in enumerate(last)})
     parts = [
-        swap(narrow(chip_sum(5)), 6),
-        swap(narrow(chip_sum(1)), 7),
-        swap(narrow(chip_sum(2)), 1),
-        swap(narrow(chip_sum(4) + wide(passed[0])), 4),
-        swap(narrow(chip_sum(7) + wide(passed[1])), 2),
+        swap(sends[1], 6),
+        swap(sends[2], 7),
+        swap(narrow(sums[1]), 1),
+        swap(narrow(sums[4] + wide(passed[0])), 4),
+        swap(narrow(sums[2] + wide(passed[1])), 2),
     ]
-    return chip_sum(6) + sum(wide(part) for part in parts)
-
-
-def sum_together(mine, arrived, devices):
+    return sums[0] + sum(wide(part) for part in parts)
+
+
+def sum_together(rows, projection, arrived, devices):
+    mine = sketch_own(rows, projection, devices, tuple(range(K // 2 // STEP)), arrived.shape[2])
     parts = (mine + arrived).astype(jnp.float16)
     same_core = [[i for i in range(devices) if i % 2 == c] for c in range(2)]
     parts = lax.all_to_all(
@@ -299,11 +311,10 @@
     theirs, rows = sketch_other(gathered, loaded, count, devices, blocks)
     theirs = theirs.astype(jnp.float16)
     arrived = lax.ppermute(theirs, "smp", [(i, i ^ 1) for i in range(devices)])
-    mine = sketch_own(rows, projection, devices, blocks)
     if is_direct(devices):
-        summed = sum_direct(mine, arrived, devices)
+        summed = sum_direct(rows, projection, arrived, devices)
     else:
-        summed = sum_together(mine, arrived, devices)
+        summed = sum_together(rows, projection, arrived, devices)
 
     message = gram(summed, inv, pc, devices)
     parts = lax.all_to_all(message, "smp", split_axis=0, concat_axis=0, tiled=True)

time: 44.6 us -> 44.5 us (level)
  waiting for transfers between devices: 11.8 us -> 9.83 us
  Pallas kernels: 7.81 us -> 8.94 us
    ppermute x6, waiting for transfers between devices: 6.79 us -> 4.48 us  [swap(): return lax.ppermute(part, 'smp', [(i, i ^ 2 * k) for i in range(devices)])]
    pallas_call x1 -> x2, Pallas kernels: 2.26 us -> 3.39 us  [sketch_own(): pl.pallas_call(functools.partial(own_kernel, devices, ks), in_specs=[pl.B...]
  transfers between devices with their start and end apart: 8 -> 8, of which waited for: 4 -> 4; matrix products, arithmetic and copies ran while one was open for 0% -> 0% of each run, Pallas kernels for 9% -> 12%
where the time goes in v6:
time: 44.5 us; the launch traced here: 44.1 us
  starting transfers between devices  14.6 us (33%)
  blocking collectives  10.2 us (23%)
  waiting for transfers between devices  9.83 us (22%)
  Pallas kernels  8.94 us (20%)
  other arithmetic  0.49 us (1%)
    all_to_all x1, blocking collectives, shards(): lax.all_to_all(message, 'smp', split_axis=0, concat_axis=0, tiled=True)  10.2 us
    all_to_all x1, starting transfers between devices, shards(): lax.all_to_all(rows, 'smp', split_axis=0, concat_axis=0, tiled=True)  7.36 us
    ppermute x6, starting transfers between devices, swap(): return lax.ppermute(part, 'smp', [(i, i ^ 2 * k) for i in range(devices)])  7.18 us
    all_to_all x1, waiting for transfers between devices, shards(): lax.all_to_all(rows, 'smp', split_axis=0, concat_axis=0, tiled=True)  4.98 us
    ppermute x6, waiting for transfers between devices, swap(): return lax.ppermute(part, 'smp', [(i, i ^ 2 * k) for i in range(devices)])  4.48 us
    pallas_call x2, Pallas kernels, sketch_own(): pl.pallas_call(functools.partial(own_kernel, devices, ks), in_specs=[pl.B...  3.39 us
    pallas_call x1, Pallas kernels, load(): pl.pallas_call(load_kernel, in_specs=[pl.BlockSpec(memory_space=pl.ANY)],...  1.91 us
    pallas_call x1, Pallas kernels, prepare(): pl.pallas_call(prep_kernel, out_shape=(in_vmem(shape, jnp.bfloat16), in_v...  1.59 us
  transfers between devices with their start and end apart: 8, of which 4 were waited for; matrix products, arithmetic and copies ran while one was open for 0% of the time, Pallas kernels for 12%

profile of v6, /device:TPU:0, one launch (start us, length us, event | category | flops | bytes accessed | tf_op | source)
XLA Modules:
  0.0 44.1 jit_solution(14262599295030293495)
XLA Ops:
  0.0 1.6 %prepare.1 = (bf16[16,16,128]{2,1,0:T(8,128)(2,1)}, f32[8,128]{1,0:T(8,128)S(1)}) custom-call(bf16[4,6144]{1,0:T(4,128)(2,1)} %cand_ref.1, bf16[1,6144]{1,0:T(2,128)(2,1)} %tgt_ref.1), custom_call_target="tpu_custom_call" | custom-call | tf_op jit(solution)/shard_map/prepare/pallas_call | solution.py:56
  1.6 7.4 %all-to-all-start = ((bf16[16,16,128]{2,1,0:T(8,128)(2,1)}), bf16[16,16,128]{2,1,0:T(8,128)(2,1)S(1)}, u32[]{:S(2)}, u32[]{:S(2)}) async-start(bf16[16,16,128]{2,1,0:T(8,128)(2,1)} %get-tuple-element.13), calls=%async_computation | async-start | bytes 131072 | tf_op jit(solution)/shard_map/all_to_all | solution.py:308
  9.0 1.9 %load.1.proj_ref = bf16[384,4096]{1,0:T(8,128)(2,1)S(1)} custom-call(bf16[384,8192]{1,0:T(8,128)(2,1)} %proj_ref.5), custom_call_target="tpu_custom_call" | custom-call | bytes 6291456 | tf_op jit(solution)/shard_map/load/pallas_call | solution.py:93
  10.9 5.0 %all-to-all-done = bf16[16,16,128]{2,1,0:T(8,128)(2,1)S(1)} async-done(((bf16[16,16,128]{2,1,0:T(8,128)(2,1)}), bf16[16,16,128]{2,1,0:T(8,128)(2,1)S(1)}, u32[]{:S(2)}, u32[]{:S(2)}) %all-to-all-start) | async-done | bytes 65568 | tf_op jit(solution)/shard_map/all_to_all | solution.py:308
  15.8 0.8 %sketch_other.1 = (f32[8,80,512]{2,1,0:T(8,128)S(1)}, bf16[80,384]{1,0:T(8,128)(2,1)S(1)}) custom-call(bf16[256,128]{1,0:T(8,128)(2,1)S(1)} %bitcast.19, bf16[384,4096]{1,0:T(8,128)(2,1)S(1)} %load.1.proj_ref), custom_call_target="tpu_custom_call" | custom-call | flops 251658240 | bytes 1572864 | tf_op jit(solution)/shard_map/sketch_other/pallas_call | solution.py:158
  16.7 0.1 convert_element_type.89
  16.8 0.1 collective-permute-start
  16.9 1.7 %sketch_own.2 = f32[4,80,512]{2,1,0:T(8,128)S(1)} custom-call(bf16[80,384]{1,0:T(8,128)(2,1)S(1)} %get-tuple-element.16.rows_ref, bf16[384,8192]{1,0:T(8,128)(2,1)} %proj_ref.5), custom_call_target="tpu_custom_call" | custom-call | flops 125829120 | bytes 1572864 | tf_op jit(solution)/shard_map/sketch_own/pallas_call | solution.py:175
  18.6 0.4 collective-permute-done
  19.0 0.1 fusion.12
  19.2 0.2 collective-permute-start.4
  19.4 1.1 %collective-permute-start.1 = (f16[80,512]{1,0:T(8,128)(2,1)S(1)}, f16[80,512]{1,0:T(8,128)(2,1)S(1)}, u32[]{:S(2)}, u32[]{:S(2)}) collective-permute-start(f16[80,512]{1,0:T(8,128)(2,1)S(1)} %get-tuple-element.17), channel_id=1, source_target_pairs={{0,12},{1,13},{2,14},{3,15},{4,8},{5,9},{6,10},{7,11},{8,4},{9,5},... | collective-permute-start | bytes 245768 | tf_op jit(solution)/shard_map/ppermute | solution.py:262
  20.4 4.1 %collective-permute-start.2 = (f16[80,512]{1,0:T(8,128)(2,1)S(1)}, f16[80,512]{1,0:T(8,128)(2,1)S(1)}, u32[]{:S(2)}, u32[]{:S(2)}) collective-permute-start(f16[80,512]{1,0:T(8,128)(2,1)S(1)} %get-tuple-element.18), channel_id=1, source_target_pairs={{0,14},{1,15},{2,12},{3,13},{4,10},{5,11},{6,8},{7,9},{8,6},{9,7},... | collective-permute-start | bytes 245768 | tf_op jit(solution)/shard_map/ppermute | solution.py:262
  24.5 1.7 %sketch_own.3 = f32[4,80,512]{2,1,0:T(8,128)S(1)} custom-call(bf16[80,384]{1,0:T(8,128)(2,1)S(1)} %get-tuple-element.16.rows_ref, bf16[384,8192]{1,0:T(8,128)(2,1)} %proj_ref.5), custom_call_target="tpu_custom_call" | custom-call | flops 125829120 | bytes 1572864 | tf_op jit(solution)/shard_map/sketch_own/pallas_call | solution.py:175
  26.2 0.0 collective-permute-done.4
  26.2 0.1 fusion.14
  26.3 0.1 collective-permute-start.5
  26.4 1.1 %collective-permute-start.6 = (f16[80,512]{1,0:T(8,128)(2,1)S(1)}, f16[80,512]{1,0:T(8,128)(2,1)S(1)}, u32[]{:S(2)}, u32[]{:S(2)}) collective-permute-start(f16[80,512]{1,0:T(8,128)(2,1)S(1)} %get-tuple-element.22), channel_id=1, source_target_pairs={{0,4},{1,5},{2,6},{3,7},{4,0},{5,1},{6,2},{7,3},{8,12},{9,13},{10,... | collective-permute-start | bytes 245768 | tf_op jit(solution)/shard_map/ppermute | solution.py:262
  27.5 0.7 %collective-permute-start.3 = (f16[80,512]{1,0:T(8,128)(2,1)S(1)}, f16[80,512]{1,0:T(8,128)(2,1)S(1)}, u32[]{:S(2)}, u32[]{:S(2)}) collective-permute-start(f16[80,512]{1,0:T(8,128)(2,1)S(1)} %get-tuple-element.23), channel_id=1, source_target_pairs={{0,2},{1,3},{2,0},{3,1},{4,6},{5,7},{6,4},{7,5},{8,10},{9,11},{10,... | collective-permute-start | bytes 245768 | tf_op jit(solution)/shard_map/ppermute | solution.py:262
  28.2 0.0 collective-permute-done.1
  28.2 0.4 collective-permute-done.2
  28.6 4.1 %collective-permute-done.5 = f16[80,512]{1,0:T(8,128)(2,1)S(1)} collective-permute-done((f16[80,512]{1,0:T(8,128)(2,1)S(1)}, f16[80,512]{1,0:T(8,128)(2,1)S(1)}, u32[]{:S(2)}, u32[]{:S(2)}) %collective-permute-start.5) | collective-permute-done | bytes 81952 | tf_op jit(solution)/shard_map/ppermute | solution.py:262
  32.7 0.0 collective-permute-done.6
  32.7 0.0 collective-permute-done.3
  32.7 0.1 fusion.6.sum_ref
  32.8 0.3 gram.1
  33.1 10.2 %all_to_all.16 = f32[16,1,128]{2,1,0:T(1,128)S(1)} all-to-all(f32[16,1,128]{2,1,0:T(1,128)S(1)} %bitcast.20), channel_id=1, replica_groups=mesh['grp'=2,'smp'=16] {'smp'}, dimensions={0} | all-to-all | bytes 16384 | tf_op jit(solution)/shard_map/all_to_all | solution.py:320
  43.3 0.9 %finish.1 = f32[4,16]{1,0:T(4,128)} custom-call(f32[16,128]{1,0:T(8,128)S(1)} %bitcast.21, f32[8,128]{1,0:T(8,128)S(1)} %get-tuple-element.20.inv_ref), custom_call_target="tpu_custom_call" | custom-call | tf_op jit(solution)/shard_map/finish/pallas_call | solution.py:252
  (1 shorter events, 0.0 us)
Async XLA Ops:
  1.6 14.3 %all-to-all-start = ((bf16[16,16,128]{2,1,0:T(8,128)(2,1)}), bf16[16,16,128]{2,1,0:T(8,128)(2,1)S(1)}, u32[]{:S(2)}, u32[]{:S(2)}) async-start(bf16[16,16,128]{2,1,0:T(8,128)(2,1)} %get-tuple-element.13), calls=%async_computation | async-start | bytes 131072 | tf_op jit(solution)/shard_map/all_to_all | solution.py:308
  16.8 2.2 %collective-permute-start = (f16[8,80,512]{2,1,0:T(8,128)(2,1)S(1)}, f16[8,80,512]{2,1,0:T(8,128)(2,1)S(1)}, u32[]{:S(2)}, u32[]{:S(2)}) collective-permute-start(f16[8,80,512]{2,1,0:T(8,128)(2,1)S(1)} %convert_element_type.89), channel_id=1, source_target_pairs={{0,1},{1,0},{2,3},{3,2},{4,5},{5,4},{6,7},{7,6},{8,9},{9,8},{10,11... | collective-permute-start | bytes 1966088 | tf_op jit(solution)/shard_map/ppermute | solution.py:313
  19.2 7.0 %collective-permute-start.4 = (f16[2,80,512]{2,1,0:T(8,128)(2,1)S(1)}, f16[2,80,512]{2,1,0:T(8,128)(2,1)S(1)}, u32[]{:S(2)}, u32[]{:S(2)}) collective-permute-start(f16[2,80,512]{2,1,0:T(8,128)(2,1)S(1)} %pad_maximum_fusion), channel_id=1, source_target_pairs={{0,2},{1,3},{2,0},{3,1},{4,6},{5,7},{6,4},{7,5},{8,10},{9,11},{10,... | collective-permute-start | bytes 491528 | tf_op jit(solution)/shard_map/ppermute | solution.py:262
  19.4 8.8 %collective-permute-start.1 = (f16[80,512]{1,0:T(8,128)(2,1)S(1)}, f16[80,512]{1,0:T(8,128)(2,1)S(1)}, u32[]{:S(2)}, u32[]{:S(2)}) collective-permute-start(f16[80,512]{1,0:T(8,128)(2,1)S(1)} %get-tuple-element.17), channel_id=1, source_target_pairs={{0,12},{1,13},{2,14},{3,15},{4,8},{5,9},{6,10},{7,11},{8,4},{9,5},... | collective-permute-start | bytes 245768 | tf_op jit(solution)/shard_map/ppermute | solution.py:262
  20.4 8.2 %collective-permute-start.2 = (f16[80,512]{1,0:T(8,128)(2,1)S(1)}, f16[80,512]{1,0:T(8,128)(2,1)S(1)}, u32[]{:S(2)}, u32[]{:S(2)}) collective-permute-start(f16[80,512]{1,0:T(8,128)(2,1)S(1)} %get-tuple-element.18), channel_id=1, source_target_pairs={{0,14},{1,15},{2,12},{3,13},{4,10},{5,11},{6,8},{7,9},{8,6},{9,7},... | collective-permute-start | bytes 245768 | tf_op jit(solution)/shard_map/ppermute | solution.py:262
  26.3 6.3 %collective-permute-start.5 = (f16[80,512]{1,0:T(8,128)(2,1)S(1)}, f16[80,512]{1,0:T(8,128)(2,1)S(1)}, u32[]{:S(2)}, u32[]{:S(2)}) collective-permute-start(f16[80,512]{1,0:T(8,128)(2,1)S(1)} %get-tuple-element.21), channel_id=1, source_target_pairs={{0,8},{1,9},{2,10},{3,11},{4,12},{5,13},{6,14},{7,15},{8,0},{9,1},... | collective-permute-start | bytes 245768 | tf_op jit(solution)/shard_map/ppermute | solution.py:262
  26.4 6.2 %collective-permute-start.6 = (f16[80,512]{1,0:T(8,128)(2,1)S(1)}, f16[80,512]{1,0:T(8,128)(2,1)S(1)}, u32[]{:S(2)}, u32[]{:S(2)}) collective-permute-start(f16[80,512]{1,0:T(8,128)(2,1)S(1)} %get-tuple-element.22), channel_id=1, source_target_pairs={{0,4},{1,5},{2,6},{3,7},{4,0},{5,1},{6,2},{7,3},{8,12},{9,13},{10,... | collective-permute-start | bytes 245768 | tf_op jit(solution)/shard_map/ppermute | solution.py:262
  27.5 5.1 %collective-permute-start.3 = (f16[80,512]{1,0:T(8,128)(2,1)S(1)}, f16[80,512]{1,0:T(8,128)(2,1)S(1)}, u32[]{:S(2)}, u32[]{:S(2)}) collective-permute-start(f16[80,512]{1,0:T(8,128)(2,1)S(1)} %get-tuple-element.23), channel_id=1, source_target_pairs={{0,2},{1,3},{2,0},{3,1},{4,6},{5,7},{6,4},{7,5},{8,10},{9,11},{10,... | collective-permute-start | bytes 245768 | tf_op jit(solution)/shard_map/ppermute | solution.py:262

commit v7 on v6

--- a/solution.py
+++ b/solution.py
@@ -73,11 +73,14 @@
     return devices == 16
 
 
-def place_of(block, devices):
+ROLES = ((5, 7), (7, 3), (1, 6), (3, 4), (4, 5), (6, 1), (2, 2), (0, 0))
+
+
+def block_of(place, core, devices):
     if not is_direct(devices):
-        return block
-    k = jnp.bitwise_xor(block, lax.axis_index("smp") // 2)
-    return (1 - k % 2) * 4 + jnp.bitwise_xor(k // 2, 2)
+        return place
+    even, odd = ROLES[place]
+    return jnp.bitwise_xor(lax.axis_index("smp") // 2, jnp.where(core == 0, even, odd))
 
 
 def load_kernel(proj_ref, out_ref, sem):
@@ -102,12 +105,6 @@
         compiler_params=pltpu.CompilerParams(vmem_limit_bytes=60 << 20),
         name="load",
     )(pltpu.with_memory_space_constraint(projection, pltpu.HBM))
-
-
-def store_blocks(out_ref, start, part, devices):
-    width = out_ref.shape[2]
-    for at in range(0, part.shape[1], width):
-        out_ref[place_of((start + at) // width, devices)] = part[:, at : at + width]
 
 
 def other_kernel(devices, gathered_ref, proj_ref, out_ref, rows_ref):
@@ -122,34 +119,36 @@
             pick, gathered_ref[...], preferred_element_type=jnp.float32
         ).astype(rows_ref.dtype)
     rows = rows_ref[...]
-    for start in range(0, proj_ref.shape[1], STEP):
-        part = jnp.dot(
-            rows, proj_ref[:, start : start + STEP], preferred_element_type=jnp.float32
-        )
-        store_blocks(out_ref, start, part, devices)
-
-
-def own_kernel(devices, ks, rows_ref, proj_ref, out_ref, held, sems):
+    core = 1 - lax.axis_index("smp") % 2
+    width = out_ref.shape[2]
+    for place in range(proj_ref.shape[1] // STEP):
+        start = pl.multiple_of(block_of(place, core, devices) * STEP, STEP)
+        part = jnp.dot(rows, proj_ref[:, pl.ds(start, STEP)], preferred_element_type=jnp.float32)
+        for at in range(0, STEP, width):
+            out_ref[(place * STEP + at) // width] = part[:, at : at + width]
+
+
+def own_kernel(devices, places, rows_ref, proj_ref, out_ref, held, sems):
     core = lax.axis_index("smp") % 2
     copies = []
-    for place, k in enumerate(ks):
-        block = jnp.bitwise_xor(lax.axis_index("smp") // 2, k) if is_direct(devices) else k
-        offset = pl.multiple_of((core * (K // 2 // STEP) + block) * STEP, STEP)
+    for at, place in enumerate(places):
+        block = core * (K // 2 // STEP) + block_of(place, core, devices)
+        offset = pl.multiple_of(block * STEP, STEP)
         copy = pltpu.make_async_copy(
-            proj_ref.at[:, pl.ds(offset, STEP)], held.at[place], sems.at[place]
+            proj_ref.at[:, pl.ds(offset, STEP)], held.at[at], sems.at[at]
         )
         copy.start()
         copies.append(copy)
     rows = rows_ref[...]
     width = out_ref.shape[2]
-    for start in range(0, len(ks), GROUP):
-        places = range(start, min(start + GROUP, len(ks)))
-        for place in places:
-            copies[place].wait()
-        for place in places:
-            part = jnp.dot(rows, held[place], preferred_element_type=jnp.float32)
-            for at in range(0, STEP, width):
-                out_ref[(place * STEP + at) // width] = part[:, at : at + width]
+    for start in range(0, len(places), GROUP):
+        some = range(start, min(start + GROUP, len(places)))
+        for at in some:
+            copies[at].wait()
+        for at in some:
+            part = jnp.dot(rows, held[at], preferred_element_type=jnp.float32)
+            for column in range(0, STEP, width):
+                out_ref[(at * STEP + column) // width] = part[:, column : column + width]
 
 
 def sketch_other(gathered, loaded, count, devices, blocks):
@@ -169,11 +168,11 @@
     )(gathered, pltpu.with_memory_space_constraint(loaded, pltpu.VMEM))
 
 
-def sketch_own(rows, projection, devices, ks, width):
+def sketch_own(rows, projection, devices, places, width):
     params = projection.shape[0]
-    shape = (len(ks) * STEP // width, rows.shape[0], width)
-    return pl.pallas_call(
-        functools.partial(own_kernel, devices, ks),
+    shape = (len(places) * STEP // width, rows.shape[0], width)
+    return pl.pallas_call(
+        functools.partial(own_kernel, devices, places),
         in_specs=[
             pl.BlockSpec(memory_space=pltpu.VMEM),
             pl.BlockSpec(memory_space=pl.ANY),
@@ -181,12 +180,12 @@
         out_specs=pl.BlockSpec(memory_space=pltpu.VMEM),
         out_shape=in_vmem(shape, jnp.float32),
         scratch_shapes=[
-            pltpu.VMEM((len(ks), params, STEP), projection.dtype),
-            pltpu.SemaphoreType.DMA((len(ks),)),
+            pltpu.VMEM((len(places), params, STEP), projection.dtype),
+            pltpu.SemaphoreType.DMA((len(places),)),
         ],
         cost_estimate=pl.CostEstimate(
             flops=2 * params * math.prod(shape),
-            bytes_accessed=params * STEP * 2 * len(ks),
+            bytes_accessed=params * STEP * 2 * len(places),
             transcendentals=0,
         ),
         compiler_params=pltpu.CompilerParams(vmem_limit_bytes=40 << 20),
@@ -257,39 +256,43 @@
     )(parts, inv)
 
 
+def narrow(part):
+    return part.astype(jnp.float16)
+
+
+def wide(part):
+    return part.astype(jnp.float32)
+
+
+def swap(part, even, odd, devices):
+    pairs = [(i, i ^ (2 * (odd if i % 2 else even))) for i in range(devices)]
+    return lax.ppermute(part, "smp", pairs)
+
+
 def sum_direct(rows, projection, arrived, devices):
-    def swap(part, k):
-        return lax.ppermute(part, "smp", [(i, i ^ (2 * k)) for i in range(devices)])
-
-    def narrow(part):
-        return part.astype(jnp.float16)
-
-    def wide(part):
-        return part.astype(jnp.float32)
-
-    def from_other(k):
-        return arrived[(5, 7, 1, 3, 4, 6, 0, 2).index(k)]
-
-    first, last = (5, 3, 6, 7), (4, 2, 1, 0)
+    def trade(part, place):
+        return swap(part, *ROLES[place], devices)
+
+    first, last = range(7), range(7, 8)
     own = sketch_own(rows, projection, devices, first, STEP)
-    sums = {k: own[place] + from_other(k) for place, k in enumerate(first)}
-    sends = narrow(jnp.stack([sums[5], sums[3]])), narrow(sums[6]), narrow(sums[7])
+    sums = [own[at] + wide(arrived[at]) for at in first]
+    sends = narrow(jnp.stack(sums[:2])), narrow(sums[2]), narrow(sums[3])
     *sends, rows = lax.optimization_barrier((*sends, rows))
-    passed = swap(sends[0], 1)
+    passed = swap(sends[0], 1, 2, devices)
     own = sketch_own(rows, projection, devices, last, STEP)
-    sums.update({k: own[place] + from_other(k) for place, k in enumerate(last)})
+    sums += [own[at - 7] + wide(arrived[at]) for at in last]
     parts = [
-        swap(sends[1], 6),
-        swap(sends[2], 7),
-        swap(narrow(sums[1]), 1),
-        swap(narrow(sums[4] + wide(passed[0])), 4),
-        swap(narrow(sums[2] + wide(passed[1])), 2),
+        trade(sends[1], 2),
+        trade(sends[2], 3),
+        trade(narrow(sums[4] + wide(passed[0])), 4),
+        trade(narrow(sums[5] + wide(passed[1])), 5),
+        trade(narrow(sums[6]), 6),
     ]
-    return sums[0] + sum(wide(part) for part in parts)
+    return sums[7] + sum(wide(part) for part in parts)
 
 
 def sum_together(rows, projection, arrived, devices):
-    mine = sketch_own(rows, projection, devices, tuple(range(K // 2 // STEP)), arrived.shape[2])
+    mine = sketch_own(rows, projection, devices, range(K // 2 // STEP), arrived.shape[2])
     parts = (mine + arrived).astype(jnp.float16)
     same_core = [[i for i in range(devices) if i % 2 == c] for c in range(2)]
     parts = lax.all_to_all(

time: 44.5 us -> 44 us (0.989)
  waiting for transfers between devices: 9.83 us -> 11.2 us
  starting transfers between devices: 14.6 us -> 13.4 us
  blocking collectives: 10.2 us -> 9.48 us
    ppermute x6, waiting for transfers between devices: 4.48 us -> 6.21 us  [swap(): return lax.ppermute(part, 'smp', pairs)]
    ppermute x6, starting transfers between devices: 7.18 us -> 5.95 us  [swap(): return lax.ppermute(part, 'smp', pairs)]
    all_to_all x1, blocking collectives: 10.2 us -> 9.48 us  [shards(): lax.all_to_all(message, 'smp', split_axis=0, concat_axis=0, tiled=True)]
  transfers between devices with their start and end apart: 8 -> 8, of which waited for: 4 -> 5; matrix products, arithmetic and copies ran while one was open for 0% -> 0% of each run, Pallas kernels for 12% -> 12%
where the time goes in v7:
time: 44 us; the launch traced here: 43.6 us
  starting transfers between devices  13.4 us (30%)
  waiting for transfers between devices  11.2 us (25%)
  blocking collectives  9.48 us (22%)
  Pallas kernels  8.97 us (20%)
  other arithmetic  0.49 us (1%)
    all_to_all x1, blocking collectives, shards(): lax.all_to_all(message, 'smp', split_axis=0, concat_axis=0, tiled=True)  9.48 us
    all_to_all x1, starting transfers between devices, shards(): lax.all_to_all(rows, 'smp', split_axis=0, concat_axis=0, tiled=True)  7.36 us
    ppermute x6, waiting for transfers between devices, swap(): return lax.ppermute(part, 'smp', pairs)  6.21 us
    ppermute x6, starting transfers between devices, swap(): return lax.ppermute(part, 'smp', pairs)  5.95 us
    all_to_all x1, waiting for transfers between devices, shards(): lax.all_to_all(rows, 'smp', split_axis=0, concat_axis=0, tiled=True)  4.98 us
    pallas_call x2, Pallas kernels, sketch_own(): pl.pallas_call(functools.partial(own_kernel, devices, places), in_specs=[...  3.42 us
    pallas_call x1, Pallas kernels, load(): pl.pallas_call(load_kernel, in_specs=[pl.BlockSpec(memory_space=pl.ANY)],...  1.91 us
    pallas_call x1, Pallas kernels, prepare(): pl.pallas_call(prep_kernel, out_shape=(in_vmem(shape, jnp.bfloat16), in_v...  1.59 us
  transfers between devices with their start and end apart: 8, of which 5 were waited for; matrix products, arithmetic and copies ran while one was open for 0% of the time, Pallas kernels for 12%

profile of v7, /device:TPU:0, one launch (start us, length us, event | category | flops | bytes accessed | tf_op | source)
XLA Modules:
  0.0 43.6 jit_solution(6708514631793704423)
XLA Ops:
  0.0 1.6 %prepare.1 = (bf16[16,16,128]{2,1,0:T(8,128)(2,1)}, f32[8,128]{1,0:T(8,128)S(1)}) custom-call(bf16[4,6144]{1,0:T(4,128)(2,1)} %cand_ref.1, bf16[1,6144]{1,0:T(2,128)(2,1)} %tgt_ref.1), custom_call_target="tpu_custom_call" | custom-call | tf_op jit(solution)/shard_map/prepare/pallas_call | solution.py:56
  1.6 7.4 %all-to-all-start = ((bf16[16,16,128]{2,1,0:T(8,128)(2,1)}), bf16[16,16,128]{2,1,0:T(8,128)(2,1)S(1)}, u32[]{:S(2)}, u32[]{:S(2)}) async-start(bf16[16,16,128]{2,1,0:T(8,128)(2,1)} %get-tuple-element.13), calls=%async_computation | async-start | bytes 131072 | tf_op jit(solution)/shard_map/all_to_all | solution.py:311
  9.0 1.9 %load.1.proj_ref = bf16[384,4096]{1,0:T(8,128)(2,1)S(1)} custom-call(bf16[384,8192]{1,0:T(8,128)(2,1)} %proj_ref.5), custom_call_target="tpu_custom_call" | custom-call | bytes 6291456 | tf_op jit(solution)/shard_map/load/pallas_call | solution.py:96
  10.9 5.0 %all-to-all-done = bf16[16,16,128]{2,1,0:T(8,128)(2,1)S(1)} async-done(((bf16[16,16,128]{2,1,0:T(8,128)(2,1)}), bf16[16,16,128]{2,1,0:T(8,128)(2,1)S(1)}, u32[]{:S(2)}, u32[]{:S(2)}) %all-to-all-start) | async-done | bytes 65568 | tf_op jit(solution)/shard_map/all_to_all | solution.py:311
  15.8 0.8 %sketch_other.1 = (f32[8,80,512]{2,1,0:T(8,128)S(1)}, bf16[80,384]{1,0:T(8,128)(2,1)S(1)}) custom-call(bf16[256,128]{1,0:T(8,128)(2,1)S(1)} %bitcast.17, bf16[384,4096]{1,0:T(8,128)(2,1)S(1)} %load.1.proj_ref), custom_call_target="tpu_custom_call" | custom-call | flops 251658240 | bytes 1572864 | tf_op jit(solution)/shard_map/sketch_other/pallas_call | solution.py:157
  16.7 0.1 convert_element_type.89
  16.8 0.1 collective-permute-start
  16.9 2.2 %sketch_own.2 = f32[7,80,512]{2,1,0:T(8,128)S(1)} custom-call(bf16[80,384]{1,0:T(8,128)(2,1)S(1)} %get-tuple-element.16.rows_ref, bf16[384,8192]{1,0:T(8,128)(2,1)} %proj_ref.5), custom_call_target="tpu_custom_call" | custom-call | flops 220200960 | bytes 2752512 | tf_op jit(solution)/shard_map/sketch_own/pallas_call | solution.py:174
  19.1 0.0 collective-permute-done
  19.1 0.1 fusion.10
  19.3 0.3 collective-permute-start.3
  19.6 1.8 %collective-permute-start.1 = (f16[80,512]{1,0:T(8,128)(2,1)S(1)}, f16[80,512]{1,0:T(8,128)(2,1)S(1)}, u32[]{:S(2)}, u32[]{:S(2)}) collective-permute-start(f16[80,512]{1,0:T(8,128)(2,1)S(1)} %get-tuple-element.17), channel_id=1, source_target_pairs={{0,2},{1,13},{2,0},{3,15},{4,6},{5,9},{6,4},{7,11},{8,10},{9,5},{1... | collective-permute-start | bytes 245768 | tf_op jit(solution)/shard_map/ppermute | solution.py:269
  21.4 0.3 collective-permute-start.2
  21.7 3.0 %collective-permute-done.3 = f16[2,80,512]{2,1,0:T(8,128)(2,1)S(1)} collective-permute-done((f16[2,80,512]{2,1,0:T(8,128)(2,1)S(1)}, f16[2,80,512]{2,1,0:T(8,128)(2,1)S(1)}, u32[]{:S(2)}, u32[]{:S(2)}) %collective-permute-start.3) | collective-permute-done | bytes 163872 | tf_op jit(solution)/shard_map/ppermute | solution.py:269
  24.7 0.1 fusion.11
  24.8 0.4 collective-permute-start.4
  25.2 2.3 %collective-permute-start.5 = (f16[80,512]{1,0:T(8,128)(2,1)S(1)}, f16[80,512]{1,0:T(8,128)(2,1)S(1)}, u32[]{:S(2)}, u32[]{:S(2)}) collective-permute-start(f16[80,512]{1,0:T(8,128)(2,1)S(1)} %get-tuple-element.22), channel_id=1, source_target_pairs={{0,12},{1,3},{2,14},{3,1},{4,8},{5,7},{6,10},{7,5},{8,4},{9,11},{1... | collective-permute-start | bytes 245768 | tf_op jit(solution)/shard_map/ppermute | solution.py:269
  27.5 0.9 %collective-permute-start.6 = (f16[80,512]{1,0:T(8,128)(2,1)S(1)}, f16[80,512]{1,0:T(8,128)(2,1)S(1)}, u32[]{:S(2)}, u32[]{:S(2)}) collective-permute-start(f16[80,512]{1,0:T(8,128)(2,1)S(1)} %get-tuple-element.23), channel_id=1, source_target_pairs={{0,4},{1,5},{2,6},{3,7},{4,0},{5,1},{6,2},{7,3},{8,12},{9,13},{10,... | collective-permute-start | bytes 245768 | tf_op jit(solution)/shard_map/ppermute | solution.py:269
  28.4 1.2 %sketch_own.3 = f32[1,80,512]{2,1,0:T(8,128)S(1)} custom-call(bf16[80,384]{1,0:T(8,128)(2,1)S(1)} %get-tuple-element.16.rows_ref, bf16[384,8192]{1,0:T(8,128)(2,1)} %proj_ref.5), custom_call_target="tpu_custom_call" | custom-call | flops 31457280 | bytes 393216 | tf_op jit(solution)/shard_map/sketch_own/pallas_call | solution.py:174
  29.6 0.0 collective-permute-done.1
  29.6 0.0 collective-permute-done.2
  29.6 2.1 %collective-permute-done.4 = f16[80,512]{1,0:T(8,128)(2,1)S(1)} collective-permute-done((f16[80,512]{1,0:T(8,128)(2,1)S(1)}, f16[80,512]{1,0:T(8,128)(2,1)S(1)}, u32[]{:S(2)}, u32[]{:S(2)}) %collective-permute-start.4) | collective-permute-done | bytes 81952 | tf_op jit(solution)/shard_map/ppermute | solution.py:269
  31.7 0.6 %collective-permute-done.5 = f16[80,512]{1,0:T(8,128)(2,1)S(1)} collective-permute-done((f16[80,512]{1,0:T(8,128)(2,1)S(1)}, f16[80,512]{1,0:T(8,128)(2,1)S(1)}, u32[]{:S(2)}, u32[]{:S(2)}) %collective-permute-start.5) | collective-permute-done | bytes 81952 | tf_op jit(solution)/shard_map/ppermute | solution.py:269
  32.2 0.6 %collective-permute-done.6 = f16[80,512]{1,0:T(8,128)(2,1)S(1)} collective-permute-done((f16[80,512]{1,0:T(8,128)(2,1)S(1)}, f16[80,512]{1,0:T(8,128)(2,1)S(1)}, u32[]{:S(2)}, u32[]{:S(2)}) %collective-permute-start.6) | collective-permute-done | bytes 81952 | tf_op jit(solution)/shard_map/ppermute | solution.py:269
  32.8 0.1 bitcast_add_fusion.sum_ref
  32.9 0.3 gram.1
  33.3 9.5 %all_to_all.16 = f32[16,1,128]{2,1,0:T(1,128)S(1)} all-to-all(f32[16,1,128]{2,1,0:T(1,128)S(1)} %bitcast.18), channel_id=1, replica_groups=mesh['grp'=2,'smp'=16] {'smp'}, dimensions={0} | all-to-all | bytes 16384 | tf_op jit(solution)/shard_map/all_to_all | solution.py:323
  42.8 0.9 %finish.1 = f32[4,16]{1,0:T(4,128)} custom-call(f32[16,128]{1,0:T(8,128)S(1)} %bitcast.19, f32[8,128]{1,0:T(8,128)S(1)} %get-tuple-element.20.inv_ref), custom_call_target="tpu_custom_call" | custom-call | tf_op jit(solution)/shard_map/finish/pallas_call | solution.py:251
  (1 shorter events, 0.0 us)
Async XLA Ops:
  1.6 14.3 %all-to-all-start = ((bf16[16,16,128]{2,1,0:T(8,128)(2,1)}), bf16[16,16,128]{2,1,0:T(8,128)(2,1)S(1)}, u32[]{:S(2)}, u32[]{:S(2)}) async-start(bf16[16,16,128]{2,1,0:T(8,128)(2,1)} %get-tuple-element.13), calls=%async_computation | async-start | bytes 131072 | tf_op jit(solution)/shard_map/all_to_all | solution.py:311
  16.8 2.3 %collective-permute-start = (f16[8,80,512]{2,1,0:T(8,128)(2,1)S(1)}, f16[8,80,512]{2,1,0:T(8,128)(2,1)S(1)}, u32[]{:S(2)}, u32[]{:S(2)}) collective-permute-start(f16[8,80,512]{2,1,0:T(8,128)(2,1)S(1)} %convert_element_type.89), channel_id=1, source_target_pairs={{0,1},{1,0},{2,3},{3,2},{4,5},{5,4},{6,7},{7,6},{8,9},{9,8},{10,11... | collective-permute-start | bytes 1966088 | tf_op jit(solution)/shard_map/ppermute | solution.py:316
  19.3 5.4 %collective-permute-start.3 = (f16[2,80,512]{2,1,0:T(8,128)(2,1)S(1)}, f16[2,80,512]{2,1,0:T(8,128)(2,1)S(1)}, u32[]{:S(2)}, u32[]{:S(2)}) collective-permute-start(f16[2,80,512]{2,1,0:T(8,128)(2,1)S(1)} %pad_maximum_fusion), channel_id=1, source_target_pairs={{0,2},{1,5},{2,0},{3,7},{4,6},{5,1},{6,4},{7,3},{8,10},{9,13},{10,... | collective-permute-start | bytes 491528 | tf_op jit(solution)/shard_map/ppermute | solution.py:269
  19.6 10.0 %collective-permute-start.1 = (f16[80,512]{1,0:T(8,128)(2,1)S(1)}, f16[80,512]{1,0:T(8,128)(2,1)S(1)}, u32[]{:S(2)}, u32[]{:S(2)}) collective-permute-start(f16[80,512]{1,0:T(8,128)(2,1)S(1)} %get-tuple-element.17), channel_id=1, source_target_pairs={{0,2},{1,13},{2,0},{3,15},{4,6},{5,9},{6,4},{7,11},{8,10},{9,5},{1... | collective-permute-start | bytes 245768 | tf_op jit(solution)/shard_map/ppermute | solution.py:269
  21.4 8.2 %collective-permute-start.2 = (f16[80,512]{1,0:T(8,128)(2,1)S(1)}, f16[80,512]{1,0:T(8,128)(2,1)S(1)}, u32[]{:S(2)}, u32[]{:S(2)}) collective-permute-start(f16[80,512]{1,0:T(8,128)(2,1)S(1)} %get-tuple-element.18), channel_id=1, source_target_pairs={{0,6},{1,9},{2,4},{3,11},{4,2},{5,13},{6,0},{7,15},{8,14},{9,1},{1... | collective-permute-start | bytes 245768 | tf_op jit(solution)/shard_map/ppermute | solution.py:269
  24.8 6.8 %collective-permute-start.4 = (f16[80,512]{1,0:T(8,128)(2,1)S(1)}, f16[80,512]{1,0:T(8,128)(2,1)S(1)}, u32[]{:S(2)}, u32[]{:S(2)}) collective-permute-start(f16[80,512]{1,0:T(8,128)(2,1)S(1)} %get-tuple-element.21), channel_id=1, source_target_pairs={{0,8},{1,11},{2,10},{3,9},{4,12},{5,15},{6,14},{7,13},{8,0},{9,3},... | collective-permute-start | bytes 245768 | tf_op jit(solution)/shard_map/ppermute | solution.py:269
  25.2 7.1 %collective-permute-start.5 = (f16[80,512]{1,0:T(8,128)(2,1)S(1)}, f16[80,512]{1,0:T(8,128)(2,1)S(1)}, u32[]{:S(2)}, u32[]{:S(2)}) collective-permute-start(f16[80,512]{1,0:T(8,128)(2,1)S(1)} %get-tuple-element.22), channel_id=1, source_target_pairs={{0,12},{1,3},{2,14},{3,1},{4,8},{5,7},{6,10},{7,5},{8,4},{9,11},{1... | collective-permute-start | bytes 245768 | tf_op jit(solution)/shard_map/ppermute | solution.py:269
  27.5 5.4 %collective-permute-start.6 = (f16[80,512]{1,0:T(8,128)(2,1)S(1)}, f16[80,512]{1,0:T(8,128)(2,1)S(1)}, u32[]{:S(2)}, u32[]{:S(2)}) collective-permute-start(f16[80,512]{1,0:T(8,128)(2,1)S(1)} %get-tuple-element.23), channel_id=1, source_target_pairs={{0,4},{1,5},{2,6},{3,7},{4,0},{5,1},{6,2},{7,3},{8,12},{9,13},{10,... | collective-permute-start | bytes 245768 | tf_op jit(solution)/shard_map/ppermute | solution.py:269

commit v8 on v7

--- a/solution.py
+++ b/solution.py
@@ -273,20 +273,15 @@
     def trade(part, place):
         return swap(part, *ROLES[place], devices)
 
-    first, last = range(7), range(7, 8)
-    own = sketch_own(rows, projection, devices, first, STEP)
-    sums = [own[at] + wide(arrived[at]) for at in first]
-    sends = narrow(jnp.stack(sums[:2])), narrow(sums[2]), narrow(sums[3])
-    *sends, rows = lax.optimization_barrier((*sends, rows))
-    passed = swap(sends[0], 1, 2, devices)
-    own = sketch_own(rows, projection, devices, last, STEP)
-    sums += [own[at - 7] + wide(arrived[at]) for at in last]
+    own = sketch_own(rows, projection, devices, range(8), STEP)
+    sums = [own[at] + wide(arrived[at]) for at in range(8)]
+    passed = swap(narrow(jnp.stack(sums[:2])), 1, 2, devices)
     parts = [
-        trade(sends[1], 2),
-        trade(sends[2], 3),
+        trade(narrow(sums[2]), 2),
+        trade(narrow(sums[6]), 6),
+        trade(narrow(sums[3]), 3),
         trade(narrow(sums[4] + wide(passed[0])), 4),
         trade(narrow(sums[5] + wide(passed[1])), 5),
-        trade(narrow(sums[6]), 6),
     ]
     return sums[7] + sum(wide(part) for part in parts)
 

time: 44 us -> 43.7 us (level)
  Pallas kernels: 8.97 us -> 7.83 us
    pallas_call x2 -> x1, Pallas kernels: 3.42 us -> 2.28 us  [sketch_own(): pl.pallas_call(functools.partial(own_kernel, devices, places), in_specs=[...]
    ppermute x6, starting transfers between devices: 5.95 us -> 6.41 us  [swap(): return lax.ppermute(part, 'smp', pairs)]
  transfers between devices with their start and end apart: 8 -> 8, of which waited for: 5 -> 5; matrix products, arithmetic and copies ran while one was open for 0% -> 0% of each run, Pallas kernels for 12% -> 10%
where the time goes in v8:
time: 43.7 us; the launch traced here: 43.4 us
  starting transfers between devices  13.8 us (32%)
  waiting for transfers between devices  11.4 us (26%)
  blocking collectives  9.76 us (22%)
  Pallas kernels  7.83 us (18%)
  other arithmetic  0.48 us (1%)
    all_to_all x1, blocking collectives, shards(): lax.all_to_all(message, 'smp', split_axis=0, concat_axis=0, tiled=True)  9.76 us
    all_to_all x1, starting transfers between devices, shards(): lax.all_to_all(rows, 'smp', split_axis=0, concat_axis=0, tiled=True)  7.36 us
    ppermute x6, waiting for transfers between devices, swap(): return lax.ppermute(part, 'smp', pairs)  6.44 us
    ppermute x6, starting transfers between devices, swap(): return lax.ppermute(part, 'smp', pairs)  6.41 us
    all_to_all x1, waiting for transfers between devices, shards(): lax.all_to_all(rows, 'smp', split_axis=0, concat_axis=0, tiled=True)  4.98 us
    pallas_call x1, Pallas kernels, sketch_own(): pl.pallas_call(functools.partial(own_kernel, devices, places), in_specs=[...  2.28 us
    pallas_call x1, Pallas kernels, load(): pl.pallas_call(load_kernel, in_specs=[pl.BlockSpec(memory_space=pl.ANY)],...  1.91 us
    pallas_call x1, Pallas kernels, prepare(): pl.pallas_call(prep_kernel, out_shape=(in_vmem(shape, jnp.bfloat16), in_v...  1.59 us
  transfers between devices with their start and end apart: 8, of which 5 were waited for; matrix products, arithmetic and copies ran while one was open for 0% of the time, Pallas kernels for 10%

profile of v8, /device:TPU:0, one launch (start us, length us, event | category | flops | bytes accessed | tf_op | source)
XLA Modules:
  0.0 43.4 jit_solution(15038462793302477379)
XLA Ops:
  0.0 1.6 %prepare.1 = (bf16[16,16,128]{2,1,0:T(8,128)(2,1)}, f32[8,128]{1,0:T(8,128)S(1)}) custom-call(bf16[4,6144]{1,0:T(4,128)(2,1)} %cand_ref.1, bf16[1,6144]{1,0:T(2,128)(2,1)} %tgt_ref.1), custom_call_target="tpu_custom_call" | custom-call | tf_op jit(solution)/shard_map/prepare/pallas_call | solution.py:56
  1.6 7.4 %all-to-all-start = ((bf16[16,16,128]{2,1,0:T(8,128)(2,1)}), bf16[16,16,128]{2,1,0:T(8,128)(2,1)S(1)}, u32[]{:S(2)}, u32[]{:S(2)}) async-start(bf16[16,16,128]{2,1,0:T(8,128)(2,1)} %get-tuple-element.9), calls=%async_computation | async-start | bytes 131072 | tf_op jit(solution)/shard_map/all_to_all | solution.py:306
  9.0 1.9 %load.1.proj_ref = bf16[384,4096]{1,0:T(8,128)(2,1)S(1)} custom-call(bf16[384,8192]{1,0:T(8,128)(2,1)} %proj_ref.3), custom_call_target="tpu_custom_call" | custom-call | bytes 6291456 | tf_op jit(solution)/shard_map/load/pallas_call | solution.py:96
  10.9 5.0 %all-to-all-done = bf16[16,16,128]{2,1,0:T(8,128)(2,1)S(1)} async-done(((bf16[16,16,128]{2,1,0:T(8,128)(2,1)}), bf16[16,16,128]{2,1,0:T(8,128)(2,1)S(1)}, u32[]{:S(2)}, u32[]{:S(2)}) %all-to-all-start) | async-done | bytes 65568 | tf_op jit(solution)/shard_map/all_to_all | solution.py:306
  15.8 0.8 %sketch_other.1 = (f32[8,80,512]{2,1,0:T(8,128)S(1)}, bf16[80,384]{1,0:T(8,128)(2,1)S(1)}) custom-call(bf16[256,128]{1,0:T(8,128)(2,1)S(1)} %bitcast.19, bf16[384,4096]{1,0:T(8,128)(2,1)S(1)} %load.1.proj_ref), custom_call_target="tpu_custom_call" | custom-call | flops 251658240 | bytes 1572864 | tf_op jit(solution)/shard_map/sketch_other/pallas_call | solution.py:157
  16.7 0.1 convert_element_type.89
  16.8 0.1 collective-permute-start
  16.9 2.3 %sketch_own.1 = f32[8,80,512]{2,1,0:T(8,128)S(1)} custom-call(bf16[80,384]{1,0:T(8,128)(2,1)S(1)} %get-tuple-element.10.rows_ref, bf16[384,8192]{1,0:T(8,128)(2,1)} %proj_ref.3), custom_call_target="tpu_custom_call" | custom-call | flops 251658240 | bytes 3145728 | tf_op jit(solution)/shard_map/sketch_own/pallas_call | solution.py:174
  19.2 0.0 collective-permute-done
  19.2 0.1 fusion.11
  19.4 0.3 collective-permute-start.4
  19.7 1.8 %collective-permute-start.1 = (f16[80,512]{1,0:T(8,128)(2,1)S(1)}, f16[80,512]{1,0:T(8,128)(2,1)S(1)}, u32[]{:S(2)}, u32[]{:S(2)}) collective-permute-start(f16[80,512]{1,0:T(8,128)(2,1)S(1)} %get-tuple-element.15), channel_id=1, source_target_pairs={{0,2},{1,13},{2,0},{3,15},{4,6},{5,9},{6,4},{7,11},{8,10},{9,5},{1... | collective-permute-start | bytes 245768 | tf_op jit(solution)/shard_map/ppermute | solution.py:269
  21.5 0.3 collective-permute-start.3
  21.8 1.4 %collective-permute-start.2 = (f16[80,512]{1,0:T(8,128)(2,1)S(1)}, f16[80,512]{1,0:T(8,128)(2,1)S(1)}, u32[]{:S(2)}, u32[]{:S(2)}) collective-permute-start(f16[80,512]{1,0:T(8,128)(2,1)S(1)} %get-tuple-element.19), channel_id=1, source_target_pairs={{0,4},{1,5},{2,6},{3,7},{4,0},{5,1},{6,2},{7,3},{8,12},{9,13},{10,... | collective-permute-start | bytes 245768 | tf_op jit(solution)/shard_map/ppermute | solution.py:269
  23.2 1.6 %collective-permute-done.4 = f16[2,80,512]{2,1,0:T(8,128)(2,1)S(1)} collective-permute-done((f16[2,80,512]{2,1,0:T(8,128)(2,1)S(1)}, f16[2,80,512]{2,1,0:T(8,128)(2,1)S(1)}, u32[]{:S(2)}, u32[]{:S(2)}) %collective-permute-start.4) | collective-permute-done | bytes 163872 | tf_op jit(solution)/shard_map/ppermute | solution.py:269
  24.8 0.1 fusion.14
  24.9 0.4 collective-permute-start.5
  25.2 2.3 %collective-permute-start.6 = (f16[80,512]{1,0:T(8,128)(2,1)S(1)}, f16[80,512]{1,0:T(8,128)(2,1)S(1)}, u32[]{:S(2)}, u32[]{:S(2)}) collective-permute-start(f16[80,512]{1,0:T(8,128)(2,1)S(1)} %get-tuple-element.14), channel_id=1, source_target_pairs={{0,12},{1,3},{2,14},{3,1},{4,8},{5,7},{6,10},{7,5},{8,4},{9,11},{1... | collective-permute-start | bytes 245768 | tf_op jit(solution)/shard_map/ppermute | solution.py:269
  27.5 0.0 collective-permute-done.1
  27.5 0.3 collective-permute-done.3
  27.8 2.0 %collective-permute-done.2 = f16[80,512]{1,0:T(8,128)(2,1)S(1)} collective-permute-done((f16[80,512]{1,0:T(8,128)(2,1)S(1)}, f16[80,512]{1,0:T(8,128)(2,1)S(1)}, u32[]{:S(2)}, u32[]{:S(2)}) %collective-permute-start.2) | collective-permute-done | bytes 81952 | tf_op jit(solution)/shard_map/ppermute | solution.py:269
  29.8 2.5 %collective-permute-done.5 = f16[80,512]{1,0:T(8,128)(2,1)S(1)} collective-permute-done((f16[80,512]{1,0:T(8,128)(2,1)S(1)}, f16[80,512]{1,0:T(8,128)(2,1)S(1)}, u32[]{:S(2)}, u32[]{:S(2)}) %collective-permute-start.5) | collective-permute-done | bytes 81952 | tf_op jit(solution)/shard_map/ppermute | solution.py:269
  32.3 0.0 collective-permute-done.6
  32.3 0.1 fusion.10.sum_ref
  32.4 0.3 gram.1
  32.8 9.8 %all_to_all.16 = f32[16,1,128]{2,1,0:T(1,128)S(1)} all-to-all(f32[16,1,128]{2,1,0:T(1,128)S(1)} %bitcast.20), channel_id=1, replica_groups=mesh['grp'=2,'smp'=16] {'smp'}, dimensions={0} | all-to-all | bytes 16384 | tf_op jit(solution)/shard_map/all_to_all | solution.py:318
  42.5 0.9 %finish.1 = f32[4,16]{1,0:T(4,128)} custom-call(f32[16,128]{1,0:T(8,128)S(1)} %bitcast.21, f32[8,128]{1,0:T(8,128)S(1)} %get-tuple-element.12.inv_ref), custom_call_target="tpu_custom_call" | custom-call | tf_op jit(solution)/shard_map/finish/pallas_call | solution.py:251
  (1 shorter events, 0.0 us)
Async XLA Ops:
  1.6 14.3 %all-to-all-start = ((bf16[16,16,128]{2,1,0:T(8,128)(2,1)}), bf16[16,16,128]{2,1,0:T(8,128)(2,1)S(1)}, u32[]{:S(2)}, u32[]{:S(2)}) async-start(bf16[16,16,128]{2,1,0:T(8,128)(2,1)} %get-tuple-element.9), calls=%async_computation | async-start | bytes 131072 | tf_op jit(solution)/shard_map/all_to_all | solution.py:306
  16.8 2.4 %collective-permute-start = (f16[8,80,512]{2,1,0:T(8,128)(2,1)S(1)}, f16[8,80,512]{2,1,0:T(8,128)(2,1)S(1)}, u32[]{:S(2)}, u32[]{:S(2)}) collective-permute-start(f16[8,80,512]{2,1,0:T(8,128)(2,1)S(1)} %convert_element_type.89), channel_id=1, source_target_pairs={{0,1},{1,0},{2,3},{3,2},{4,5},{5,4},{6,7},{7,6},{8,9},{9,8},{10,11... | collective-permute-start | bytes 1966088 | tf_op jit(solution)/shard_map/ppermute | solution.py:311
  19.4 5.4 %collective-permute-start.4 = (f16[2,80,512]{2,1,0:T(8,128)(2,1)S(1)}, f16[2,80,512]{2,1,0:T(8,128)(2,1)S(1)}, u32[]{:S(2)}, u32[]{:S(2)}) collective-permute-start(f16[2,80,512]{2,1,0:T(8,128)(2,1)S(1)} %pad_maximum_fusion), channel_id=1, source_target_pairs={{0,2},{1,5},{2,0},{3,7},{4,6},{5,1},{6,4},{7,3},{8,10},{9,13},{10,... | collective-permute-start | bytes 491528 | tf_op jit(solution)/shard_map/ppermute | solution.py:269
  19.7 7.8 %collective-permute-start.1 = (f16[80,512]{1,0:T(8,128)(2,1)S(1)}, f16[80,512]{1,0:T(8,128)(2,1)S(1)}, u32[]{:S(2)}, u32[]{:S(2)}) collective-permute-start(f16[80,512]{1,0:T(8,128)(2,1)S(1)} %get-tuple-element.15), channel_id=1, source_target_pairs={{0,2},{1,13},{2,0},{3,15},{4,6},{5,9},{6,4},{7,11},{8,10},{9,5},{1... | collective-permute-start | bytes 245768 | tf_op jit(solution)/shard_map/ppermute | solution.py:269
  21.5 6.4 %collective-permute-start.3 = (f16[80,512]{1,0:T(8,128)(2,1)S(1)}, f16[80,512]{1,0:T(8,128)(2,1)S(1)}, u32[]{:S(2)}, u32[]{:S(2)}) collective-permute-start(f16[80,512]{1,0:T(8,128)(2,1)S(1)} %get-tuple-element.18), channel_id=1, source_target_pairs={{0,6},{1,9},{2,4},{3,11},{4,2},{5,13},{6,0},{7,15},{8,14},{9,1},{1... | collective-permute-start | bytes 245768 | tf_op jit(solution)/shard_map/ppermute | solution.py:269
  21.8 8.0 %collective-permute-start.2 = (f16[80,512]{1,0:T(8,128)(2,1)S(1)}, f16[80,512]{1,0:T(8,128)(2,1)S(1)}, u32[]{:S(2)}, u32[]{:S(2)}) collective-permute-start(f16[80,512]{1,0:T(8,128)(2,1)S(1)} %get-tuple-element.19), channel_id=1, source_target_pairs={{0,4},{1,5},{2,6},{3,7},{4,0},{5,1},{6,2},{7,3},{8,12},{9,13},{10,... | collective-permute-start | bytes 245768 | tf_op jit(solution)/shard_map/ppermute | solution.py:269
  24.9 7.5 %collective-permute-start.5 = (f16[80,512]{1,0:T(8,128)(2,1)S(1)}, f16[80,512]{1,0:T(8,128)(2,1)S(1)}, u32[]{:S(2)}, u32[]{:S(2)}) collective-permute-start(f16[80,512]{1,0:T(8,128)(2,1)S(1)} %get-tuple-element.13), channel_id=1, source_target_pairs={{0,8},{1,11},{2,10},{3,9},{4,12},{5,15},{6,14},{7,13},{8,0},{9,3},... | collective-permute-start | bytes 245768 | tf_op jit(solution)/shard_map/ppermute | solution.py:269
  25.2 7.1 %collective-permute-start.6 = (f16[80,512]{1,0:T(8,128)(2,1)S(1)}, f16[80,512]{1,0:T(8,128)(2,1)S(1)}, u32[]{:S(2)}, u32[]{:S(2)}) collective-permute-start(f16[80,512]{1,0:T(8,128)(2,1)S(1)} %get-tuple-element.14), channel_id=1, source_target_pairs={{0,12},{1,3},{2,14},{3,1},{4,8},{5,7},{6,10},{7,5},{8,4},{9,11},{1... | collective-permute-start | bytes 245768 | tf_op jit(solution)/shard_map/ppermute | solution.py:269

commit v9 on v8

--- a/solution.py
+++ b/solution.py
@@ -238,13 +238,14 @@
     t_sq = total[:, pc * devices : (pc + 1) * devices]
     inv_t = total[:, (pc + 1) * devices : (pc + 2) * devices]
     t_scale = inv_t * lax.rsqrt(t_sq / K * inv_t * inv_t + EPS)
-    for slot in range(pc):
-        at = (pc + 2) * devices + slot
-        c_sq = total[:, at : at + 1]
-        inv_c = inv_ref[slot : slot + 1, 0:1]
-        c_scale = inv_c * lax.rsqrt(c_sq / K * inv_c * inv_c + EPS)
-        scores = total[:, slot * devices : (slot + 1) * devices]
-        out_ref[slot : slot + 1, :] = scores * c_scale * t_scale / K
+    c_sq = total[:, (pc + 2) * devices : (pc + 2) * devices + pc]
+    row = lax.broadcasted_iota(jnp.int32, (pc, pc), 0)
+    column = lax.broadcasted_iota(jnp.int32, (pc, pc), 1)
+    c_sq = jnp.sum(jnp.where(row == column, c_sq, 0.0), axis=1, keepdims=True)
+    inv_c = inv_ref[:pc, 0:1]
+    c_scale = inv_c * lax.rsqrt(c_sq / K * inv_c * inv_c + EPS)
+    slots = [total[:, slot * devices : (slot + 1) * devices] for slot in range(pc)]
+    out_ref[...] = jnp.concatenate(slots, axis=0) * c_scale * t_scale / K
 
 
 def finish(parts, inv, pc, devices):

time: 43.7 us -> 43.7 us (level)
  no operation moved by 1% of the time
where the time goes in v9:
time: 43.7 us; the launch traced here: 43.4 us
  starting transfers between devices  13.8 us (32%)
  waiting for transfers between devices  11.4 us (26%)
  blocking collectives  9.76 us (22%)
  Pallas kernels  7.76 us (18%)
  other arithmetic  0.48 us (1%)
    all_to_all x1, blocking collectives, shards(): lax.all_to_all(message, 'smp', split_axis=0, concat_axis=0, tiled=True)  9.76 us
    all_to_all x1, starting transfers between devices, shards(): lax.all_to_all(rows, 'smp', split_axis=0, concat_axis=0, tiled=True)  7.36 us
    ppermute x6, waiting for transfers between devices, swap(): return lax.ppermute(part, 'smp', pairs)  6.44 us
    ppermute x6, starting transfers between devices, swap(): return lax.ppermute(part, 'smp', pairs)  6.41 us
    all_to_all x1, waiting for transfers between devices, shards(): lax.all_to_all(rows, 'smp', split_axis=0, concat_axis=0, tiled=True)  4.98 us
    pallas_call x1, Pallas kernels, sketch_own(): pl.pallas_call(functools.partial(own_kernel, devices, places), in_specs=[...  2.28 us
    pallas_call x1, Pallas kernels, load(): pl.pallas_call(load_kernel, in_specs=[pl.BlockSpec(memory_space=pl.ANY)],...  1.91 us
    pallas_call x1, Pallas kernels, prepare(): pl.pallas_call(prep_kernel, out_shape=(in_vmem(shape, jnp.bfloat16), in_v...  1.59 us
  transfers between devices with their start and end apart: 8, of which 5 were waited for; matrix products, arithmetic and copies ran while one was open for 0% of the time, Pallas kernels for 10%

profile of v9, /device:TPU:0, one launch (start us, length us, event | category | flops | bytes accessed | tf_op | source)
XLA Modules:
  0.0 43.4 jit_solution(16812095388360927652)
XLA Ops:
  0.0 1.6 %prepare.1 = (bf16[16,16,128]{2,1,0:T(8,128)(2,1)}, f32[8,128]{1,0:T(8,128)S(1)}) custom-call(bf16[4,6144]{1,0:T(4,128)(2,1)} %cand_ref.1, bf16[1,6144]{1,0:T(2,128)(2,1)} %tgt_ref.1), custom_call_target="tpu_custom_call" | custom-call | tf_op jit(solution)/shard_map/prepare/pallas_call | solution.py:56
  1.6 7.4 %all-to-all-start = ((bf16[16,16,128]{2,1,0:T(8,128)(2,1)}), bf16[16,16,128]{2,1,0:T(8,128)(2,1)S(1)}, u32[]{:S(2)}, u32[]{:S(2)}) async-start(bf16[16,16,128]{2,1,0:T(8,128)(2,1)} %get-tuple-element.9), calls=%async_computation | async-start | bytes 131072 | tf_op jit(solution)/shard_map/all_to_all | solution.py:307
  9.0 1.9 %load.1.proj_ref = bf16[384,4096]{1,0:T(8,128)(2,1)S(1)} custom-call(bf16[384,8192]{1,0:T(8,128)(2,1)} %proj_ref.3), custom_call_target="tpu_custom_call" | custom-call | bytes 6291456 | tf_op jit(solution)/shard_map/load/pallas_call | solution.py:96
  10.9 5.0 %all-to-all-done = bf16[16,16,128]{2,1,0:T(8,128)(2,1)S(1)} async-done(((bf16[16,16,128]{2,1,0:T(8,128)(2,1)}), bf16[16,16,128]{2,1,0:T(8,128)(2,1)S(1)}, u32[]{:S(2)}, u32[]{:S(2)}) %all-to-all-start) | async-done | bytes 65568 | tf_op jit(solution)/shard_map/all_to_all | solution.py:307
  15.8 0.8 %sketch_other.1 = (f32[8,80,512]{2,1,0:T(8,128)S(1)}, bf16[80,384]{1,0:T(8,128)(2,1)S(1)}) custom-call(bf16[256,128]{1,0:T(8,128)(2,1)S(1)} %bitcast.19, bf16[384,4096]{1,0:T(8,128)(2,1)S(1)} %load.1.proj_ref), custom_call_target="tpu_custom_call" | custom-call | flops 251658240 | bytes 1572864 | tf_op jit(solution)/shard_map/sketch_other/pallas_call | solution.py:157
  16.7 0.1 convert_element_type.89
  16.8 0.1 collective-permute-start
  16.9 2.3 %sketch_own.1 = f32[8,80,512]{2,1,0:T(8,128)S(1)} custom-call(bf16[80,384]{1,0:T(8,128)(2,1)S(1)} %get-tuple-element.10.rows_ref, bf16[384,8192]{1,0:T(8,128)(2,1)} %proj_ref.3), custom_call_target="tpu_custom_call" | custom-call | flops 251658240 | bytes 3145728 | tf_op jit(solution)/shard_map/sketch_own/pallas_call | solution.py:174
  19.2 0.0 collective-permute-done
  19.2 0.1 fusion.11
  19.4 0.3 collective-permute-start.4
  19.7 1.8 %collective-permute-start.1 = (f16[80,512]{1,0:T(8,128)(2,1)S(1)}, f16[80,512]{1,0:T(8,128)(2,1)S(1)}, u32[]{:S(2)}, u32[]{:S(2)}) collective-permute-start(f16[80,512]{1,0:T(8,128)(2,1)S(1)} %get-tuple-element.15), channel_id=1, source_target_pairs={{0,2},{1,13},{2,0},{3,15},{4,6},{5,9},{6,4},{7,11},{8,10},{9,5},{1... | collective-permute-start | bytes 245768 | tf_op jit(solution)/shard_map/ppermute | solution.py:270
  21.5 0.3 collective-permute-start.3
  21.8 1.4 %collective-permute-start.2 = (f16[80,512]{1,0:T(8,128)(2,1)S(1)}, f16[80,512]{1,0:T(8,128)(2,1)S(1)}, u32[]{:S(2)}, u32[]{:S(2)}) collective-permute-start(f16[80,512]{1,0:T(8,128)(2,1)S(1)} %get-tuple-element.19), channel_id=1, source_target_pairs={{0,4},{1,5},{2,6},{3,7},{4,0},{5,1},{6,2},{7,3},{8,12},{9,13},{10,... | collective-permute-start | bytes 245768 | tf_op jit(solution)/shard_map/ppermute | solution.py:270
  23.2 1.6 %collective-permute-done.4 = f16[2,80,512]{2,1,0:T(8,128)(2,1)S(1)} collective-permute-done((f16[2,80,512]{2,1,0:T(8,128)(2,1)S(1)}, f16[2,80,512]{2,1,0:T(8,128)(2,1)S(1)}, u32[]{:S(2)}, u32[]{:S(2)}) %collective-permute-start.4) | collective-permute-done | bytes 163872 | tf_op jit(solution)/shard_map/ppermute | solution.py:270
  24.8 0.1 fusion.14
  24.9 0.4 collective-permute-start.5
  25.2 2.3 %collective-permute-start.6 = (f16[80,512]{1,0:T(8,128)(2,1)S(1)}, f16[80,512]{1,0:T(8,128)(2,1)S(1)}, u32[]{:S(2)}, u32[]{:S(2)}) collective-permute-start(f16[80,512]{1,0:T(8,128)(2,1)S(1)} %get-tuple-element.14), channel_id=1, source_target_pairs={{0,12},{1,3},{2,14},{3,1},{4,8},{5,7},{6,10},{7,5},{8,4},{9,11},{1... | collective-permute-start | bytes 245768 | tf_op jit(solution)/shard_map/ppermute | solution.py:270
  27.5 0.0 collective-permute-done.1
  27.5 0.3 collective-permute-done.3
  27.8 2.0 %collective-permute-done.2 = f16[80,512]{1,0:T(8,128)(2,1)S(1)} collective-permute-done((f16[80,512]{1,0:T(8,128)(2,1)S(1)}, f16[80,512]{1,0:T(8,128)(2,1)S(1)}, u32[]{:S(2)}, u32[]{:S(2)}) %collective-permute-start.2) | collective-permute-done | bytes 81952 | tf_op jit(solution)/shard_map/ppermute | solution.py:270
  29.8 2.5 %collective-permute-done.5 = f16[80,512]{1,0:T(8,128)(2,1)S(1)} collective-permute-done((f16[80,512]{1,0:T(8,128)(2,1)S(1)}, f16[80,512]{1,0:T(8,128)(2,1)S(1)}, u32[]{:S(2)}, u32[]{:S(2)}) %collective-permute-start.5) | collective-permute-done | bytes 81952 | tf_op jit(solution)/shard_map/ppermute | solution.py:270
  32.3 0.0 collective-permute-done.6
  32.3 0.1 fusion.10.sum_ref
  32.4 0.3 gram.1
  32.8 9.8 %all_to_all.16 = f32[16,1,128]{2,1,0:T(1,128)S(1)} all-to-all(f32[16,1,128]{2,1,0:T(1,128)S(1)} %bitcast.20), channel_id=1, replica_groups=mesh['grp'=2,'smp'=16] {'smp'}, dimensions={0} | all-to-all | bytes 16384 | tf_op jit(solution)/shard_map/all_to_all | solution.py:319
  42.5 0.8 %finish.1 = f32[4,16]{1,0:T(4,128)} custom-call(f32[16,128]{1,0:T(8,128)S(1)} %bitcast.21, f32[8,128]{1,0:T(8,128)S(1)} %get-tuple-element.12.inv_ref), custom_call_target="tpu_custom_call" | custom-call | tf_op jit(solution)/shard_map/finish/pallas_call | solution.py:252
  (1 shorter events, 0.0 us)
Async XLA Ops:
  1.6 14.3 %all-to-all-start = ((bf16[16,16,128]{2,1,0:T(8,128)(2,1)}), bf16[16,16,128]{2,1,0:T(8,128)(2,1)S(1)}, u32[]{:S(2)}, u32[]{:S(2)}) async-start(bf16[16,16,128]{2,1,0:T(8,128)(2,1)} %get-tuple-element.9), calls=%async_computation | async-start | bytes 131072 | tf_op jit(solution)/shard_map/all_to_all | solution.py:307
  16.8 2.4 %collective-permute-start = (f16[8,80,512]{2,1,0:T(8,128)(2,1)S(1)}, f16[8,80,512]{2,1,0:T(8,128)(2,1)S(1)}, u32[]{:S(2)}, u32[]{:S(2)}) collective-permute-start(f16[8,80,512]{2,1,0:T(8,128)(2,1)S(1)} %convert_element_type.89), channel_id=1, source_target_pairs={{0,1},{1,0},{2,3},{3,2},{4,5},{5,4},{6,7},{7,6},{8,9},{9,8},{10,11... | collective-permute-start | bytes 1966088 | tf_op jit(solution)/shard_map/ppermute | solution.py:312
  19.4 5.4 %collective-permute-start.4 = (f16[2,80,512]{2,1,0:T(8,128)(2,1)S(1)}, f16[2,80,512]{2,1,0:T(8,128)(2,1)S(1)}, u32[]{:S(2)}, u32[]{:S(2)}) collective-permute-start(f16[2,80,512]{2,1,0:T(8,128)(2,1)S(1)} %pad_maximum_fusion), channel_id=1, source_target_pairs={{0,2},{1,5},{2,0},{3,7},{4,6},{5,1},{6,4},{7,3},{8,10},{9,13},{10,... | collective-permute-start | bytes 491528 | tf_op jit(solution)/shard_map/ppermute | solution.py:270
  19.7 7.8 %collective-permute-start.1 = (f16[80,512]{1,0:T(8,128)(2,1)S(1)}, f16[80,512]{1,0:T(8,128)(2,1)S(1)}, u32[]{:S(2)}, u32[]{:S(2)}) collective-permute-start(f16[80,512]{1,0:T(8,128)(2,1)S(1)} %get-tuple-element.15), channel_id=1, source_target_pairs={{0,2},{1,13},{2,0},{3,15},{4,6},{5,9},{6,4},{7,11},{8,10},{9,5},{1... | collective-permute-start | bytes 245768 | tf_op jit(solution)/shard_map/ppermute | solution.py:270
  21.5 6.4 %collective-permute-start.3 = (f16[80,512]{1,0:T(8,128)(2,1)S(1)}, f16[80,512]{1,0:T(8,128)(2,1)S(1)}, u32[]{:S(2)}, u32[]{:S(2)}) collective-permute-start(f16[80,512]{1,0:T(8,128)(2,1)S(1)} %get-tuple-element.18), channel_id=1, source_target_pairs={{0,6},{1,9},{2,4},{3,11},{4,2},{5,13},{6,0},{7,15},{8,14},{9,1},{1... | collective-permute-start | bytes 245768 | tf_op jit(solution)/shard_map/ppermute | solution.py:270
  21.8 8.0 %collective-permute-start.2 = (f16[80,512]{1,0:T(8,128)(2,1)S(1)}, f16[80,512]{1,0:T(8,128)(2,1)S(1)}, u32[]{:S(2)}, u32[]{:S(2)}) collective-permute-start(f16[80,512]{1,0:T(8,128)(2,1)S(1)} %get-tuple-element.19), channel_id=1, source_target_pairs={{0,4},{1,5},{2,6},{3,7},{4,0},{5,1},{6,2},{7,3},{8,12},{9,13},{10,... | collective-permute-start | bytes 245768 | tf_op jit(solution)/shard_map/ppermute | solution.py:270
  24.9 7.5 %collective-permute-start.5 = (f16[80,512]{1,0:T(8,128)(2,1)S(1)}, f16[80,512]{1,0:T(8,128)(2,1)S(1)}, u32[]{:S(2)}, u32[]{:S(2)}) collective-permute-start(f16[80,512]{1,0:T(8,128)(2,1)S(1)} %get-tuple-element.13), channel_id=1, source_target_pairs={{0,8},{1,11},{2,10},{3,9},{4,12},{5,15},{6,14},{7,13},{8,0},{9,3},... | collective-permute-start | bytes 245768 | tf_op jit(solution)/shard_map/ppermute | solution.py:270
  25.2 7.1 %collective-permute-start.6 = (f16[80,512]{1,0:T(8,128)(2,1)S(1)}, f16[80,512]{1,0:T(8,128)(2,1)S(1)}, u32[]{:S(2)}, u32[]{:S(2)}) collective-permute-start(f16[80,512]{1,0:T(8,128)(2,1)S(1)} %get-tuple-element.14), channel_id=1, source_target_pairs={{0,12},{1,3},{2,14},{3,1},{4,8},{5,7},{6,10},{7,5},{8,4},{9,11},{1... | collective-permute-start | bytes 245768 | tf_op jit(solution)/shard_map/ppermute | solution.py:270

commit v10 on v9

--- a/solution.py
+++ b/solution.py
@@ -73,7 +73,7 @@
     return devices == 16
 
 
-ROLES = ((5, 7), (7, 3), (1, 6), (3, 4), (4, 5), (6, 1), (2, 2), (0, 0))
+ROLES = ((5, 7), (7, 3), (3, 6), (1, 4), (4, 5), (6, 1), (2, 2), (0, 0))
 
 
 def block_of(place, core, devices):

time: 43.7 us -> 43.7 us (level)
  transfers between devices with their start and end apart: 8 -> 8, of which waited for: 5 -> 4; matrix products, arithmetic and copies ran while one was open for 0% -> 0% of each run, Pallas kernels for 10% -> 10%
where the time goes in v10:
time: 43.7 us; the launch traced here: 43.4 us
  starting transfers between devices  13.7 us (31%)
  waiting for transfers between devices  11.4 us (26%)
  blocking collectives  9.95 us (23%)
  Pallas kernels  7.76 us (18%)
  other arithmetic  0.48 us (1%)
    all_to_all x1, blocking collectives, shards(): lax.all_to_all(message, 'smp', split_axis=0, concat_axis=0, tiled=True)  9.95 us
    all_to_all x1, starting transfers between devices, shards(): lax.all_to_all(rows, 'smp', split_axis=0, concat_axis=0, tiled=True)  7.36 us
    ppermute x6, waiting for transfers between devices, swap(): return lax.ppermute(part, 'smp', pairs)  6.42 us
    ppermute x6, starting transfers between devices, swap(): return lax.ppermute(part, 'smp', pairs)  6.24 us
    all_to_all x1, waiting for transfers between devices, shards(): lax.all_to_all(rows, 'smp', split_axis=0, concat_axis=0, tiled=True)  4.98 us
    pallas_call x1, Pallas kernels, sketch_own(): pl.pallas_call(functools.partial(own_kernel, devices, places), in_specs=[...  2.28 us
    pallas_call x1, Pallas kernels, load(): pl.pallas_call(load_kernel, in_specs=[pl.BlockSpec(memory_space=pl.ANY)],...  1.91 us
    pallas_call x1, Pallas kernels, prepare(): pl.pallas_call(prep_kernel, out_shape=(in_vmem(shape, jnp.bfloat16), in_v...  1.59 us
  transfers between devices with their start and end apart: 8, of which 4 were waited for; matrix products, arithmetic and copies ran while one was open for 0% of the time, Pallas kernels for 10%

profile of v10, /device:TPU:0, one launch (start us, length us, event | category | flops | bytes accessed | tf_op | source)
XLA Modules:
  0.0 43.4 jit_solution(55118920182381628)
XLA Ops:
  0.0 1.6 %prepare.1 = (bf16[16,16,128]{2,1,0:T(8,128)(2,1)}, f32[8,128]{1,0:T(8,128)S(1)}) custom-call(bf16[4,6144]{1,0:T(4,128)(2,1)} %cand_ref.1, bf16[1,6144]{1,0:T(2,128)(2,1)} %tgt_ref.1), custom_call_target="tpu_custom_call" | custom-call | tf_op jit(solution)/shard_map/prepare/pallas_call | solution.py:56
  1.6 7.4 %all-to-all-start = ((bf16[16,16,128]{2,1,0:T(8,128)(2,1)}), bf16[16,16,128]{2,1,0:T(8,128)(2,1)S(1)}, u32[]{:S(2)}, u32[]{:S(2)}) async-start(bf16[16,16,128]{2,1,0:T(8,128)(2,1)} %get-tuple-element.9), calls=%async_computation | async-start | bytes 131072 | tf_op jit(solution)/shard_map/all_to_all | solution.py:307
  9.0 1.9 %load.1.proj_ref = bf16[384,4096]{1,0:T(8,128)(2,1)S(1)} custom-call(bf16[384,8192]{1,0:T(8,128)(2,1)} %proj_ref.3), custom_call_target="tpu_custom_call" | custom-call | bytes 6291456 | tf_op jit(solution)/shard_map/load/pallas_call | solution.py:96
  10.9 5.0 %all-to-all-done = bf16[16,16,128]{2,1,0:T(8,128)(2,1)S(1)} async-done(((bf16[16,16,128]{2,1,0:T(8,128)(2,1)}), bf16[16,16,128]{2,1,0:T(8,128)(2,1)S(1)}, u32[]{:S(2)}, u32[]{:S(2)}) %all-to-all-start) | async-done | bytes 65568 | tf_op jit(solution)/shard_map/all_to_all | solution.py:307
  15.8 0.8 %sketch_other.1 = (f32[8,80,512]{2,1,0:T(8,128)S(1)}, bf16[80,384]{1,0:T(8,128)(2,1)S(1)}) custom-call(bf16[256,128]{1,0:T(8,128)(2,1)S(1)} %bitcast.19, bf16[384,4096]{1,0:T(8,128)(2,1)S(1)} %load.1.proj_ref), custom_call_target="tpu_custom_call" | custom-call | flops 251658240 | bytes 1572864 | tf_op jit(solution)/shard_map/sketch_other/pallas_call | solution.py:157
  16.7 0.1 convert_element_type.89
  16.8 0.1 collective-permute-start
  16.9 2.3 %sketch_own.1 = f32[8,80,512]{2,1,0:T(8,128)S(1)} custom-call(bf16[80,384]{1,0:T(8,128)(2,1)S(1)} %get-tuple-element.10.rows_ref, bf16[384,8192]{1,0:T(8,128)(2,1)} %proj_ref.3), custom_call_target="tpu_custom_call" | custom-call | flops 251658240 | bytes 3145728 | tf_op jit(solution)/shard_map/sketch_own/pallas_call | solution.py:174
  19.2 0.0 collective-permute-done
  19.2 0.1 fusion.11
  19.4 0.3 collective-permute-start.4
  19.7 1.5 %collective-permute-start.1 = (f16[80,512]{1,0:T(8,128)(2,1)S(1)}, f16[80,512]{1,0:T(8,128)(2,1)S(1)}, u32[]{:S(2)}, u32[]{:S(2)}) collective-permute-start(f16[80,512]{1,0:T(8,128)(2,1)S(1)} %get-tuple-element.15), channel_id=1, source_target_pairs={{0,6},{1,13},{2,4},{3,15},{4,2},{5,9},{6,0},{7,11},{8,14},{9,5},{1... | collective-permute-start | bytes 245768 | tf_op jit(solution)/shard_map/ppermute | solution.py:270
  21.1 0.7 %collective-permute-start.3 = (f16[80,512]{1,0:T(8,128)(2,1)S(1)}, f16[80,512]{1,0:T(8,128)(2,1)S(1)}, u32[]{:S(2)}, u32[]{:S(2)}) collective-permute-start(f16[80,512]{1,0:T(8,128)(2,1)S(1)} %get-tuple-element.18), channel_id=1, source_target_pairs={{0,2},{1,9},{2,0},{3,11},{4,6},{5,13},{6,4},{7,15},{8,10},{9,1},{1... | collective-permute-start | bytes 245768 | tf_op jit(solution)/shard_map/ppermute | solution.py:270
  21.8 1.4 %collective-permute-start.2 = (f16[80,512]{1,0:T(8,128)(2,1)S(1)}, f16[80,512]{1,0:T(8,128)(2,1)S(1)}, u32[]{:S(2)}, u32[]{:S(2)}) collective-permute-start(f16[80,512]{1,0:T(8,128)(2,1)S(1)} %get-tuple-element.19), channel_id=1, source_target_pairs={{0,4},{1,5},{2,6},{3,7},{4,0},{5,1},{6,2},{7,3},{8,12},{9,13},{10,... | collective-permute-start | bytes 245768 | tf_op jit(solution)/shard_map/ppermute | solution.py:270
  23.2 1.9 %collective-permute-done.4 = f16[2,80,512]{2,1,0:T(8,128)(2,1)S(1)} collective-permute-done((f16[2,80,512]{2,1,0:T(8,128)(2,1)S(1)}, f16[2,80,512]{2,1,0:T(8,128)(2,1)S(1)}, u32[]{:S(2)}, u32[]{:S(2)}) %collective-permute-start.4) | collective-permute-done | bytes 163872 | tf_op jit(solution)/shard_map/ppermute | solution.py:270
  25.1 0.1 fusion.14
  25.1 0.3 collective-permute-start.5
  25.4 2.2 %collective-permute-start.6 = (f16[80,512]{1,0:T(8,128)(2,1)S(1)}, f16[80,512]{1,0:T(8,128)(2,1)S(1)}, u32[]{:S(2)}, u32[]{:S(2)}) collective-permute-start(f16[80,512]{1,0:T(8,128)(2,1)S(1)} %get-tuple-element.14), channel_id=1, source_target_pairs={{0,12},{1,3},{2,14},{3,1},{4,8},{5,7},{6,10},{7,5},{8,4},{9,11},{1... | collective-permute-start | bytes 245768 | tf_op jit(solution)/shard_map/ppermute | solution.py:270
  27.6 0.0 collective-permute-done.1
  27.6 0.0 collective-permute-done.3
  27.6 2.1 %collective-permute-done.2 = f16[80,512]{1,0:T(8,128)(2,1)S(1)} collective-permute-done((f16[80,512]{1,0:T(8,128)(2,1)S(1)}, f16[80,512]{1,0:T(8,128)(2,1)S(1)}, u32[]{:S(2)}, u32[]{:S(2)}) %collective-permute-start.2) | collective-permute-done | bytes 81952 | tf_op jit(solution)/shard_map/ppermute | solution.py:270
  29.7 2.4 %collective-permute-done.5 = f16[80,512]{1,0:T(8,128)(2,1)S(1)} collective-permute-done((f16[80,512]{1,0:T(8,128)(2,1)S(1)}, f16[80,512]{1,0:T(8,128)(2,1)S(1)}, u32[]{:S(2)}, u32[]{:S(2)}) %collective-permute-start.5) | collective-permute-done | bytes 81952 | tf_op jit(solution)/shard_map/ppermute | solution.py:270
  32.1 0.0 collective-permute-done.6
  32.1 0.1 fusion.10.sum_ref
  32.2 0.3 gram.1
  32.6 9.9 %all_to_all.16 = f32[16,1,128]{2,1,0:T(1,128)S(1)} all-to-all(f32[16,1,128]{2,1,0:T(1,128)S(1)} %bitcast.20), channel_id=1, replica_groups=mesh['grp'=2,'smp'=16] {'smp'}, dimensions={0} | all-to-all | bytes 16384 | tf_op jit(solution)/shard_map/all_to_all | solution.py:319
  42.5 0.8 %finish.1 = f32[4,16]{1,0:T(4,128)} custom-call(f32[16,128]{1,0:T(8,128)S(1)} %bitcast.21, f32[8,128]{1,0:T(8,128)S(1)} %get-tuple-element.12.inv_ref), custom_call_target="tpu_custom_call" | custom-call | tf_op jit(solution)/shard_map/finish/pallas_call | solution.py:252
  (1 shorter events, 0.0 us)
Async XLA Ops:
  1.6 14.3 %all-to-all-start = ((bf16[16,16,128]{2,1,0:T(8,128)(2,1)}), bf16[16,16,128]{2,1,0:T(8,128)(2,1)S(1)}, u32[]{:S(2)}, u32[]{:S(2)}) async-start(bf16[16,16,128]{2,1,0:T(8,128)(2,1)} %get-tuple-element.9), calls=%async_computation | async-start | bytes 131072 | tf_op jit(solution)/shard_map/all_to_all | solution.py:307
  16.8 2.4 %collective-permute-start = (f16[8,80,512]{2,1,0:T(8,128)(2,1)S(1)}, f16[8,80,512]{2,1,0:T(8,128)(2,1)S(1)}, u32[]{:S(2)}, u32[]{:S(2)}) collective-permute-start(f16[8,80,512]{2,1,0:T(8,128)(2,1)S(1)} %convert_element_type.89), channel_id=1, source_target_pairs={{0,1},{1,0},{2,3},{3,2},{4,5},{5,4},{6,7},{7,6},{8,9},{9,8},{10,11... | collective-permute-start | bytes 1966088 | tf_op jit(solution)/shard_map/ppermute | solution.py:312
  19.4 5.7 %collective-permute-start.4 = (f16[2,80,512]{2,1,0:T(8,128)(2,1)S(1)}, f16[2,80,512]{2,1,0:T(8,128)(2,1)S(1)}, u32[]{:S(2)}, u32[]{:S(2)}) collective-permute-start(f16[2,80,512]{2,1,0:T(8,128)(2,1)S(1)} %pad_maximum_fusion), channel_id=1, source_target_pairs={{0,2},{1,5},{2,0},{3,7},{4,6},{5,1},{6,4},{7,3},{8,10},{9,13},{10,... | collective-permute-start | bytes 491528 | tf_op jit(solution)/shard_map/ppermute | solution.py:270
  19.7 7.9 %collective-permute-start.1 = (f16[80,512]{1,0:T(8,128)(2,1)S(1)}, f16[80,512]{1,0:T(8,128)(2,1)S(1)}, u32[]{:S(2)}, u32[]{:S(2)}) collective-permute-start(f16[80,512]{1,0:T(8,128)(2,1)S(1)} %get-tuple-element.15), channel_id=1, source_target_pairs={{0,6},{1,13},{2,4},{3,15},{4,2},{5,9},{6,0},{7,11},{8,14},{9,5},{1... | collective-permute-start | bytes 245768 | tf_op jit(solution)/shard_map/ppermute | solution.py:270
  21.1 6.5 %collective-permute-start.3 = (f16[80,512]{1,0:T(8,128)(2,1)S(1)}, f16[80,512]{1,0:T(8,128)(2,1)S(1)}, u32[]{:S(2)}, u32[]{:S(2)}) collective-permute-start(f16[80,512]{1,0:T(8,128)(2,1)S(1)} %get-tuple-element.18), channel_id=1, source_target_pairs={{0,2},{1,9},{2,0},{3,11},{4,6},{5,13},{6,4},{7,15},{8,10},{9,1},{1... | collective-permute-start | bytes 245768 | tf_op jit(solution)/shard_map/ppermute | solution.py:270
  21.8 7.9 %collective-permute-start.2 = (f16[80,512]{1,0:T(8,128)(2,1)S(1)}, f16[80,512]{1,0:T(8,128)(2,1)S(1)}, u32[]{:S(2)}, u32[]{:S(2)}) collective-permute-start(f16[80,512]{1,0:T(8,128)(2,1)S(1)} %get-tuple-element.19), channel_id=1, source_target_pairs={{0,4},{1,5},{2,6},{3,7},{4,0},{5,1},{6,2},{7,3},{8,12},{9,13},{10,... | collective-permute-start | bytes 245768 | tf_op jit(solution)/shard_map/ppermute | solution.py:270
  25.1 7.0 %collective-permute-start.5 = (f16[80,512]{1,0:T(8,128)(2,1)S(1)}, f16[80,512]{1,0:T(8,128)(2,1)S(1)}, u32[]{:S(2)}, u32[]{:S(2)}) collective-permute-start(f16[80,512]{1,0:T(8,128)(2,1)S(1)} %get-tuple-element.13), channel_id=1, source_target_pairs={{0,8},{1,11},{2,10},{3,9},{4,12},{5,15},{6,14},{7,13},{8,0},{9,3},... | collective-permute-start | bytes 245768 | tf_op jit(solution)/shard_map/ppermute | solution.py:270
  25.4 6.7 %collective-permute-start.6 = (f16[80,512]{1,0:T(8,128)(2,1)S(1)}, f16[80,512]{1,0:T(8,128)(2,1)S(1)}, u32[]{:S(2)}, u32[]{:S(2)}) collective-permute-start(f16[80,512]{1,0:T(8,128)(2,1)S(1)} %get-tuple-element.14), channel_id=1, source_target_pairs={{0,12},{1,3},{2,14},{3,1},{4,8},{5,7},{6,10},{7,5},{8,4},{9,11},{1... | collective-permute-start | bytes 245768 | tf_op jit(solution)/shard_map/ppermute | solution.py:270
